TPU v7x, 32 devices: a whole 2x2x4 slice. The times are simulated.
32 devices in a mesh: dp: 2 (over y), blk: 4 (over z), tensor: 4 (over x, core).
Axes of the slice: x: 2, y: 2, z: 4, core: 2. Of those that a mesh axis runs over, the one named last changes fastest.
Arguments:
- target: bfloat16 [16, 512, 1024], P('dp', 'blk'), may hold values from -6 to 6
- source: bfloat16 [16, 4096, 1024], P('dp', 'blk'), may hold values from -6 to 6
- target_segments: int32 [16, 512], P('dp', 'blk'), may hold values from 0 to 15, never falling along the last dimension, each value on 1 to 80 neighbouring positions
- source_segments: int32 [16, 4096], P('dp', 'blk'), may hold values from 0 to 15, never falling along the last dimension, each value on 1 to 1024 neighbouring positions
- self_query: bfloat16 [1024, 1024], P(None, 'tensor'), may hold values from -0.1875 to 0.1875
- self_key: bfloat16 [1024, 1024], P(None, 'tensor'), may hold values from -0.1875 to 0.1875
- self_value: bfloat16 [1024, 1024], P(None, 'tensor'), may hold values from -0.1875 to 0.1875
- self_output: bfloat16 [1024, 1024], P('tensor'), may hold values from -0.75 to 0.75
- cross_query: bfloat16 [1024, 1024], P(None, 'tensor'), may hold values from -0.1875 to 0.1875
- cross_key: bfloat16 [1024, 1024], P(None, 'tensor'), may hold values from -0.1875 to 0.1875
- cross_value: bfloat16 [1024, 1024], P(None, 'tensor'), may hold values from -0.1875 to 0.1875
- cross_output: bfloat16 [1024, 1024], P('tensor'), may hold values from -1 to 1
- ffn_in: bfloat16 [1024, 4096], P(None, 'tensor'), may hold values from -0.1875 to 0.1875
- ffn_out: bfloat16 [4096, 1024], P('tensor'), may hold values from -0.09375 to 0.09375
- adapter_down: bfloat16 [1024, 512], P(None, 'tensor'), may hold values from -0.1875 to 0.1875
- adapter_up: bfloat16 [512, 1024], P('tensor'), may hold values from -0.0625 to 0.0625
- first_gain: float32 [1024], replicated, may hold values from 0.5 to 1.5
- first_shift: float32 [1024], replicated, may hold values from -3 to 3
- second_gain: float32 [1024], replicated, may hold values from 0.5 to 1.5
- second_shift: float32 [1024], replicated, may hold values from -3 to 3
- third_gain: float32 [1024], replicated, may hold values from 0.5 to 1.5
- third_shift: float32 [1024], replicated, may hold values from -3 to 3
- out_cotangent: bfloat16 [16, 512, 1024], P('dp', 'blk'), may hold values from -6 to 6
Outputs:
- output: bfloat16 [16, 512, 1024], P('dp', 'blk')
- target_grad: float32 [16, 512, 1024], P('dp', 'blk')
- source_grad: float32 [16, 4096, 1024], P('dp', 'blk', 'tensor')
- self_query_grad: float32 [1024, 1024], P(None, 'tensor')
- self_key_grad: float32 [1024, 1024], P(None, 'tensor')
- self_value_grad: float32 [1024, 1024], P(None, 'tensor')
- self_output_grad: float32 [1024, 1024], P('tensor')
- cross_query_grad: float32 [1024, 1024], P(None, 'tensor')
- cross_key_grad: float32 [1024, 1024], P(None, 'tensor')
- cross_value_grad: float32 [1024, 1024], P(None, 'tensor')
- cross_output_grad: float32 [1024, 1024], P('tensor')
- adapter_down_grad: float32 [1024, 512], P(None, 'tensor')
- adapter_up_grad: float32 [512, 1024], P('tensor')
- first_gain_grad: float32 [1024], P('tensor')
- first_shift_grad: float32 [1024], P('tensor')
- second_gain_grad: float32 [1024], P('tensor')
- second_shift_grad: float32 [1024], P('tensor')
- third_gain_grad: float32 [1024], P('tensor')
- third_shift_grad: float32 [1024], P('tensor')
Inputs may be any that keep to these rules, and one draw needn't show every extreme that they name: `target_segments`: in every row both id sequences never fall and hold each id 0 to 15; a summary has 1 to 80 slots and some has exactly 80; a document has 1 to 1024 slots and some has exactly 1024. `source_segments`: document ids pair with summary ids of the same row.
All inputs are finite; a program needn't handle non-finite values.
Results may differ from a plain program's by a relative error of at most 0.022.
Values may be sent and summed in bfloat16 or wider, within the bound.
No kernel may reach another device: no remote copies, remote signals or barrier semaphores. Data moves between devices by JAX's collectives and lax.ppermute only.
A program may use at most 320 MiB of HBM per device.

v0:
```python
import jax
import jax.numpy as jnp
from jax import lax
from jax.sharding import PartitionSpec as P

HEAD_DIM = 64


epsilon = 1e-05
negative = -1e30


def layer_norm(values, gain, shift):
    centered = values - jnp.mean(values, axis=-1, keepdims=True)
    variance = jnp.mean(centered * centered, axis=-1, keepdims=True)
    return centered * lax.rsqrt(variance + epsilon) * gain + shift


def exact_gelu(values):
    return jax.nn.gelu(values, approximate=False)


def smooth_gate(values):
    return jax.nn.silu(values)


def forward_mul(left, right):
    return jnp.einsum("rti,ij->rtj", left, right, preferred_element_type=jnp.float32)


def backward_mul(left, right):
    return jnp.einsum("rtj,ij->rti", left, right, preferred_element_type=jnp.float32)


def weight_mul(left, right):
    return jnp.einsum("rti,rtj->ij", left, right, preferred_element_type=jnp.float32)


def head_sum(partial_sum):
    return lax.psum(partial_sum, "tensor")


def split_heads(flat):
    return flat.reshape(flat.shape[0], flat.shape[1], flat.shape[2] // HEAD_DIM, HEAD_DIM)


def merge_heads(split):
    moved = jnp.transpose(split, (0, 2, 1, 3))
    return moved.reshape(moved.shape[0], moved.shape[1], moved.shape[2] * moved.shape[3])


def causal_mask(query_ids, query_place):

    def mask_of(key_ids, start, count):
        key_place = jnp.arange(count, dtype=jnp.int32)
        same = query_ids[:, :, None] == key_ids[:, None, :]
        earlier = key_place[None, :] <= query_place[:, None]
        return (same & earlier[None])[:, None]

    return mask_of


def pairing_mask(query_ids):

    def mask_of(key_ids, start, count):
        return (query_ids[:, :, None] == key_ids[:, None, :])[:, None]

    return mask_of


def empty_state(queries):
    batch, length, heads, _ = queries.shape
    best = jnp.full((batch, heads, length), negative, jnp.float32)
    return (best, jnp.zeros_like(best), jnp.zeros((batch, heads, length, HEAD_DIM), jnp.float32))


def attend_block(carry, pieces, start, queries, mask_of):
    best, total, summed = carry
    keys, values, key_ids = pieces
    scale = HEAD_DIM ** (-0.5)
    scores = (
        jnp.einsum(
            "rqhd,rkhd->rhqk", queries, split_heads(keys), preferred_element_type=jnp.float32
        )
        * scale
    )
    allowed = mask_of(key_ids, start, keys.shape[1])
    masked = jnp.where(allowed, scores, negative)
    fresh = jnp.maximum(best, jnp.max(masked, axis=-1))
    weights = jnp.where(allowed, jnp.exp(masked - fresh[..., None]), 0.0)
    total = jnp.sum(weights, axis=-1)
    summed = jnp.einsum(
        "rhqk,rkhd->rhqd",
        weights,
        split_heads(values).astype(jnp.float32),
        precision=lax.Precision.HIGHEST,
        preferred_element_type=jnp.float32,
    )
    return (fresh, total, summed)


def attend_back(pieces, start, queries, grads, best, total, delta, mask_of):
    keys, values, key_ids = pieces
    count = keys.shape[1]
    scale = HEAD_DIM ** (-0.5)
    keys_split = split_heads(keys)
    scores = (
        jnp.einsum("rqhd,rkhd->rhqk", queries, keys_split, preferred_element_type=jnp.float32)
        * scale
    )
    allowed = mask_of(key_ids, start, count)
    raw = jnp.exp(jnp.where(allowed, scores - best[..., None], negative))
    probs = raw / total[..., None]
    dprob = jnp.einsum(
        "rqhd,rkhd->rhqk", grads, split_heads(values), preferred_element_type=jnp.float32
    )
    dscore = (probs * (dprob - delta[..., None])).astype(jnp.bfloat16)
    query_grad = (
        jnp.einsum("rhqk,rkhd->rhqd", dscore, keys_split, preferred_element_type=jnp.float32)
        * scale
    )
    key_piece = (
        jnp.einsum("rhqk,rqhd->rkhd", dscore, queries, preferred_element_type=jnp.float32) * scale
    )
    scaled_grads = grads.astype(jnp.float32) / jnp.transpose(total, (0, 2, 1))[..., None]
    value_piece = jnp.einsum(
        "rhqk,rqhd->rkhd",
        raw,
        scaled_grads,
        precision=lax.Precision.HIGHEST,
        preferred_element_type=jnp.float32,
    )
    batch = keys.shape[0]
    key_grad = key_piece.reshape(batch, count, -1)
    value_grad = value_piece.reshape(batch, count, -1)
    return (query_grad, key_grad, value_grad)


def finish(state):
    best, total, summed = state
    return (summed / total[..., None], best, total)


def on_device(
    target,
    source,
    target_segments,
    source_segments,
    self_query,
    self_key,
    self_value,
    self_output,
    cross_query,
    cross_key,
    cross_value,
    cross_output,
    ffn_in,
    ffn_out,
    adapter_down,
    adapter_up,
    first_gain,
    first_shift,
    second_gain,
    second_shift,
    third_gain,
    third_shift,
    out_cotangent,
):
    local_target = target.shape[1]
    query_offset = lax.axis_index("blk") * local_target
    query_place = query_offset + jnp.arange(local_target, dtype=jnp.int32)
    self_mask = causal_mask(target_segments, query_place)
    cross_mask = pairing_mask(target_segments)
    queries = forward_mul(target, self_query).astype(jnp.bfloat16)
    keys = forward_mul(target, self_key).astype(jnp.bfloat16)
    values = forward_mul(target, self_value).astype(jnp.bfloat16)
    query_split = split_heads(queries)
    self_state = attend_block(
        empty_state(query_split),
        (
            lax.all_gather(keys, "blk", axis=1, tiled=True),
            lax.all_gather(values, "blk", axis=1, tiled=True),
            lax.all_gather(target_segments, "blk", axis=1, tiled=True),
        ),
        jnp.int32(0),
        queries=query_split,
        mask_of=self_mask,
    )
    self_mixed, self_best, self_total = finish(self_state)
    self_low = merge_heads(self_mixed).astype(jnp.bfloat16)
    first_in = target.astype(jnp.float32) + head_sum(forward_mul(self_low, self_output))
    first, first_back = jax.vjp(layer_norm, first_in, first_gain, first_shift)
    first_low = first.astype(jnp.bfloat16)
    cross_queries = forward_mul(first_low, cross_query).astype(jnp.bfloat16)
    cross_keys = forward_mul(source, cross_key).astype(jnp.bfloat16)
    cross_values = forward_mul(source, cross_value).astype(jnp.bfloat16)
    cross_split = split_heads(cross_queries)
    local_source = (cross_keys, cross_values, source_segments)
    cross_state = attend_block(
        empty_state(cross_split),
        (
            lax.all_gather(local_source[0], "blk", axis=1, tiled=True),
            lax.all_gather(local_source[1], "blk", axis=1, tiled=True),
            lax.all_gather(local_source[2], "blk", axis=1, tiled=True),
        ),
        jnp.int32(0),
        queries=cross_split,
        mask_of=cross_mask,
    )
    cross_mixed, cross_best, cross_total = finish(cross_state)
    cross_low = merge_heads(cross_mixed).astype(jnp.bfloat16)
    second_in = first + head_sum(forward_mul(cross_low, cross_output))
    second, second_back = jax.vjp(layer_norm, second_in, second_gain, second_shift)
    second_low = second.astype(jnp.bfloat16)
    gate = forward_mul(second_low, ffn_in)
    active_value, gelu_back = jax.vjp(exact_gelu, gate)
    active = active_value.astype(jnp.bfloat16)
    down = forward_mul(second_low, adapter_down)
    rect_value, silu_back = jax.vjp(smooth_gate, down)
    rectified = rect_value.astype(jnp.bfloat16)
    branch_part = forward_mul(active, ffn_out) + 4.0 * forward_mul(rectified, adapter_up)
    third_in = second + head_sum(branch_part)
    result, third_back = jax.vjp(layer_norm, third_in, third_gain, third_shift)
    third_grad, third_gain_grad, third_shift_grad = third_back(out_cotangent.astype(jnp.float32))
    branch_grad = third_grad.astype(jnp.bfloat16)
    gate_grad = gelu_back(backward_mul(branch_grad, ffn_out))[0].astype(jnp.bfloat16)
    rect_grad = 4.0 * backward_mul(branch_grad, adapter_up)
    down_grad = silu_back(rect_grad)[0].astype(jnp.bfloat16)
    adapter_up_grad = 4.0 * weight_mul(rectified, branch_grad)
    adapter_down_grad = weight_mul(second_low, down_grad)
    second_grad = third_grad + head_sum(
        backward_mul(gate_grad, ffn_in) + backward_mul(down_grad, adapter_down)
    )
    cross_grad, second_gain_grad, second_shift_grad = second_back(second_grad)
    cross_branch_grad = cross_grad.astype(jnp.bfloat16)
    cross_output_grad = weight_mul(cross_low, cross_branch_grad)
    cross_heads_grad = split_heads(
        backward_mul(cross_branch_grad, cross_output).astype(jnp.bfloat16)
    )
    cross_delta = jnp.einsum("rqhd,rhqd->rhq", cross_heads_grad.astype(jnp.float32), cross_mixed)
    cross_q_grad, cross_k_all, cross_v_all = attend_back(
        (
            lax.all_gather(local_source[0], "blk", axis=1, tiled=True),
            lax.all_gather(local_source[1], "blk", axis=1, tiled=True),
            lax.all_gather(local_source[2], "blk", axis=1, tiled=True),
        ),
        jnp.int32(0),
        queries=cross_split,
        grads=cross_heads_grad,
        best=cross_best,
        total=cross_total,
        delta=cross_delta,
        mask_of=cross_mask,
    )
    cross_k_grad, cross_v_grad = (
        lax.psum_scatter(
            cross_k_all.astype(jnp.bfloat16), "blk", scatter_dimension=1, tiled=True
        ).astype(jnp.float32),
        lax.psum_scatter(
            cross_v_all.astype(jnp.bfloat16), "blk", scatter_dimension=1, tiled=True
        ).astype(jnp.float32),
    )
    cross_k_low = cross_k_grad.astype(jnp.bfloat16)
    cross_v_low = cross_v_grad.astype(jnp.bfloat16)
    cross_q_low = merge_heads(cross_q_grad).astype(jnp.bfloat16)
    cross_query_grad = weight_mul(first_low, cross_q_low)
    cross_key_grad = weight_mul(source, cross_k_low)
    cross_value_grad = weight_mul(source, cross_v_low)
    source_terms = backward_mul(cross_k_low, cross_key) + backward_mul(cross_v_low, cross_value)
    source_grad = lax.psum_scatter(
        source_terms.astype(jnp.bfloat16), "tensor", scatter_dimension=2, tiled=True
    ).astype(jnp.float32)
    first_grad = cross_grad + head_sum(backward_mul(cross_q_low, cross_query))
    self_grad, first_gain_grad, first_shift_grad = first_back(first_grad)
    self_branch_grad = self_grad.astype(jnp.bfloat16)
    self_output_grad = weight_mul(self_low, self_branch_grad)
    self_heads_grad = split_heads(backward_mul(self_branch_grad, self_output).astype(jnp.bfloat16))
    self_delta = jnp.einsum("rqhd,rhqd->rhq", self_heads_grad.astype(jnp.float32), self_mixed)
    self_q_grad, self_k_all, self_v_all = attend_back(
        (
            lax.all_gather(keys, "blk", axis=1, tiled=True),
            lax.all_gather(values, "blk", axis=1, tiled=True),
            lax.all_gather(target_segments, "blk", axis=1, tiled=True),
        ),
        jnp.int32(0),
        queries=query_split,
        grads=self_heads_grad,
        best=self_best,
        total=self_total,
        delta=self_delta,
        mask_of=self_mask,
    )
    self_k_grad, self_v_grad = (
        lax.psum_scatter(
            self_k_all.astype(jnp.bfloat16), "blk", scatter_dimension=1, tiled=True
        ).astype(jnp.float32),
        lax.psum_scatter(
            self_v_all.astype(jnp.bfloat16), "blk", scatter_dimension=1, tiled=True
        ).astype(jnp.float32),
    )
    self_k_low = self_k_grad.astype(jnp.bfloat16)
    self_v_low = self_v_grad.astype(jnp.bfloat16)
    self_q_low = merge_heads(self_q_grad).astype(jnp.bfloat16)
    self_query_grad = weight_mul(target, self_q_low)
    self_key_grad = weight_mul(target, self_k_low)
    self_value_grad = weight_mul(target, self_v_low)
    input_terms = (
        backward_mul(self_q_low, self_query)
        + backward_mul(self_k_low, self_key)
        + backward_mul(self_v_low, self_value)
    )
    target_grad = self_grad + head_sum(input_terms)
    share = first_gain.shape[0] // lax.axis_size("tensor")
    offset = lax.axis_index("tensor") * share

    def own_part(vector):
        return lax.dynamic_slice_in_dim(vector, offset, share, 0)

    summed = (
        lax.psum(self_query_grad.astype(jnp.bfloat16), ("dp", "blk")).astype(jnp.float32),
        lax.psum(self_key_grad.astype(jnp.bfloat16), ("dp", "blk")).astype(jnp.float32),
        lax.psum(self_value_grad.astype(jnp.bfloat16), ("dp", "blk")).astype(jnp.float32),
        lax.psum(self_output_grad.astype(jnp.bfloat16), ("dp", "blk")).astype(jnp.float32),
        lax.psum(cross_query_grad.astype(jnp.bfloat16), ("dp", "blk")).astype(jnp.float32),
        lax.psum(cross_key_grad.astype(jnp.bfloat16), ("dp", "blk")).astype(jnp.float32),
        lax.psum(cross_value_grad.astype(jnp.bfloat16), ("dp", "blk")).astype(jnp.float32),
        lax.psum(cross_output_grad.astype(jnp.bfloat16), ("dp", "blk")).astype(jnp.float32),
        lax.psum(adapter_down_grad.astype(jnp.bfloat16), ("dp", "blk")).astype(jnp.float32),
        lax.psum(adapter_up_grad.astype(jnp.bfloat16), ("dp", "blk")).astype(jnp.float32),
        lax.psum(own_part(first_gain_grad).astype(jnp.bfloat16), ("dp", "blk")).astype(jnp.float32),
        lax.psum(own_part(first_shift_grad).astype(jnp.bfloat16), ("dp", "blk")).astype(
            jnp.float32
        ),
        lax.psum(own_part(second_gain_grad).astype(jnp.bfloat16), ("dp", "blk")).astype(
            jnp.float32
        ),
        lax.psum(own_part(second_shift_grad).astype(jnp.bfloat16), ("dp", "blk")).astype(
            jnp.float32
        ),
        lax.psum(own_part(third_gain_grad).astype(jnp.bfloat16), ("dp", "blk")).astype(jnp.float32),
        lax.psum(own_part(third_shift_grad).astype(jnp.bfloat16), ("dp", "blk")).astype(
            jnp.float32
        ),
    )
    return (
        result.astype(jnp.bfloat16),
        target_grad,
        source_grad,
        summed[0],
        summed[1],
        summed[2],
        summed[3],
        summed[4],
        summed[5],
        summed[6],
        summed[7],
        summed[8],
        summed[9],
        summed[10],
        summed[11],
        summed[12],
        summed[13],
        summed[14],
        summed[15],
    )


def solution(mesh):
    return jax.shard_map(
        on_device,
        mesh=mesh,
        in_specs=(
            P("dp", "blk", None),
            P("dp", "blk", None),
            P("dp", "blk"),
            P("dp", "blk"),
            P(None, "tensor"),
            P(None, "tensor"),
            P(None, "tensor"),
            P("tensor", None),
            P(None, "tensor"),
            P(None, "tensor"),
            P(None, "tensor"),
            P("tensor", None),
            P(None, "tensor"),
            P("tensor", None),
            P(None, "tensor"),
            P("tensor", None),
            P(),
            P(),
            P(),
            P(),
            P(),
            P(),
            P("dp", "blk", None),
        ),
        out_specs=(
            P("dp", "blk", None),
            P("dp", "blk", None),
            P("dp", "blk", "tensor"),
            P(None, "tensor"),
            P(None, "tensor"),
            P(None, "tensor"),
            P("tensor", None),
            P(None, "tensor"),
            P(None, "tensor"),
            P(None, "tensor"),
            P("tensor", None),
            P(None, "tensor"),
            P("tensor", None),
            P("tensor"),
            P("tensor"),
            P("tensor"),
            P("tensor"),
            P("tensor"),
            P("tensor"),
        ),
        check_vma=False,
    )
```

profile of v0, /device:TPU:0, one launch (start us, length us, event | category | flops | bytes accessed | tf_op | source)
XLA Modules:
  0.0 2440.4 jit_solution(14724097940544991696)
XLA Ops:
  18.4 15.0 all_gather.24
  34.0 25.7 %all-gather.5.cloned.1.call-done = bf16[8,512,256]{2,1,0:T(8,128)(2,1)} async-done(((bf16[8,128,256]{2,1,0:T(8,128)(2,1)}), bf16[8,512,256]{2,1,0:T(8,128)(2,1)}) %all-gather.5.cloned.1.call-update) | async-done | bytes 2097168 | tf_op jit(solution)/shard_map/all_gather | solution.py:181
  59.7 3.9 copy.99
  63.7 3.5 select_reduce_fusion.1
  73.3 33.3 %all-gather.7.cloned.1.call-done = bf16[8,512,256]{2,1,0:T(8,128)(2,1)} async-done(((bf16[8,128,256]{2,1,0:T(8,128)(2,1)}), bf16[8,512,256]{2,1,0:T(8,128)(2,1)}) %all-gather.7.cloned.1.call-update) | async-done | bytes 2097168 | tf_op jit(solution)/shard_map/all_gather | solution.py:182
  106.5 3.9 copy.100
  110.5 11.9 fusion.71
  126.3 13.2 convolution_convert_fusion.1
  140.5 12.4 convolution_convert_fusion
  153.7 13.8 all_gather.27
  167.5 4.8 broadcast_compare_fusion
  172.3 38.1 %all-reduce.10.cloned.1.call-done = f32[8,128,1024]{2,1,0:T(8,128)} async-done(((f32[8,128,1024]{2,1,0:T(8,128)}), f32[8,128,1024]{2,1,0:T(8,128)}) %all-reduce.10.cloned.1.call-update) | async-done | bytes 4194320 | tf_op jit(solution)/shard_map/psum | solution.py:40
  216.9 281.9 %all-gather.9.cloned.1.call-done = bf16[8,4096,256]{2,1,0:T(8,128)(2,1)} async-done(((bf16[8,1024,256]{2,1,0:T(8,128)(2,1)}), bf16[8,4096,256]{2,1,0:T(8,128)(2,1)}) %all-gather.9.cloned.1.call-update) | async-done | bytes 16777232 | tf_op jit(solution)/shard_map/all_gather | solution.py:202
  498.8 22.0 copy.103
  520.8 31.6 %select_reduce_fusion = (f32[8,4,128]{2,1,0:T(4,128)S(1)}, f32[8,4,128,4096]{3,2,1,0:T(8,128)}) fusion(pred[8,128,4096]{2,1,0:T(8,128)(4,1)} %broadcast_compare_fusion, bf16[8,128,4,64]{1,3,2,0:T(8,128)(2,1)S(1)} %bitcast.255, bf16[8,4096,4,64]{1,3,2,0:T(8,128)(2,1)} %bitcast.242), kind=kOutput, calls=%fused_computation.3 | convolution fusion | flops 2197811200 | bytes 88621056 | tf_op jit(solution)/shard_map/rqhd,rkhd->rhqk/dot_general | solution.py:82
  552.4 23.0 fusion.1
  575.4 209.9 %all-gather.11.cloned.1.call-done = bf16[8,4096,256]{2,1,0:T(8,128)(2,1)} async-done(((bf16[8,1024,256]{2,1,0:T(8,128)(2,1)}), bf16[8,4096,256]{2,1,0:T(8,128)(2,1)}) %all-gather.11.cloned.1.call-update) | async-done | bytes 16777232 | tf_op jit(solution)/shard_map/all_gather | solution.py:203
  785.3 21.0 copy.104
  806.3 63.4 %fusion.70 = (bf16[8,128,4,64]{1,3,2,0:T(8,128)(2,1)S(1)}, f32[8,4,128,64]{2,3,1,0:T(8,128)}) fusion(f32[8,128,4]{1,2,0:T(4,128)S(1)} %bitcast.280, bf16[8,4096,4,64]{1,3,2,0:T(8,128)(2,1)} %bitcast.247, f32[8,4,128,4096]{3,2,1,0:T(8,128)} %get-tuple-element.125, f32[8,4,128]{2,1,0:T(4,128)S(1)} %broadcast_maximum_fusion, ...), kind=kOutput, calls=%fused_computation.146 | convolution fusion | flops 12952535040 | bytes 89686016 | tf_op jit(solution)/shard_map/rhqk,rkhd->rhqd/dot_general | solution.py:92
  873.3 83.8 %all-reduce.12.cloned.1.call-done = f32[8,128,1024]{2,1,0:T(8,128)} async-done(((f32[8,128,1024]{2,1,0:T(8,128)}), f32[8,128,1024]{2,1,0:T(8,128)}) %all-reduce.12.cloned.1.call-update) | async-done | bytes 4194320 | tf_op jit(solution)/shard_map/psum | solution.py:40
  957.1 4.3 fusion.134
  967.4 9.0 fusion.19
  981.6 85.7 %all-reduce.14.cloned.1.call-done = f32[8,128,1024]{2,1,0:T(8,128)} async-done(((f32[8,128,1024]{2,1,0:T(8,128)}), f32[8,128,1024]{2,1,0:T(8,128)}) %all-reduce.14.cloned.1.call-update) | async-done | bytes 4194320 | tf_op jit(solution)/shard_map/psum | solution.py:40
  1067.3 4.7 fusion.132
  1079.5 11.4 fusion.42
  1096.8 85.7 %all-reduce.16.cloned.1.call-done = f32[8,128,1024]{2,1,0:T(8,128)} async-done(((f32[8,128,1024]{2,1,0:T(8,128)}), f32[8,128,1024]{2,1,0:T(8,128)}) %all-reduce.16.cloned.1.call-update) | async-done | bytes 4194320 | tf_op jit(solution)/shard_map/psum | solution.py:40
  1182.6 8.5 multiply_reduce_fusion
  1195.8 44.9 %multiply_convert_fusion = bf16[8,4,128,4096]{3,2,1,0:T(8,128)(2,1)} fusion(f32[8,4,128,4096]{3,2,1,0:T(8,128)} %get-tuple-element.125, bf16[8,128,4,64]{1,3,2,0:T(8,128)(2,1)S(1)} %bitcast.261, bf16[8,4096,4,64]{1,3,2,0:T(8,128)(2,1)} %bitcast.248, f32[8,4,128]{2,1,0:T(4,128)S(1)} %fusion.69, f32[8,4,128]{2,1,0:T(4,128)S(1)} %fusion.1, ...), kind=kOutput, calls=%fused_computation | convolution fusion | flops 2264924160 | bytes 122208256 | tf_op jit(solution)/shard_map/rqhd,rkhd->rhqk/dot_general | solution.py:114
  1240.8 20.4 fusion.57
  1264.1 85.7 %all-reduce.18.cloned.1.call-done = f32[8,128,1024]{2,1,0:T(8,128)} async-done(((f32[8,128,1024]{2,1,0:T(8,128)}), f32[8,128,1024]{2,1,0:T(8,128)}) %all-reduce.18.cloned.1.call-update) | async-done | bytes 4194320 | tf_op jit(solution)/shard_map/psum | solution.py:40
  1349.8 6.6 multiply_reduce_fusion.1
  1360.9 10.1 fusion.47
  1378.0 6.4 multiply_convert_fusion.2
  1390.3 3.7 copy.155
  1394.0 19.7 multiply_convert_fusion.1
  1414.8 60.7 %fusion.12 = bf16[8,4,64,4096]{3,2,1,0:T(8,128)(2,1)} fusion(f32[8,4,128,4096]{3,2,1,0:T(8,128)} %get-tuple-element.125, f32[8,4,128]{2,1,0:T(4,128)S(1)} %broadcast_maximum_fusion, pred[8,128,4096]{2,1,0:T(8,128)(4,1)} %broadcast_compare_fusion, bf16[8,128,4,64]{1,3,2,0:T(8,128)(2,1)S(1)} %bitcast.262, f32[8,128,4]{1,2,0:T(4,128)S(1)} %bitcast.281), kind=kOutput, calls=%fused_computation.18 | convolution fusion | flops 12944146432 | bytes 88637440 | tf_op jit(solution)/shard_map/rhqk,rqhd->rkhd/dot_general | solution.py:126
  1505.7 242.3 %reduce-scatter.10.cloned.1.call-done = bf16[8,1024,256]{1,2,0:T(8,128)(2,1)} async-done(((bf16[8,4096,256]{1,2,0:T(8,128)(2,1)}), bf16[8,1024,256]{1,2,0:T(8,128)(2,1)}) %reduce-scatter.10.cloned.1.call-update) | async-done | bytes 4194320 | tf_op jit(solution)/shard_map/reduce_scatter | solution.py:256
  1748.0 12.3 fusion.65
  1760.3 271.1 %reduce-scatter.12.cloned.1.call-done = bf16[8,1024,256]{1,2,0:T(8,128)(2,1)} async-done(((bf16[8,4096,256]{1,2,0:T(8,128)(2,1)}), bf16[8,1024,256]{1,2,0:T(8,128)(2,1)}) %reduce-scatter.12.cloned.1.call-update) | async-done | bytes 4194320 | tf_op jit(solution)/shard_map/reduce_scatter | solution.py:259
  2031.4 12.3 fusion.64
  2044.8 15.8 fusion.86
  2060.6 17.4 add_convert_fusion
  2082.5 21.5 all-reduce
  2107.4 13.3 all-reduce.20.cloned.1.call-done
  2120.6 6.0 add_add_fusion.4
  2126.6 173.1 %all-reduce.22.cloned.1.call-done = (bf16[1024,256]{0,1:T(8,128)(2,1)}, bf16[1024,256]{0,1:T(8,128)(2,1)}, bf16[1024,256]{0,1:T(8,128)(2,1)}, bf16[1024,256]{0,1...) async-done(((bf16[1024,256]{0,1:T(8,128)(2,1)}, ...) | async-done | bytes 4718608 | tf_op jit(solution)/shard_map/psum | solution.py:320
  2314.9 112.2 %reduce-scatter.14.cloned.1.call-done = bf16[8,1024,256]{2,1,0:T(8,128)(2,1)} async-done(((bf16[8,1024,1024]{2,1,0:T(8,128)(2,1)}), bf16[8,1024,256]{2,1,0:T(8,128)(2,1)}) %reduce-scatter.14.cloned.1.call-update) | async-done | bytes 4194320 | tf_op jit(solution)/shard_map/reduce_scatter | solution.py:270
  2427.1 6.3 convert_element_type.314
  (299 shorter events, 137.9 us)
Async XLA Ops:
  7.2 956.9 %copy-start = (bf16[1024,1024]{1,0:T(8,128)(2,1)S(1)}, bf16[1024,1024]{1,0:T(8,128)(2,1)}, u32[]{:S(2)}) copy-start(bf16[1024,1024]{1,0:T(8,128)(2,1)} %param.35) | copy-start | bytes 6291460
  7.2 52.5 %all-gather.5.cloned.1.call-start = ((), (), s32[]{:S(2)}) async-start(), calls=%async_computation.5 | async-start | bytes 2621440 | tf_op jit(solution)/shard_map/all_gather | solution.py:181
  10.7 95.9 %all-gather.7.cloned.1.call-start = ((), (), s32[]{:S(2)}) async-start(), calls=%async_computation.6 | async-start | bytes 2621440 | tf_op jit(solution)/shard_map/all_gather | solution.py:182
  13.9 196.4 %all-reduce.10.cloned.1.call-start = ((), (), s32[]{:S(2)}) async-start(), calls=%async_computation.7 | async-start | bytes 8388608 | tf_op jit(solution)/shard_map/psum | solution.py:40
  18.4 48.8 %copy-start.28 = (bf16[8,128,256]{1,2,0:T(8,128)(2,1)}, bf16[8,128,256]{1,2,0:T(8,128)(2,1)S(1)}, u32[]{:S(2)}) copy-start(bf16[8,128,256]{1,2,0:T(8,128)(2,1)S(1)} %copy.98) | copy-start | bytes 1572868
  34.0 76.5 %copy-start.26 = (pred[8,128,512]{2,1,0:T(8,128)(4,1)}, pred[8,128,512]{2,1,0:T(8,128)(4,1)S(1)}, u32[]{:S(2)}) copy-start(pred[8,128,512]{2,1,0:T(8,128)(4,1)S(1)} %compare_and_fusion) | copy-start | bytes 1572868
  67.2 43.3 %copy-start.74 = (f32[8,4,128]{2,1,0:T(4,128)}, f32[8,4,128]{2,1,0:T(4,128)S(1)}, u32[]{:S(2)}) copy-start(f32[8,4,128]{2,1,0:T(4,128)S(1)} %broadcast_maximum_fusion.1) | copy-start | bytes 49156
  73.2 49.1 %copy-start.70 = (f32[8,4,128]{2,1,0:T(4,128)}, f32[8,4,128]{2,1,0:T(4,128)S(1)}, u32[]{:S(2)}) copy-start(f32[8,4,128]{2,1,0:T(4,128)S(1)} %fusion.14) | copy-start | bytes 49156
  110.5 12.7 copy-start.51
  126.0 372.8 %all-gather.9.cloned.1.call-start = ((), (), s32[]{:S(2)}) async-start(), calls=%async_computation.8 | async-start | bytes 20971520 | tf_op jit(solution)/shard_map/all_gather | solution.py:202
  139.4 645.9 %all-gather.11.cloned.1.call-start = ((), (), s32[]{:S(2)}) async-start(), calls=%async_computation.9 | async-start | bytes 20971520 | tf_op jit(solution)/shard_map/all_gather | solution.py:203
  152.9 804.1 %all-reduce.12.cloned.1.call-start = ((), (), s32[]{:S(2)}) async-start(), calls=%async_computation.10 | async-start | bytes 8388608 | tf_op jit(solution)/shard_map/psum | solution.py:40
  213.7 743.3 %copy-start.68 = (f32[8,128]{1,0:T(8,128)}, f32[8,128]{1,0:T(8,128)S(1)}, u32[]{:S(2)}) copy-start(f32[8,128]{1,0:T(8,128)S(1)} %broadcast_multiply_fusion.2) | copy-start | bytes 12292
  215.7 741.4 %copy-start.72 = (f32[8,128]{1,0:T(8,128)}, f32[8,128]{1,0:T(8,128)S(1)}, u32[]{:S(2)}) copy-start(f32[8,128]{1,0:T(8,128)S(1)} %fusion.112) | copy-start | bytes 12292
  216.9 303.9 %copy-start.24 = (bf16[8,128,256]{1,2,0:T(8,128)(2,1)}, bf16[8,128,256]{1,2,0:T(8,128)(2,1)S(1)}, u32[]{:S(2)}) copy-start(bf16[8,128,256]{1,2,0:T(8,128)(2,1)S(1)} %copy.102) | copy-start | bytes 1572868
  806.3 64.2 %copy-start.48 = (bf16[256,1024]{1,0:T(8,128)(2,1)S(1)}, bf16[256,1024]{1,0:T(8,128)(2,1)}, u32[]{:S(2)}) copy-start(bf16[256,1024]{1,0:T(8,128)(2,1)} %param.34) | copy-start | bytes 1572868
  873.2 194.0 %all-reduce.14.cloned.1.call-start = ((), (), s32[]{:S(2)}) async-start(), calls=%async_computation.11 | async-start | bytes 8388608 | tf_op jit(solution)/shard_map/psum | solution.py:40
  964.1 126.8 %copy-start.37 = (f32[8,128,128]{2,1,0:T(8,128)}, f32[8,128,128]{2,1,0:T(8,128)S(1)}, u32[]{:S(2)}) copy-start(f32[8,128,128]{2,1,0:T(8,128)S(1)} %fusion.108) | copy-start | bytes 1572868
  967.4 9.0 copy-start.18
  967.4 9.0 copy-start.31
  981.5 90.5 %copy-start.77 = (f32[1024]{0:T(1024)S(1)}, f32[1024]{0:T(1024)}, u32[]{:S(2)}) copy-start(f32[1024]{0:T(1024)} %param.43) | copy-start | bytes 12292
  981.5 201.1 %all-reduce.16.cloned.1.call-start = ((), (), s32[]{:S(2)}) async-start(), calls=%async_computation.12 | async-start | bytes 8388608 | tf_op jit(solution)/shard_map/psum | solution.py:40
  1096.8 85.8 %copy-start.10 = (bf16[8,128,1024]{2,1,0:T(8,128)(2,1)S(1)}, bf16[8,128,1024]{2,1,0:T(8,128)(2,1)}, u32[]{:S(2)}) copy-start(bf16[8,128,1024]{2,1,0:T(8,128)(2,1)} %param.45) | copy-start | bytes 6291460
  1096.8 85.8 %copy-start.87 = (f32[1024]{0:T(1024)S(1)}, f32[1024]{0:T(1024)}, u32[]{:S(2)}) copy-start(f32[1024]{0:T(1024)} %param.44) | copy-start | bytes 12292
  1096.8 253.0 %all-reduce.18.cloned.1.call-start = ((), (), s32[]{:S(2)}) async-start(), calls=%async_computation.13 | async-start | bytes 8388608 | tf_op jit(solution)/shard_map/psum | solution.py:40
  1182.6 8.5 copy-start.3
  1195.6 45.2 %copy-start.34 = (bf16[8,128,256]{1,2,0:T(8,128)(2,1)}, bf16[8,128,256]{1,2,0:T(8,128)(2,1)S(1)}, u32[]{:S(2)}) copy-start(bf16[8,128,256]{1,2,0:T(8,128)(2,1)S(1)} %copy.106) | copy-start | bytes 1572868
  1240.8 20.4 copy-start.50
  1261.1 88.7 %copy-start.69 = (f32[8,128]{1,0:T(8,128)S(1)}, f32[8,128]{1,0:T(8,128)}, u32[]{:S(2)}) copy-start(f32[8,128]{1,0:T(8,128)} %copy-done.68) | copy-start | bytes 12292
  1261.2 88.7 %copy-start.73 = (f32[8,128]{1,0:T(8,128)S(1)}, f32[8,128]{1,0:T(8,128)}, u32[]{:S(2)}) copy-start(f32[8,128]{1,0:T(8,128)} %copy-done.72) | copy-start | bytes 12292
  1261.2 88.7 %copy-start.79 = (f32[1024]{0:T(1024)S(1)}, f32[1024]{0:T(1024)}, u32[]{:S(2)}) copy-start(f32[1024]{0:T(1024)} %param.39) | copy-start | bytes 12292
  1264.0 92.4 %copy-start.82 = (f32[8,128]{1,0:T(8,128)S(1)}, f32[8,128]{1,0:T(8,128)}, u32[]{:S(2)}) copy-start(f32[8,128]{1,0:T(8,128)} %copy-done.81) | copy-start | bytes 12292
  1264.1 229.6 %reduce-scatter.18.cloned.1.call-start = ((), (), s32[]{:S(2)}) async-start(), calls=%async_computation.19 | async-start | bytes 2621440
  1360.8 10.1 copy-start.36
  1376.4 119.6 %reduce-scatter.16.cloned.1.call-start = ((), (), s32[]{:S(2)}) async-start(), calls=%async_computation.18 | async-start | bytes 2621440
  1378.0 8.4 copy-start.29
  1394.0 354.0 %reduce-scatter.10.cloned.1.call-start = ((), (), s32[]{:S(2)}) async-start(), calls=%async_computation.15 | async-start | bytes 20971520 | tf_op jit(solution)/shard_map/reduce_scatter | solution.py:256
  1413.7 617.7 %reduce-scatter.12.cloned.1.call-start = ((), (), s32[]{:S(2)}) async-start(), calls=%async_computation.16 | async-start | bytes 20971520 | tf_op jit(solution)/shard_map/reduce_scatter | solution.py:259
  1475.5 645.1 %all-reduce.20.cloned.1.call-start = ((), (), s32[]{:S(2)}) async-start(), calls=%async_computation.14 | async-start | bytes 8388608 | tf_op jit(solution)/shard_map/psum | solution.py:40
  1505.4 794.3 %all-reduce.22.cloned.1.call-start = ((), (), s32[]{:S(2)}) async-start(), calls=%async_computation.20 | async-start | bytes 9437184 | tf_op jit(solution)/shard_map/psum | solution.py:320
  2043.8 16.8 copy-start.47
  2043.8 383.3 %reduce-scatter.14.cloned.1.call-start = ((), (), s32[]{:S(2)}) async-start(), calls=%async_computation.17 | async-start | bytes 20971520 | tf_op jit(solution)/shard_map/reduce_scatter | solution.py:270
  2044.8 15.8 copy-start.23
  2299.7 9.6 copy-start.64
  2299.7 10.8 copy-start.63
  2302.1 9.6 copy-start.62
  2303.9 8.9 copy-start.61
  2313.8 119.6 %copy-start.1 = (bf16[1024,1024]{1,0:T(8,128)(2,1)S(1)}, bf16[1024,1024]{1,0:T(8,128)(2,1)}, u32[]{:S(2)}) copy-start(bf16[1024,1024]{1,0:T(8,128)(2,1)} %param.35) | copy-start | bytes 6291460
  (56 other events, 172.0 us)
Sparse Core Ops, SparseCore 0:
  10.8 48.9 all-gather.4
  61.9 44.5 all-gather.6
  126.1 84.1 all-reduce.9
  211.8 286.9 all-gather.8
  500.3 284.9 all-gather.10
  873.4 83.6 all-reduce.11
  981.6 85.6 all-reduce.13
  1096.9 85.6 all-reduce.15
  1264.2 85.6 all-reduce.17
  1376.5 44.0 reduce-scatter.17
  1422.8 43.1 reduce-scatter.15
  1468.3 279.6 reduce-scatter.9
  1750.4 281.0 reduce-scatter.11
  2034.3 86.2 all-reduce.19
  2126.5 173.2 all-reduce.21
  2302.2 124.8 reduce-scatter.13
where the time goes:
time: 2450 us; the launch traced here: 2440 us
  waiting for transfers between devices  1740 us (71%)
  matrix products  426 us (17%)
  other arithmetic  104 us (4%)
  local copies, waits for them, and re-layouts  101 us (4%)
  blocking collectives  50.3 us (2%)
    psum x6, waiting for transfers between devices, head_sum(): return lax.psum(partial_sum, 'tensor')  392 us
    all_gather x1, waiting for transfers between devices, on_device(): lax.all_gather(local_source[0], 'blk', axis=1, tiled=True)  282 us
    reduce_scatter x1, waiting for transfers between devices, on_device(): lax.psum_scatter(cross_v_all.astype(jnp.bfloat16), 'blk', scatter_dimensi...  271 us
    reduce_scatter x1, waiting for transfers between devices, on_device(): lax.psum_scatter(cross_k_all.astype(jnp.bfloat16), 'blk', scatter_dimensi...  242 us
    all_gather x1, waiting for transfers between devices, on_device(): lax.all_gather(local_source[1], 'blk', axis=1, tiled=True)  210 us
    psum x1, waiting for transfers between devices, on_device(): lax.psum(self_query_grad.astype(jnp.bfloat16), ('dp', 'blk'))  173 us
    reduce_scatter x1, waiting for transfers between devices, on_device(): lax.psum_scatter(source_terms.astype(jnp.bfloat16), 'tensor', scatter_dim...  112 us
    dot_general x2, matrix products, attend_block(): jnp.einsum('rhqk,rkhd->rhqd', weights, split_heads(values).astype(jnp.flo...  75.3 us
  transfers between devices with their start and end apart: 16, of which 14 were waited for; matrix products, arithmetic and copies ran while one was open for 14% of the time, Pallas kernels for 0%

commit v1 on v0

v1 whole, which is shorter than its diff:
```python
import functools

import jax
import jax.numpy as jnp
from jax import lax
from jax.experimental import pallas as pl
from jax.experimental.pallas import tpu as pltpu
from jax.sharding import PartitionSpec as P

HEAD_DIM = 64
HALO = 80
CHUNKS = 1
SOURCE_TILE = 256

epsilon = 1e-05
negative = -1e30
floor = -1e20
log2e = 1.4426950408889634
to_base2 = log2e * HEAD_DIM**-0.5
bf16 = jnp.bfloat16
f32 = jnp.float32


def forward_mul(left, right):
    return jnp.einsum("rti,ij->rtj", left, right, preferred_element_type=f32)


def backward_mul(left, right):
    return jnp.einsum("rtj,ij->rti", left, right, preferred_element_type=f32)


def weight_mul(left, right):
    return jnp.einsum("rti,rtj->ij", left, right, preferred_element_type=f32)


def norm_parts(values):
    centered = values - jnp.mean(values, axis=-1, keepdims=True)
    variance = jnp.mean(centered * centered, axis=-1, keepdims=True)
    scale = lax.rsqrt(variance + epsilon)
    return centered * scale, scale


def norm_back(unit, scale, gain, grad):
    inner = grad * gain
    first = jnp.mean(inner, axis=-1, keepdims=True)
    second = jnp.mean(inner * unit, axis=-1, keepdims=True)
    return (
        scale * (inner - first - unit * second),
        jnp.sum(grad * unit, axis=(0, 1)),
        jnp.sum(grad, axis=(0, 1)),
    )


def mul_nt(left, right):
    return lax.dot_general(left, right, (((1,), (1,)), ((), ())), preferred_element_type=f32)


def mul_nn(left, right):
    return lax.dot_general(left, right, (((1,), (0,)), ((), ())), preferred_element_type=f32)


def spread_heads(block, heads):
    if heads == 1:
        return block
    width = block.shape[1]
    lane = lax.broadcasted_iota(jnp.int32, (1, width), 1)
    copies = []
    for head in range(heads):
        inside = (lane >= head * HEAD_DIM) & (lane < (head + 1) * HEAD_DIM)
        copies.append(block * jnp.where(inside, 1.0, 0.0).astype(block.dtype))
    return jnp.concatenate(copies, axis=0)


def tile_lanes(block, heads):
    return jnp.concatenate([block] * heads, axis=1) if heads > 1 else block


def row_of(ref, heads):
    rows = [ref[0, head : head + 1, :] for head in range(heads)]
    return jnp.concatenate(rows, axis=1) if heads > 1 else rows[0]


def store_rows(ref, row, heads, count):
    for head in range(heads):
        ref[0, head : head + 1, :] = row[:, head * count : (head + 1) * count]


def head_products(left, right, heads, count):
    pieces = [
        mul_nn(
            left[head * HEAD_DIM : (head + 1) * HEAD_DIM, :],
            right[:, head * count : (head + 1) * count],
        )
        for head in range(heads)
    ]
    return jnp.concatenate(pieces, axis=0) if heads > 1 else pieces[0]


def head_scale(row, heads, count):
    pieces = [
        jnp.broadcast_to(row[:, head * count : (head + 1) * count], (HEAD_DIM, count))
        for head in range(heads)
    ]
    return jnp.concatenate(pieces, axis=0) if heads > 1 else pieces[0]


def cross_forward_kernel(heads, blocks, tile, shift_ref, table_ref, *refs):
    queries = refs[:blocks]
    target_ids, source_ids, keys, values = refs[blocks : blocks + 4]
    mixed = refs[blocks + 4 : 2 * blocks + 4]
    sums = refs[2 * blocks + 4 : 3 * blocks + 4]
    turned, total = refs[3 * blocks + 4 :]
    place = pl.program_id(0)
    count = queries[0].shape[1]
    tiles = keys.shape[1] // tile
    for step in range(tiles):
        turned[step] = values[0, step * tile : (step + 1) * tile, :].T
    for block in range(blocks):
        spread = spread_heads(queries[block][0], heads)
        ids = target_ids[0, block : block + 1, :]
        total[...] = jnp.zeros_like(total)

        def visit(step, carry):
            best, weight = carry
            start = pl.multiple_of(step * tile, tile)
            scores = mul_nt(keys[0, pl.ds(start, tile), :], spread) * to_base2
            allowed = source_ids[0, pl.ds(start, tile), :] == ids
            scores = jnp.where(tile_lanes(allowed, heads), scores, negative)
            fresh = jnp.maximum(best, jnp.max(scores, axis=0, keepdims=True))
            anchor = jnp.maximum(fresh, floor)
            probs = jnp.exp2(scores - anchor)
            fade = jnp.exp2(best - anchor)
            weight = weight * fade + jnp.sum(probs, axis=0, keepdims=True)
            total[...] = total[...] * head_scale(fade, heads, count) + head_products(
                turned[step], probs.astype(bf16), heads, count
            )
            return fresh, weight

        best, weight = lax.fori_loop(
            table_ref[place, 2 * block],
            table_ref[place, 2 * block + 1],
            visit,
            (jnp.full((1, heads * count), negative, f32), jnp.zeros((1, heads * count), f32)),
        )
        some = weight > 0.0
        safe = jnp.where(some, weight, 1.0)
        scaled = total[...] * head_scale(1.0 / safe, heads, count)
        mixed[block][0] = scaled.T.astype(bf16)
        store_rows(sums[block], jnp.where(some, best + jnp.log2(safe), negative), heads, count)


def cross_backward_kernel(heads, blocks, tile, shift_ref, table_ref, *refs):
    queries = refs[:blocks]
    grads = refs[blocks : 2 * blocks]
    sums = refs[2 * blocks : 3 * blocks]
    deltas = refs[3 * blocks : 4 * blocks]
    target_ids, source_ids, keys, values = refs[4 * blocks : 4 * blocks + 4]
    query_grads = refs[4 * blocks + 4 : 5 * blocks + 4]
    source_side, turned, key_grad, value_grad, total = refs[5 * blocks + 4 :]
    place = pl.program_id(0)
    count = queries[0].shape[1]
    tiles = keys.shape[1] // tile
    for step in range(tiles):
        turned[step] = keys[0, step * tile : (step + 1) * tile, :].T
    key_grad[...] = jnp.zeros_like(key_grad)
    value_grad[...] = jnp.zeros_like(value_grad)
    for block in range(blocks):
        spread = spread_heads(queries[block][0], heads)
        spread_grad = spread_heads(grads[block][0], heads)
        offset = row_of(sums[block], heads)
        delta = row_of(deltas[block], heads)
        ids = target_ids[0, block : block + 1, :]
        total[...] = jnp.zeros_like(total)

        def visit(step, carry):
            start = pl.multiple_of(step * tile, tile)
            span = pl.ds(start, tile)
            scores = mul_nt(keys[0, span, :], spread) * to_base2
            allowed = source_ids[0, span, :] == ids
            probs = jnp.where(tile_lanes(allowed, heads), jnp.exp2(scores - offset), 0.0)
            dprobs = mul_nt(values[0, span, :], spread_grad)
            dscores = (probs * (dprobs - delta)).astype(bf16)
            key_grad[span, :] += mul_nn(dscores, spread)
            value_grad[span, :] += mul_nn(probs.astype(bf16), spread_grad)
            total[...] += head_products(turned[step], dscores, heads, count)
            return carry

        lax.fori_loop(table_ref[place, 2 * block], table_ref[place, 2 * block + 1], visit, 0)
        query_grads[block][0] = (total[...] * HEAD_DIM**-0.5).T.astype(bf16)
    source_side[0] = jnp.concatenate(
        [(key_grad[...] * HEAD_DIM**-0.5).astype(bf16), value_grad[...].astype(bf16)], axis=1
    )


def self_scores(heads, queries, keys, source_ids, ids):
    spread = spread_heads(queries, heads)
    scores = mul_nt(keys, spread) * to_base2
    count = queries.shape[0]
    slots = keys.shape[0]
    key_place = lax.broadcasted_iota(jnp.int32, (slots, count), 0) - (slots - count)
    query_place = lax.broadcasted_iota(jnp.int32, (slots, count), 1)
    allowed = (source_ids == ids) & (key_place <= query_place)
    return spread, scores, tile_lanes(allowed, heads)


def with_halo(halo, own):
    missing = own.shape[0] - halo.shape[0]
    return jnp.concatenate([jnp.zeros((missing, own.shape[1]), own.dtype), halo, own], axis=0)


def self_forward_kernel(heads, shift_ref, *refs):
    queries, keys, values, key_halo, value_halo, target_ids, source_ids, mixed, sums = refs
    count = queries.shape[1]
    every_key = with_halo(key_halo[0], keys[0])
    every_value = with_halo(value_halo[0], values[0])
    _, scores, allowed = self_scores(
        heads, queries[0], every_key, source_ids[0], target_ids[0, 0:1, :]
    )
    scores = jnp.where(allowed, scores, negative)
    best = jnp.max(scores, axis=0, keepdims=True)
    probs = jnp.exp2(scores - best)
    weight = jnp.sum(probs, axis=0, keepdims=True)
    total = head_products(every_value.T, probs.astype(bf16), heads, count)
    mixed[0] = (total * head_scale(1.0 / weight, heads, count)).T.astype(bf16)
    store_rows(sums, best + jnp.log2(weight), heads, count)


def self_backward_kernel(heads, shift_ref, *refs):
    queries, keys, values, key_halo, value_halo, target_ids, source_ids, sums, grads = refs[:9]
    query_grad, key_own, value_own, side = refs[9:]
    count = queries.shape[1]
    every_key = with_halo(key_halo[0], keys[0])
    every_value = with_halo(value_halo[0], values[0])
    spread, scores, allowed = self_scores(
        heads, queries[0], every_key, source_ids[0], target_ids[0, 0:1, :]
    )
    spread_grad = spread_heads(grads[0], heads)
    probs = jnp.where(allowed, jnp.exp2(scores - row_of(sums, heads)), 0.0)
    dprobs = mul_nt(every_value, spread_grad)
    delta = jnp.sum(probs * dprobs, axis=0, keepdims=True)
    dscores = (probs * (dprobs - delta)).astype(bf16)
    key_grad = mul_nn(dscores, spread) * HEAD_DIM**-0.5
    value_grad = mul_nn(probs.astype(bf16), spread_grad)
    total = head_products(every_key.T, dscores, heads, count)
    query_grad[0] = (total * HEAD_DIM**-0.5).T.astype(bf16)
    slots = every_key.shape[0]
    first = slots - count - HALO
    key_own[0] = key_grad[slots - count :, :]
    value_own[0] = value_grad[slots - count :, :]
    side[0] = jnp.concatenate(
        [
            key_grad[first : slots - count, :].astype(bf16),
            value_grad[first : slots - count, :].astype(bf16),
        ],
        axis=1,
    )


def column_block(array, index, width):
    if width % 128 == 0:
        return array, index
    return array[..., index * width : (index + 1) * width], 0


def rolled(rows, half):
    def at(step, shift):
        return lax.rem(step + shift[0] * half, rows)

    return at


def cross_call(backward, heads, queries, extra, target_ids, source_ids, kv, table, shift):
    blocks = len(queries)
    rows, count, width = queries[0].shape
    slots = kv.shape[1]
    tile = min(SOURCE_TILE, slots)
    keys, key_column = column_block(kv, 0, width)
    values, value_column = column_block(kv, 1, width)
    turn = rolled(rows, rows // 2)
    token = pl.BlockSpec((1, count, width), lambda i, s, t: (turn(i, s), 0, 0))
    stat = pl.BlockSpec((1, heads, count), lambda i, s, t: (turn(i, s), 0, 0))
    in_specs = [token] * blocks
    operands = list(queries)
    if backward:
        grads, sums, deltas = extra
        in_specs += [token] * blocks + [stat] * (2 * blocks)
        operands += list(grads) + list(sums) + list(deltas)
    in_specs += [
        pl.BlockSpec((1, blocks, count), lambda i, s, t: (i, 0, 0)),
        pl.BlockSpec((1, slots, 1), lambda i, s, t: (i, 0, 0)),
        pl.BlockSpec((1, slots, width), lambda i, s, t: (i, 0, key_column)),
        pl.BlockSpec((1, slots, width), lambda i, s, t: (i, 0, value_column)),
    ]
    operands += [target_ids, source_ids, keys, values]
    token_out = jax.ShapeDtypeStruct((rows, count, width), bf16)
    stat_out = jax.ShapeDtypeStruct((rows, heads, count), f32)
    scratch = [pltpu.VMEM((slots // tile, width, tile), bf16)]
    if backward:
        out_shape = [token_out] * blocks + [jax.ShapeDtypeStruct((rows, slots, 2 * width), bf16)]
        out_specs = [token] * blocks + [
            pl.BlockSpec((1, slots, 2 * width), lambda i, s, t: (i, 0, 0))
        ]
        scratch += [pltpu.VMEM((slots, width), f32), pltpu.VMEM((slots, width), f32)]
    else:
        out_shape = [token_out] * blocks + [stat_out] * blocks
        out_specs = [token] * blocks + [stat] * blocks
    scratch += [pltpu.VMEM((width, count), f32)]
    work = rows * slots * blocks * count * width // 2
    return pl.pallas_call(
        functools.partial(
            cross_backward_kernel if backward else cross_forward_kernel, heads, blocks, tile
        ),
        grid_spec=pltpu.PrefetchScalarGridSpec(
            num_scalar_prefetch=2,
            grid=(rows,),
            in_specs=in_specs,
            out_specs=out_specs,
            scratch_shapes=scratch,
        ),
        out_shape=out_shape,
        compiler_params=pltpu.CompilerParams(vmem_limit_bytes=40 * 2**20),
        cost_estimate=pl.CostEstimate(
            flops=work * (20 if backward else 8),
            bytes_accessed=rows * slots * width * (8 if backward else 4),
            transcendentals=0,
        ),
        name="cross_backward" if backward else "cross_forward",
    )(shift, table, *operands)


def self_call(backward, heads, qkv, halo, extra, target_ids, source_ids, width, shift):
    rows, count = qkv.shape[:2]
    turn = rolled(rows, rows // 2)
    in_specs, operands = [], []
    for index in range(3):
        operand, column = column_block(qkv, index, width)
        operands.append(operand)
        in_specs.append(
            pl.BlockSpec((1, count, width), lambda i, s, at=column: (turn(i, s), 0, at))
        )
    for index in range(2):
        operand, column = column_block(halo, index, width)
        operands.append(operand)
        in_specs.append(pl.BlockSpec((1, HALO, width), lambda i, s, at=column: (turn(i, s), 0, at)))
    token = pl.BlockSpec((1, count, width), lambda i, s: (turn(i, s), 0, 0))
    stat = pl.BlockSpec((1, heads, count), lambda i, s: (turn(i, s), 0, 0))
    in_specs += [
        pl.BlockSpec((1, 1, count), lambda i, s: (i, 0, 0)),
        pl.BlockSpec((1, 2 * count, 1), lambda i, s: (i, 0, 0)),
    ]
    operands += [target_ids, source_ids]
    token_shape = (rows, count, width)
    if backward:
        in_specs += [stat, token]
        operands += list(extra)
        out_shape = [
            jax.ShapeDtypeStruct(token_shape, bf16),
            jax.ShapeDtypeStruct(token_shape, f32),
            jax.ShapeDtypeStruct(token_shape, f32),
            jax.ShapeDtypeStruct((rows, HALO, 2 * width), bf16),
        ]
        out_specs = [
            token,
            token,
            token,
            pl.BlockSpec((1, HALO, 2 * width), lambda i, s: (turn(i, s), 0, 0)),
        ]
    else:
        out_shape = [
            jax.ShapeDtypeStruct(token_shape, bf16),
            jax.ShapeDtypeStruct((rows, heads, count), f32),
        ]
        out_specs = [token, stat]
    work = rows * count * count * width
    return pl.pallas_call(
        functools.partial(self_backward_kernel if backward else self_forward_kernel, heads),
        grid_spec=pltpu.PrefetchScalarGridSpec(
            num_scalar_prefetch=1, grid=(rows,), in_specs=in_specs, out_specs=out_specs
        ),
        out_shape=out_shape,
        compiler_params=pltpu.CompilerParams(vmem_limit_bytes=40 * 2**20),
        cost_estimate=pl.CostEstimate(
            flops=work * (40 if backward else 16),
            bytes_accessed=rows * count * width * 12,
            transcendentals=0,
        ),
        name="self_backward" if backward else "self_forward",
    )(shift, *operands)


def send_blk(array, distance, size):
    return lax.ppermute(array, "blk", [(i, (i + distance) % size) for i in range(size)])


def send_sibling(array, size):
    return lax.ppermute(array, "tensor", [(i, i ^ 1) for i in range(size)])


def settle(array):
    return lax.optimization_barrier(array.astype(bf16))


def sum_tensor(mine, other, size):
    total = mine + send_sibling(other.astype(bf16), size).astype(f32)
    step = 2
    while step < size:
        low = settle(total)
        total = low.astype(f32) + lax.ppermute(
            low, "tensor", [(i, i ^ step) for i in range(size)]
        ).astype(f32)
        step *= 2
    return total


def halves(array):
    half = array.shape[0] // 2
    return array[:half], array[half:]


def on_device(
    target,
    source,
    target_segments,
    source_segments,
    self_query,
    self_key,
    self_value,
    self_output,
    cross_query,
    cross_key,
    cross_value,
    cross_output,
    ffn_in,
    ffn_out,
    adapter_down,
    adapter_up,
    first_gain,
    first_shift,
    second_gain,
    second_shift,
    third_gain,
    third_shift,
    out_cotangent,
):
    rows, count, depth = target.shape
    slots = source.shape[1]
    width = self_query.shape[1]
    heads = width // HEAD_DIM
    blocks = lax.axis_size("blk")
    lanes = lax.axis_size("tensor")
    place = lax.axis_index("blk")
    core = lax.rem(lax.axis_index("tensor"), 2)
    shift = core.astype(jnp.int32).reshape(1)
    many = rows // CHUNKS
    half = many // 2
    tile = min(SOURCE_TILE, slots)

    far_ids = [target_segments] + [
        send_blk(target_segments, step, blocks) for step in range(1, blocks)
    ]
    target_ids = jnp.stack(far_ids, axis=1)
    tiles = source_segments.reshape(rows, slots // tile, tile)
    table = jnp.stack(
        [
            jnp.sum(tiles[:, None, :, -1] < target_ids[:, :, :1], axis=-1, dtype=jnp.int32),
            jnp.sum(tiles[:, None, :, 0] <= target_ids[:, :, -1:], axis=-1, dtype=jnp.int32),
        ],
        axis=-1,
    ).reshape(rows, 2 * blocks)
    source_ids = source_segments[:, :, None]
    halo_ids = jnp.where(place == 0, -1, far_ids[1][:, count - HALO :]) if blocks > 1 else None
    if halo_ids is None:
        halo_ids = jnp.full((rows, HALO), -1, jnp.int32)
    self_ids = jnp.concatenate(
        [jnp.full((rows, count - HALO), -1, jnp.int32), halo_ids, target_segments], axis=1
    )[:, :, None]

    qkv_weight = jnp.concatenate([self_query, self_key, self_value], axis=1)
    kv_weight = jnp.concatenate([cross_key, cross_value], axis=1)

    def ordered(array, chunk):
        mine = lax.dynamic_slice_in_dim(array, chunk * many + core * half, half, 0)
        other = lax.dynamic_slice_in_dim(array, chunk * many + (1 - core) * half, half, 0)
        return mine, other

    def share(mine):
        return jnp.concatenate([mine, send_sibling(mine, lanes)], axis=0)

    def reduced(part_of):
        other = part_of(1)
        return sum_tensor(part_of(0), other, lanes)

    vectors = []
    weights = {}

    def add_weight(name, value):
        weights[name] = weights[name] + value if name in weights else value

    outputs = []
    for chunk in range(CHUNKS):
        own = slice(chunk * many, (chunk + 1) * many)
        target_mine, target_other = ordered(target, chunk)
        tokens = jnp.concatenate([target_mine, target_other], axis=0)
        cotangent, _ = ordered(out_cotangent, chunk)
        ids_here = target_ids[own]
        table_here = table[own]
        source_ids_here = source_ids[own]
        self_ids_here = self_ids[own]
        source_here = source[own]

        qkv = forward_mul(tokens, qkv_weight).astype(bf16)
        halo = send_blk(qkv[:, count - HALO :, width:], 1, blocks)
        self_low, self_sums = self_call(
            False, heads, qkv, halo, (), ids_here[:, :1], self_ids_here, width, shift
        )
        self_halves = halves(self_low)
        first_in = target_mine.astype(f32) + reduced(
            lambda at: forward_mul(self_halves[at], self_output)
        )
        first_unit, first_scale = norm_parts(first_in)
        first = first_unit * first_gain + first_shift
        first_low = share(first.astype(bf16))

        kv = forward_mul(source_here, kv_weight).astype(bf16)
        cross_q = forward_mul(first_low, cross_query).astype(bf16)
        far_q = [cross_q] + [send_blk(cross_q, step, blocks) for step in range(1, blocks)]
        visited = cross_call(
            False, heads, far_q, (), ids_here, source_ids_here, kv, table_here, shift
        )
        back_mixed = [visited[0]] + [
            send_blk(visited[step], -step, blocks) for step in range(1, blocks)
        ]
        back_sums = [visited[blocks]] + [
            send_blk(visited[blocks + step], -step, blocks) for step in range(1, blocks)
        ]
        best = functools.reduce(jnp.maximum, back_sums)
        shares = [jnp.exp2(each - best) for each in back_sums]
        whole = functools.reduce(jnp.add, shares)
        cross_sums = best + jnp.log2(whole)
        cross_mixed = jnp.zeros(cross_q.shape, f32)
        for part, each in zip(back_mixed, shares):
            by_slot = jnp.transpose(each / whole, (0, 2, 1))
            cross_mixed += part.astype(f32) * jnp.repeat(by_slot, HEAD_DIM, axis=2)
        cross_low = cross_mixed.astype(bf16)
        far_sums = [cross_sums] + [send_blk(cross_sums, step, blocks) for step in range(1, blocks)]
        cross_halves = halves(cross_low)
        second_in = first + reduced(lambda at: forward_mul(cross_halves[at], cross_output))
        second_unit, second_scale = norm_parts(second_in)
        second = second_unit * second_gain + second_shift
        second_low = share(second.astype(bf16))

        gate = forward_mul(second_low, ffn_in)
        normal = 0.5 * (1.0 + lax.erf(gate * 0.5**0.5))
        active = (gate * normal).astype(bf16)
        gate_slope = normal + gate * jnp.exp(-0.5 * gate * gate) * 0.3989422804014327
        down = forward_mul(second_low, adapter_down)
        smooth = jax.nn.sigmoid(down)
        rectified = (down * smooth).astype(bf16)
        down_slope = smooth * (1.0 + down * (1.0 - smooth))
        active_halves, rect_halves = halves(active), halves(rectified)
        third_in = second + reduced(
            lambda at: forward_mul(active_halves[at], ffn_out)
            + 4.0 * forward_mul(rect_halves[at], adapter_up)
        )
        third_unit, third_scale = norm_parts(third_in)
        result = (third_unit * third_gain + third_shift).astype(bf16)
        third_grad, third_gain_grad, third_shift_grad = norm_back(
            third_unit, third_scale, third_gain, cotangent.astype(f32)
        )
        branch_grad = share(third_grad.astype(bf16))
        result_other = send_sibling(result, lanes)

        gate_grad = (backward_mul(branch_grad, ffn_out) * gate_slope).astype(bf16)
        down_grad = (4.0 * backward_mul(branch_grad, adapter_up) * down_slope).astype(bf16)
        gate_halves, down_halves = halves(gate_grad), halves(down_grad)
        second_grad = third_grad + reduced(
            lambda at: backward_mul(gate_halves[at], ffn_in)
            + backward_mul(down_halves[at], adapter_down)
        )
        add_weight("adapter_up", 4.0 * weight_mul(rectified, branch_grad))
        add_weight("adapter_down", weight_mul(second_low, down_grad))
        cross_grad, second_gain_grad, second_shift_grad = norm_back(
            second_unit, second_scale, second_gain, second_grad
        )
        cross_branch = share(cross_grad.astype(bf16))

        mixed_grad = backward_mul(cross_branch, cross_output).astype(bf16)
        far_grads = [mixed_grad] + [send_blk(mixed_grad, step, blocks) for step in range(1, blocks)]
        product = mixed_grad.astype(f32) * cross_low.astype(f32)
        delta = jnp.transpose(
            jnp.sum(product.reshape(many, count, heads, HEAD_DIM), axis=-1), (0, 2, 1)
        )
        far_deltas = [delta] + [send_blk(delta, step, blocks) for step in range(1, blocks)]
        visited = cross_call(
            True,
            heads,
            far_q,
            (far_grads, far_sums, far_deltas),
            ids_here,
            source_ids_here,
            kv,
            table_here,
            shift,
        )
        kv_grad = visited[blocks]
        cross_q_sum = visited[0].astype(f32)
        for step in range(1, blocks):
            cross_q_sum += send_blk(visited[step], -step, blocks).astype(f32)
        cross_q_low = cross_q_sum.astype(bf16)
        add_weight("cross_output", weight_mul(cross_low, cross_branch))
        add_weight("cross_kv", weight_mul(source_here, kv_grad))
        source_terms = backward_mul(kv_grad, kv_weight).astype(bf16)
        source_grad = lax.psum_scatter(
            source_terms, "tensor", scatter_dimension=2, tiled=True
        ).astype(f32)
        query_halves = halves(cross_q_low)
        first_grad = cross_grad + reduced(lambda at: backward_mul(query_halves[at], cross_query))
        add_weight("cross_query", weight_mul(first_low, cross_q_low))
        self_grad, first_gain_grad, first_shift_grad = norm_back(
            first_unit, first_scale, first_gain, first_grad
        )
        self_branch = share(self_grad.astype(bf16))

        self_mixed_grad = backward_mul(self_branch, self_output).astype(bf16)
        q_grad, key_own, value_own, side = self_call(
            True,
            heads,
            qkv,
            halo,
            (self_sums, self_mixed_grad),
            ids_here[:, :1],
            self_ids_here,
            width,
            shift,
        )
        side = lax.ppermute(side, "blk", [(i, i - 1) for i in range(1, blocks)]).astype(f32)
        late = ((0, 0), (count - HALO, 0), (0, 0))
        qkv_grad = jnp.concatenate(
            [
                q_grad,
                (key_own + jnp.pad(side[:, :, :width], late)).astype(bf16),
                (value_own + jnp.pad(side[:, :, width:], late)).astype(bf16),
            ],
            axis=2,
        )
        add_weight("self_output", weight_mul(self_low, self_branch))
        add_weight("self_qkv", weight_mul(tokens, qkv_grad))
        qkv_halves = halves(qkv_grad)
        target_grad = self_grad + reduced(lambda at: backward_mul(qkv_halves[at], qkv_weight))
        target_grad_other = send_sibling(target_grad, lanes)
        vectors.append(
            jnp.stack(
                [
                    first_gain_grad,
                    first_shift_grad,
                    second_gain_grad,
                    second_shift_grad,
                    third_gain_grad,
                    third_shift_grad,
                ]
            )
        )
        outputs.append((result, result_other, target_grad, target_grad_other, source_grad))

    result_all = jnp.zeros((rows, count, depth), bf16)
    target_grad_all = jnp.zeros((rows, count, depth), f32)
    for chunk, (result, result_other, mine, other, _) in enumerate(outputs):
        first_at = chunk * many + core * half
        second_at = chunk * many + (1 - core) * half
        result_all = lax.dynamic_update_slice_in_dim(result_all, result, first_at, 0)
        result_all = lax.dynamic_update_slice_in_dim(result_all, result_other, second_at, 0)
        target_grad_all = lax.dynamic_update_slice_in_dim(target_grad_all, mine, first_at, 0)
        target_grad_all = lax.dynamic_update_slice_in_dim(target_grad_all, other, second_at, 0)
    source_grad_all = jnp.concatenate([each[4] for each in outputs], axis=0)

    vector = functools.reduce(jnp.add, vectors)
    vector = vector + send_sibling(vector, lanes)
    portion = depth // lanes
    vector = lax.dynamic_slice_in_dim(vector, lax.axis_index("tensor") * portion, portion, 1)
    vector = lax.psum(vector, ("dp", "blk"))

    def everywhere(value):
        return lax.psum(value.astype(bf16), ("dp", "blk")).astype(f32)

    qkv_sum = everywhere(weights["self_qkv"])
    kv_sum = everywhere(weights["cross_kv"])
    return (
        result_all,
        target_grad_all,
        source_grad_all,
        qkv_sum[:, :width],
        qkv_sum[:, width : 2 * width],
        qkv_sum[:, 2 * width :],
        everywhere(weights["self_output"]),
        everywhere(weights["cross_query"]),
        kv_sum[:, :width],
        kv_sum[:, width:],
        everywhere(weights["cross_output"]),
        everywhere(weights["adapter_down"]),
        everywhere(weights["adapter_up"]),
        vector[0],
        vector[1],
        vector[2],
        vector[3],
        vector[4],
        vector[5],
    )


def solution(mesh):
    return jax.shard_map(
        on_device,
        mesh=mesh,
        in_specs=(
            P("dp", "blk", None),
            P("dp", "blk", None),
            P("dp", "blk"),
            P("dp", "blk"),
            P(None, "tensor"),
            P(None, "tensor"),
            P(None, "tensor"),
            P("tensor", None),
            P(None, "tensor"),
            P(None, "tensor"),
            P(None, "tensor"),
            P("tensor", None),
            P(None, "tensor"),
            P("tensor", None),
            P(None, "tensor"),
            P("tensor", None),
            P(),
            P(),
            P(),
            P(),
            P(),
            P(),
            P("dp", "blk", None),
        ),
        out_specs=(
            P("dp", "blk", None),
            P("dp", "blk", None),
            P("dp", "blk", "tensor"),
            P(None, "tensor"),
            P(None, "tensor"),
            P(None, "tensor"),
            P("tensor", None),
            P(None, "tensor"),
            P(None, "tensor"),
            P(None, "tensor"),
            P("tensor", None),
            P(None, "tensor"),
            P("tensor", None),
            P("tensor"),
            P("tensor"),
            P("tensor"),
            P("tensor"),
            P("tensor"),
            P("tensor"),
        ),
        check_vma=False,
    )
```

time: 2450 us -> 814 us (0.33)
  waiting for transfers between devices: 1740 us -> 407 us
  matrix products: 426 us -> 86.6 us
  Pallas kernels: 0 us -> 75.6 us
  starting transfers between devices: 1.26 us -> 76.5 us
  other arithmetic: 104 us -> 45.4 us
  local copies, waits for them, and re-layouts: 101 us -> 70.8 us
  blocking collectives: 50.3 us -> 24.6 us
    reduce_scatter x3 -> x1, waiting for transfers between devices: 626 us -> 0.01 us  [on_device(): lax.psum_scatter(source_terms, 'tensor', scatter_dimension=2, tiled=True)]
    all_gather x4 -> x0, waiting for transfers between devices: 551 us -> none  [the longest x1 282 us: on_device(): lax.all_gather(local_source[0], 'blk', axis=1, tiled=True)]
    psum x7 -> x1, waiting for transfers between devices: 565 us -> 87.4 us  [everywhere(): return lax.psum(value.astype(bf16), ('dp', 'blk')).astype(f32)]
    dot_general x45 -> x33, matrix products: 426 us -> 86.6 us  [the longest x13 31.8 us: forward_mul(): return jnp.einsum('rti,ij->rtj', left, right, preferred_element_type=f32)]
    ppermute x0 -> x46, waiting for transfers between devices: none -> 320 us  [the longest x25 160 us: send_blk(): lax.ppermute(array, 'blk', [(i, (i + distance) % size) for i in range(siz...]
    ppermute x0 -> x46, starting transfers between devices: none -> 76.2 us  [the longest x25 64.2 us: send_blk(): lax.ppermute(array, 'blk', [(i, (i + distance) % size) for i in range(siz...]
    pallas_call x0 -> x4, Pallas kernels: none -> 75.6 us  [the longest x2 63.2 us: cross_call(): pl.pallas_call(functools.partial(cross_backward_kernel if backward else c...]
    all_gather x4 -> x0, local copies, waits for them, and re-layouts: 50.8 us -> none  [the longest x1 22 us: on_device(): lax.all_gather(local_source[0], 'blk', axis=1, tiled=True)]
  transfers between devices with their start and end apart: 16 -> 48, of which waited for: 14 -> 29; matrix products, arithmetic and copies ran while one was open for 14% -> 14% of each run, Pallas kernels for 0% -> 0%
where the time goes in v1:
time: 814 us; the launch traced here: 804 us
  waiting for transfers between devices  407 us (50%)
  matrix products  86.6 us (11%)
  starting transfers between devices  76.5 us (9%)
  Pallas kernels  75.6 us (9%)
  local copies, waits for them, and re-layouts  70.8 us (9%)
  other arithmetic  45.4 us (6%)
  blocking collectives  24.6 us (3%)
  between operations  17.1 us (2%)
    ppermute x25, waiting for transfers between devices, send_blk(): lax.ppermute(array, 'blk', [(i, (i + distance) % size) for i in range(siz...  160 us
    ppermute x6, waiting for transfers between devices, sum_tensor(): lax.ppermute(low, 'tensor', [(i, i ^ step) for i in range(size)])  137 us
    psum x1, waiting for transfers between devices, everywhere(): return lax.psum(value.astype(bf16), ('dp', 'blk')).astype(f32)  87.4 us
    ppermute x25, starting transfers between devices, send_blk(): lax.ppermute(array, 'blk', [(i, (i + distance) % size) for i in range(siz...  64.2 us
    pallas_call x2, Pallas kernels, cross_call(): pl.pallas_call(functools.partial(cross_backward_kernel if backward else c...  63.2 us
    unnamed x186, local copies, waits for them, and re-layouts  38.9 us
    dot_general x13, matrix products, forward_mul(): return jnp.einsum('rti,ij->rtj', left, right, preferred_element_type=f32)  31.8 us
    dot_general x13, matrix products, backward_mul(): return jnp.einsum('rtj,ij->rti', left, right, preferred_element_type=f32)  29.4 us
  transfers between devices with their start and end apart: 48, of which 29 were waited for; matrix products, arithmetic and copies ran while one was open for 14% of the time, Pallas kernels for 0%

profile of v1, /device:TPU:0, one launch (start us, length us, event | category | flops | bytes accessed | tf_op | source)
XLA Modules:
  0.0 803.8 jit_solution(16440618910916439600)
XLA Ops:
  13.3 3.0 collective-permute-start
  17.9 15.2 %collective-permute-done.1 = s32[8,128]{1,0:T(8,128)S(1)} collective-permute-done((s32[8,128]{1,0:T(8,128)S(1)}, s32[8,128]{1,0:T(8,128)S(1)}, u32[]{:S(2)}, u32[]{:S(2)}) %collective-permute-start.1) | collective-permute-done | bytes 4128 | tf_op jit(solution)/shard_map/ppermute | solution.py:392
  37.3 5.3 self_forward.1
  43.1 2.6 collective-permute-done.2
  54.5 18.2 %collective-permute-done.3 = bf16[4,128,1024]{2,1,0:T(8,128)(2,1)} collective-permute-done((bf16[4,128,1024]{2,1,0:T(8,128)(2,1)}, bf16[4,128,1024]{2,1,0:T(8,128)(2,1)}, u32[]{:S(2)}, u32[]{:S(2)}) %collective-permute-start.3) | collective-permute-done | bytes 1048608 | tf_op jit(solution)/shard_map/ppermute | solution.py:408
  77.2 17.4 %convert_bitcast_fusion.refs_6_.refs_7_.refs_18_.refs_19_ = bf16[8,1024,512]{2,1,0:T(8,128)(2,1)} fusion(bf16[8,1024,1024]{2,1,0:T(8,128)(2,1)} %param.24, bf16[1024,256]{0,1:T(8,128)(2,1)S(1)} %copy-done.62, bf16[1024,256]{0,1:T(8,128)(2,1)S(1)} %copy-done.60), kind=kOutput, calls=%fused_computation.1 | convolution fusion | flops 8596226048 | bytes 26214400 | tf_op jit(solution)/shard_map/rti,ij->rtj/dot_general | solution.py:25
  94.8 2.7 copy.115.refs_5_.refs_17_
  97.6 3.2 fusion.30.refs_0_
  104.1 12.3 %collective-permute-done.9.refs_3_ = bf16[8,128,256]{2,1,0:T(8,128)(2,1)} collective-permute-done((bf16[8,128,256]{2,1,0:T(8,128)(2,1)}, bf16[8,128,256]{2,1,0:T(8,128)(2,1)}, u32[]{:S(2)}, u32[]{:S(2)}) %collective-permute-start.9) | collective-permute-done | bytes 524320 | tf_op jit(solution)/shard_map/ppermute | solution.py:392
  116.5 31.7 %collective-permute-done.8.refs_2_ = bf16[8,128,256]{2,1,0:T(8,128)(2,1)} collective-permute-done((bf16[8,128,256]{2,1,0:T(8,128)(2,1)}, bf16[8,128,256]{2,1,0:T(8,128)(2,1)}, u32[]{:S(2)}, u32[]{:S(2)}) %collective-permute-start.8) | collective-permute-done | bytes 524320 | tf_op jit(solution)/shard_map/ppermute | solution.py:392
  150.4 29.0 %cross_forward.1 = (bf16[8,128,256]{2,1,0:T(8,128)(2,1)S(1)}, bf16[8,128,256]{2,1,0:T(8,128)(2,1)}, bf16[8,128,256]{2,1,0:T(8,128)(2,1)}, bf16[8,128,256]{2,1,0:...) custom-call(s32[1]{0:T(128)} %bitcast.shift_ref, ...), custom_call_target="tpu_custom_call" | custom-call | flops 4294967296 | bytes 8388608 | tf_op jit(solution)/shard_map/cross_forward/pallas_call | solution.py:309
  180.2 4.9 collective-permute-start.14
  188.9 25.9 %collective-permute-done.10 = f32[8,4,128]{2,1,0:T(4,128)S(1)} collective-permute-done((f32[8,4,128]{2,1,0:T(4,128)S(1)}, f32[8,4,128]{2,1,0:T(4,128)S(1)}, u32[]{:S(2)}, u32[]{:S(2)}) %collective-permute-start.10) | collective-permute-done | bytes 16416 | tf_op jit(solution)/shard_map/ppermute | solution.py:392
  214.8 17.2 %collective-permute-start.12 = (f32[8,4,128]{2,1,0:T(4,128)S(1)}, f32[8,4,128]{2,1,0:T(4,128)S(1)}, u32[]{:S(2)}, u32[]{:S(2)}) collective-permute-start(f32[8,4,128]{2,1,0:T(4,128)S(1)} %get-tuple-element.43), channel_id=1, source_target_pairs={{0,4},{4,8},{8,12},{12,0},{1,5},{5,9},{9,13},{13,1},{2,6},{6,10},{... | collective-permute-start | bytes 49160 | tf_op jit(solution)/shard_map/ppermute | solution.py:392
  247.8 3.4 add_convert_fusion.12
  251.8 2.6 collective-permute-done.16
  256.5 23.7 %collective-permute-done.17 = bf16[4,128,1024]{2,1,0:T(8,128)(2,1)S(1)} collective-permute-done((bf16[4,128,1024]{2,1,0:T(8,128)(2,1)S(1)}, bf16[4,128,1024]{2,1,0:T(8,128)(2,1)S(1)}, u32[]{:S(2)}, u32[]{:S(2)}) %collective-permute-start.17) | collective-permute-done | bytes 1048608 | tf_op jit(solution)/shard_map/ppermute | solution.py:408
  282.3 2.6 collective-permute-done.18
  295.0 23.7 %collective-permute-done.20 = bf16[4,128,1024]{2,1,0:T(8,128)(2,1)S(1)} collective-permute-done((bf16[4,128,1024]{2,1,0:T(8,128)(2,1)S(1)}, bf16[4,128,1024]{2,1,0:T(8,128)(2,1)S(1)}, u32[]{:S(2)}, u32[]{:S(2)}) %collective-permute-start.20) | collective-permute-done | bytes 1048608 | tf_op jit(solution)/shard_map/ppermute | solution.py:408
  321.9 9.8 %fusion.12 = (f32[1024]{0:T(1024)S(1)}, f32[4,128]{1,0:T(4,128)S(1)}, f32[4,128]{1,0:T(4,128)S(1)}, f32[1024]{0:T(1024)S(1)}) fusion(f32[4,128,1024]{2,1,0:T(8,128)S(1)} %get-tuple-element.143, f32[4,128]{1,0:T(4,128)S(1)} %add_rsqrt_fusion, f32[4,128]{1,0:T(4,128)S(1)} %broadcast_multiply_fusion.6, bf16[8,128,1024]{2,1,0:T(8,128)(2,1)S(1)} %copy-done.34, ...), kind=kLoop, calls=%fused_computation.21 | loop fusion | flops 5239808 | bytes 3166212 | tf_op jit(solution)/shard_map/reduce_sum | solution.py:49
  332.4 2.6 collective-permute-done.22
  335.1 3.9 fusion.5
  346.3 23.7 %collective-permute-done.24 = bf16[4,128,1024]{2,1,0:T(8,128)(2,1)S(1)} collective-permute-done((bf16[4,128,1024]{2,1,0:T(8,128)(2,1)S(1)}, bf16[4,128,1024]{2,1,0:T(8,128)(2,1)S(1)}, u32[]{:S(2)}, u32[]{:S(2)}) %collective-permute-start.24) | collective-permute-done | bytes 1048608 | tf_op jit(solution)/shard_map/ppermute | solution.py:408
  373.4 2.7 collective-permute-done.25
  378.5 3.1 collective-permute-start.27
  381.6 3.8 collective-permute-start.31
  389.3 23.8 %collective-permute-done.31.refs_11_ = f32[8,4,128]{2,1,0:T(4,128)S(1)} collective-permute-done((f32[8,4,128]{2,1,0:T(4,128)S(1)}, f32[8,4,128]{2,1,0:T(4,128)S(1)}, u32[]{:S(2)}, u32[]{:S(2)}) %collective-permute-start.31) | collective-permute-done | bytes 16416 | tf_op jit(solution)/shard_map/ppermute | solution.py:392
  413.1 15.9 %collective-permute-start.29 = (f32[8,4,128]{2,1,0:T(4,128)S(1)}, f32[8,4,128]{2,1,0:T(4,128)S(1)}, u32[]{:S(2)}, u32[]{:S(2)}) collective-permute-start(f32[8,4,128]{2,1,0:T(4,128)S(1)} %get-tuple-element.136.refs_8_), channel_id=1, source_target_pairs={{0,4},{4,8},{8,12},{12,0},{1,5},{5,9},{9,13},{13,1},{2,6},{6,10},{... | collective-permute-start | bytes 49160 | tf_op jit(solution)/shard_map/ppermute | solution.py:392
  435.3 3.0 collective-permute-done.32.refs_13_
  447.1 34.2 %cross_backward.1 = (bf16[8,128,256]{2,1,0:T(8,128)(2,1)S(1)}, bf16[8,128,256]{2,1,0:T(8,128)(2,1)S(1)}, bf16[8,128,256]{2,1,0:T(8,128)(2,1)S(1)}, bf16[8,128,256]{2,1,0:T(8,128)(2,1)S(1)}, bf16[8,1024,512]{2,1,0:T(8,128)(2,1)}) custom-call(s32[1]{0:T(128)} %bitcast.shift_ref, s32[8,8]{1,0:T(8,128)S(1)} %copy.114.table_ref, ...), custom_call_target="tpu_custom_call" | custom-call | flops 10737418240 | bytes 16777216 | tf_op jit(solution)/shard_map/cross_backward/pallas_call | solution.py:309
  481.5 3.5 collective-permute-start.36
  485.0 9.0 %collective-permute-done.35 = bf16[8,128,256]{2,1,0:T(8,128)(2,1)S(1)} collective-permute-done((bf16[8,128,256]{2,1,0:T(8,128)(2,1)S(1)}, bf16[8,128,256]{2,1,0:T(8,128)(2,1)S(1)}, u32[]{:S(2)}, u32[]{:S(2)}) %collective-permute-start.35) | collective-permute-done | bytes 524320 | tf_op jit(solution)/shard_map/ppermute | solution.py:392
  493.9 33.1 %collective-permute-done.36 = bf16[8,128,256]{2,1,0:T(8,128)(2,1)S(1)} collective-permute-done((bf16[8,128,256]{2,1,0:T(8,128)(2,1)S(1)}, bf16[8,128,256]{2,1,0:T(8,128)(2,1)S(1)}, u32[]{:S(2)}, u32[]{:S(2)}) %collective-permute-start.36) | collective-permute-done | bytes 524320 | tf_op jit(solution)/shard_map/ppermute | solution.py:392
  527.9 2.6 collective-permute-done.38
  532.6 23.7 %collective-permute-done.39 = bf16[4,128,1024]{2,1,0:T(8,128)(2,1)S(1)} collective-permute-done((bf16[4,128,1024]{2,1,0:T(8,128)(2,1)S(1)}, bf16[4,128,1024]{2,1,0:T(8,128)(2,1)S(1)}, u32[]{:S(2)}, u32[]{:S(2)}) %collective-permute-start.39) | collective-permute-done | bytes 1048608 | tf_op jit(solution)/shard_map/ppermute | solution.py:408
  567.4 7.0 self_backward.1
  575.8 13.4 %fusion.26 = bf16[1024,512]{0,1:T(8,128)(2,1)} fusion(bf16[8,1024,512]{2,1,0:T(8,128)(2,1)S(1)} %bitcast.196, bf16[8,1024,1024]{2,1,0:T(8,128)(2,1)} %param.24), kind=kOutput, calls=%fused_computation.80 | convolution fusion | flops 8590458880 | bytes 26214400 | tf_op jit(solution)/shard_map/rti,rtj->ij/dot_general | solution.py:33
  589.2 3.1 fusion.34
  595.5 3.0 bitcast_convert_fusion
  599.7 15.8 %convolution_convert_fusion = bf16[8,1024,1024]{2,1,0:T(8,128)(2,1)} fusion(bf16[8,1024,512]{2,1,0:T(8,128)(2,1)} %get-tuple-element.56, bf16[1024,256]{0,1:T(8,128)(2,1)S(1)} %copy-done.63, bf16[1024,256]{0,1:T(8,128)(2,1)S(1)} %copy-done.61), kind=kOutput, calls=%fused_computation | convolution fusion | flops 8600420352 | bytes 26214400 | tf_op jit(solution)/shard_map/rtj,ij->rti/dot_general | solution.py:29
  618.2 2.6 collective-permute-done.42
  623.5 23.7 %collective-permute-done.43 = bf16[4,128,1024]{2,1,0:T(8,128)(2,1)S(1)} collective-permute-done((bf16[4,128,1024]{2,1,0:T(8,128)(2,1)S(1)}, bf16[4,128,1024]{2,1,0:T(8,128)(2,1)S(1)}, u32[]{:S(2)}, u32[]{:S(2)}) %collective-permute-start.43) | collective-permute-done | bytes 1048608 | tf_op jit(solution)/shard_map/ppermute | solution.py:408
  650.2 2.9 copy-done.28
  658.6 24.6 %psum.63 = f32[6,256]{1,0:T(8,128)S(1)} all-reduce(f32[6,256]{1,0:T(8,128)S(1)} %dynamic-slice_add_fusion), channel_id=1, replica_groups=mesh['dp'=2,'blk'=4,'tensor'=4] {'dp','blk'}, use_global_device_ids=true, to_apply=%region_29.30 | all-reduce | flops 1536 | bytes 12288 | tf_op jit(solution)/shard_map/psum | solution.py:680
  683.8 3.2 constant_dynamic-update-slice_fusion
  687.0 87.4 %all-reduce.5.cloned.1.call-done = (bf16[1024,768]{1,0:T(8,128)(2,1)}, bf16[1024,512]{0,1:T(8,128)(2,1)}, bf16[256,1024]{1,0:T(8,128)(2,1)}, bf16[1024,256]{1,0:...) async-done(((bf16[1024,768]{1,0:T(8,128)(2,1)}, bf16[1024,512]{0,1:T(8,128)(2,1)}, bf16[256,1024]{1,0:T(8,128)(2,1)}, ...) | async-done | bytes 4718608 | tf_op jit(solution)/shard_map/psum | solution.py:683
  783.7 2.6 copy.133
  789.4 6.5 convert_element_type.314
  (352 shorter events, 147.4 us)
Async XLA Ops:
  8.0 766.4 %all-reduce.5.cloned.1.call-start = ((), (), s32[]{:S(2)}) async-start(), calls=%async_computation.2 | async-start | bytes 9437184 | tf_op jit(solution)/shard_map/psum | solution.py:683
  13.3 21.4 %collective-permute-start = (bf16[8,80,512]{2,1,0:T(8,128)(2,1)S(1)}, bf16[8,80,512]{2,1,0:T(8,128)(2,1)S(1)}, u32[]{:S(2)}, u32[]{:S(2)}) collective-permute-start(bf16[8,80,512]{2,1,0:T(8,128)(2,1)S(1)} %slice.140), channel_id=1, source_target_pairs={{0,4},{4,8},{8,12},{12,0},{1,5},{5,9},{9,13},{13,1},{2,6},{6,10},{... | collective-permute-start | bytes 1966088 | tf_op jit(solution)/shard_map/ppermute | solution.py:392
  16.3 16.8 %collective-permute-start.1 = (s32[8,128]{1,0:T(8,128)S(1)}, s32[8,128]{1,0:T(8,128)S(1)}, u32[]{:S(2)}, u32[]{:S(2)}) collective-permute-start(s32[8,128]{1,0:T(8,128)S(1)} %copy-done.10), channel_id=1, source_target_pairs={{0,4},{4,8},{8,12},{12,0},{1,5},{5,9},{9,13},{13,1},{2,6},{6,10},{... | collective-permute-start | bytes 12296 | tf_op jit(solution)/shard_map/ppermute | solution.py:392
  43.0 2.7 collective-permute-start.2
  47.2 25.5 %collective-permute-start.3 = (bf16[4,128,1024]{2,1,0:T(8,128)(2,1)}, bf16[4,128,1024]{2,1,0:T(8,128)(2,1)}, u32[]{:S(2)}, u32[]{:S(2)}) collective-permute-start(bf16[4,128,1024]{2,1,0:T(8,128)(2,1)} %add_convert_fusion.8), channel_id=1, source_target_pairs={{0,2},{1,3},{2,0},{3,1},{4,6},{5,7},{6,4},{7,5},{8,10},{9,11},{10,... | collective-permute-start | bytes 3145736 | tf_op jit(solution)/shard_map/ppermute | solution.py:408
  48.7 48.8 %collective-permute-start.5 = (s32[8,128]{1,0:T(8,128)S(1)}, s32[8,128]{1,0:T(8,128)S(1)}, u32[]{:S(2)}, u32[]{:S(2)}) collective-permute-start(s32[8,128]{1,0:T(8,128)S(1)} %copy-done.10), channel_id=1, source_target_pairs={{0,12},{4,0},{8,4},{12,8},{1,13},{5,1},{9,5},{13,9},{2,14},{6,2},{... | collective-permute-start | bytes 12296 | tf_op jit(solution)/shard_map/ppermute | solution.py:392
  50.4 47.1 %collective-permute-start.4 = (s32[8,128]{1,0:T(8,128)S(1)}, s32[8,128]{1,0:T(8,128)S(1)}, u32[]{:S(2)}, u32[]{:S(2)}) collective-permute-start(s32[8,128]{1,0:T(8,128)S(1)} %copy-done.10), channel_id=1, source_target_pairs={{0,8},{4,12},{8,0},{12,4},{1,9},{5,13},{9,1},{13,5},{2,10},{6,14},... | collective-permute-start | bytes 12296 | tf_op jit(solution)/shard_map/ppermute | solution.py:392
  77.2 20.3 %collective-permute-start.6 = (bf16[4,128,1024]{2,1,0:T(8,128)(2,1)}, bf16[4,128,1024]{2,1,0:T(8,128)(2,1)}, u32[]{:S(2)}, u32[]{:S(2)}) collective-permute-start(bf16[4,128,1024]{2,1,0:T(8,128)(2,1)} %fusion.24), channel_id=1, source_target_pairs={{0,1},{1,0},{2,3},{3,2},{4,5},{5,4},{6,7},{7,6},{8,9},{9,8},{10,11... | collective-permute-start | bytes 3145736 | tf_op jit(solution)/shard_map/ppermute | solution.py:396
  100.7 15.7 %collective-permute-start.9 = (bf16[8,128,256]{2,1,0:T(8,128)(2,1)}, bf16[8,128,256]{2,1,0:T(8,128)(2,1)}, u32[]{:S(2)}, u32[]{:S(2)}) collective-permute-start(bf16[8,128,256]{2,1,0:T(8,128)(2,1)} %fusion.30.refs_0_), channel_id=1, source_target_pairs={{0,12},{4,0},{8,4},{12,8},{1,13},{5,1},{9,5},{13,9},{2,14},{6,2},{... | collective-permute-start | bytes 1572872 | tf_op jit(solution)/shard_map/ppermute | solution.py:392
  102.5 45.7 %collective-permute-start.8 = (bf16[8,128,256]{2,1,0:T(8,128)(2,1)}, bf16[8,128,256]{2,1,0:T(8,128)(2,1)}, u32[]{:S(2)}, u32[]{:S(2)}) collective-permute-start(bf16[8,128,256]{2,1,0:T(8,128)(2,1)} %fusion.30.refs_0_), channel_id=1, source_target_pairs={{0,8},{4,12},{8,0},{12,4},{1,9},{5,13},{9,1},{13,5},{2,10},{6,14},... | collective-permute-start | bytes 1572872 | tf_op jit(solution)/shard_map/ppermute | solution.py:392
  102.5 45.7 %collective-permute-start.7 = (bf16[8,128,256]{2,1,0:T(8,128)(2,1)}, bf16[8,128,256]{2,1,0:T(8,128)(2,1)}, u32[]{:S(2)}, u32[]{:S(2)}) collective-permute-start(bf16[8,128,256]{2,1,0:T(8,128)(2,1)} %fusion.30.refs_0_), channel_id=1, source_target_pairs={{0,4},{4,8},{8,12},{12,0},{1,5},{5,9},{9,13},{13,1},{2,6},{6,10},{... | collective-permute-start | bytes 1572872 | tf_op jit(solution)/shard_map/ppermute | solution.py:392
  180.2 67.6 %collective-permute-start.13 = (bf16[8,128,256]{2,1,0:T(8,128)(2,1)}, bf16[8,128,256]{2,1,0:T(8,128)(2,1)}, u32[]{:S(2)}, u32[]{:S(2)}) collective-permute-start(bf16[8,128,256]{2,1,0:T(8,128)(2,1)} %get-tuple-element.44), channel_id=1, source_target_pairs={{0,12},{4,0},{8,4},{12,8},{1,13},{5,1},{9,5},{13,9},{2,14},{6,2},{... | collective-permute-start | bytes 1572872 | tf_op jit(solution)/shard_map/ppermute | solution.py:392
  180.2 67.6 %collective-permute-start.14 = (bf16[8,128,256]{2,1,0:T(8,128)(2,1)}, bf16[8,128,256]{2,1,0:T(8,128)(2,1)}, u32[]{:S(2)}, u32[]{:S(2)}) collective-permute-start(bf16[8,128,256]{2,1,0:T(8,128)(2,1)} %get-tuple-element.45), channel_id=1, source_target_pairs={{0,8},{4,12},{8,0},{12,4},{1,9},{5,13},{9,1},{13,5},{2,10},{6,14},... | collective-permute-start | bytes 1572872 | tf_op jit(solution)/shard_map/ppermute | solution.py:392
  185.1 62.7 %collective-permute-start.15 = (bf16[8,128,256]{2,1,0:T(8,128)(2,1)}, bf16[8,128,256]{2,1,0:T(8,128)(2,1)}, u32[]{:S(2)}, u32[]{:S(2)}) collective-permute-start(bf16[8,128,256]{2,1,0:T(8,128)(2,1)} %get-tuple-element.46), channel_id=1, source_target_pairs={{0,4},{4,8},{8,12},{12,0},{1,5},{5,9},{9,13},{13,1},{2,6},{6,10},{... | collective-permute-start | bytes 1572872 | tf_op jit(solution)/shard_map/ppermute | solution.py:392
  186.6 28.3 %collective-permute-start.10 = (f32[8,4,128]{2,1,0:T(4,128)S(1)}, f32[8,4,128]{2,1,0:T(4,128)S(1)}, u32[]{:S(2)}, u32[]{:S(2)}) collective-permute-start(f32[8,4,128]{2,1,0:T(4,128)S(1)} %get-tuple-element.41), channel_id=1, source_target_pairs={{0,12},{4,0},{8,4},{12,8},{1,13},{5,1},{9,5},{13,9},{2,14},{6,2},{... | collective-permute-start | bytes 49160 | tf_op jit(solution)/shard_map/ppermute | solution.py:392
  188.9 43.1 %collective-permute-start.11 = (f32[8,4,128]{2,1,0:T(4,128)S(1)}, f32[8,4,128]{2,1,0:T(4,128)S(1)}, u32[]{:S(2)}, u32[]{:S(2)}) collective-permute-start(f32[8,4,128]{2,1,0:T(4,128)S(1)} %get-tuple-element.42), channel_id=1, source_target_pairs={{0,8},{4,12},{8,0},{12,4},{1,9},{5,13},{9,1},{13,5},{2,10},{6,14},... | collective-permute-start | bytes 49160 | tf_op jit(solution)/shard_map/ppermute | solution.py:392
  214.8 18.6 %collective-permute-start.12 = (f32[8,4,128]{2,1,0:T(4,128)S(1)}, f32[8,4,128]{2,1,0:T(4,128)S(1)}, u32[]{:S(2)}, u32[]{:S(2)}) collective-permute-start(f32[8,4,128]{2,1,0:T(4,128)S(1)} %get-tuple-element.43), channel_id=1, source_target_pairs={{0,4},{4,8},{8,12},{12,0},{1,5},{5,9},{9,13},{13,1},{2,6},{6,10},{... | collective-permute-start | bytes 49160 | tf_op jit(solution)/shard_map/ppermute | solution.py:392
  251.7 2.7 collective-permute-start.16
  254.9 25.3 %collective-permute-start.17 = (bf16[4,128,1024]{2,1,0:T(8,128)(2,1)S(1)}, bf16[4,128,1024]{2,1,0:T(8,128)(2,1)S(1)}, u32[]{:S(2)}, u32[]{:S(2)}) collective-permute-start(bf16[4,128,1024]{2,1,0:T(8,128)(2,1)S(1)} %add_convert_fusion.7), channel_id=1, source_target_pairs={{0,2},{1,3},{2,0},{3,1},{4,6},{5,7},{6,4},{7,5},{8,10},{9,11},{10,... | collective-permute-start | bytes 3145736 | tf_op jit(solution)/shard_map/ppermute | solution.py:408
  282.2 2.7 collective-permute-start.18
  290.2 2.7 collective-permute-start.19
  293.5 25.3 %collective-permute-start.20 = (bf16[4,128,1024]{2,1,0:T(8,128)(2,1)S(1)}, bf16[4,128,1024]{2,1,0:T(8,128)(2,1)S(1)}, u32[]{:S(2)}, u32[]{:S(2)}) collective-permute-start(bf16[4,128,1024]{2,1,0:T(8,128)(2,1)S(1)} %add_convert_fusion.5), channel_id=1, source_target_pairs={{0,2},{1,3},{2,0},{3,1},{4,6},{5,7},{6,4},{7,5},{8,10},{9,11},{10,... | collective-permute-start | bytes 3145736 | tf_op jit(solution)/shard_map/ppermute | solution.py:408
  332.4 2.7 collective-permute-start.22
  341.5 2.7 collective-permute-start.23
  344.8 25.3 %collective-permute-start.24 = (bf16[4,128,1024]{2,1,0:T(8,128)(2,1)S(1)}, bf16[4,128,1024]{2,1,0:T(8,128)(2,1)S(1)}, u32[]{:S(2)}, u32[]{:S(2)}) collective-permute-start(bf16[4,128,1024]{2,1,0:T(8,128)(2,1)S(1)} %add_convert_fusion.2), channel_id=1, source_target_pairs={{0,2},{1,3},{2,0},{3,1},{4,6},{5,7},{6,4},{7,5},{8,10},{9,11},{10,... | collective-permute-start | bytes 3145736 | tf_op jit(solution)/shard_map/ppermute | solution.py:408
  373.4 2.7 collective-permute-start.25
  377.8 60.5 %collective-permute-start.28 = (bf16[8,128,256]{2,1,0:T(8,128)(2,1)S(1)}, bf16[8,128,256]{2,1,0:T(8,128)(2,1)S(1)}, u32[]{:S(2)}, u32[]{:S(2)}) collective-permute-start(bf16[8,128,256]{2,1,0:T(8,128)(2,1)S(1)} %get-tuple-element.174.refs_4_), channel_id=1, source_target_pairs={{0,12},{4,0},{8,4},{12,8},{1,13},{5,1},{9,5},{13,9},{2,14},{6,2},{... | collective-permute-start | bytes 1572872 | tf_op jit(solution)/shard_map/ppermute | solution.py:392
  378.5 60.6 %collective-permute-start.27 = (bf16[8,128,256]{2,1,0:T(8,128)(2,1)S(1)}, bf16[8,128,256]{2,1,0:T(8,128)(2,1)S(1)}, u32[]{:S(2)}, u32[]{:S(2)}) collective-permute-start(bf16[8,128,256]{2,1,0:T(8,128)(2,1)S(1)} %get-tuple-element.174.refs_4_), channel_id=1, source_target_pairs={{0,8},{4,12},{8,0},{12,4},{1,9},{5,13},{9,1},{13,5},{2,10},{6,14},... | collective-permute-start | bytes 1572872 | tf_op jit(solution)/shard_map/ppermute | solution.py:392
  381.6 58.3 %collective-permute-start.26 = (bf16[8,128,256]{2,1,0:T(8,128)(2,1)S(1)}, bf16[8,128,256]{2,1,0:T(8,128)(2,1)S(1)}, u32[]{:S(2)}, u32[]{:S(2)}) collective-permute-start(bf16[8,128,256]{2,1,0:T(8,128)(2,1)S(1)} %get-tuple-element.174.refs_4_), channel_id=1, source_target_pairs={{0,4},{4,8},{8,12},{12,0},{1,5},{5,9},{9,13},{13,1},{2,6},{6,10},{... | collective-permute-start | bytes 1572872 | tf_op jit(solution)/shard_map/ppermute | solution.py:392
  381.6 31.5 %collective-permute-start.31 = (f32[8,4,128]{2,1,0:T(4,128)S(1)}, f32[8,4,128]{2,1,0:T(4,128)S(1)}, u32[]{:S(2)}, u32[]{:S(2)}) collective-permute-start(f32[8,4,128]{2,1,0:T(4,128)S(1)} %get-tuple-element.136.refs_8_), channel_id=1, source_target_pairs={{0,12},{4,0},{8,4},{12,8},{1,13},{5,1},{9,5},{13,9},{2,14},{6,2},{... | collective-permute-start | bytes 49160 | tf_op jit(solution)/shard_map/ppermute | solution.py:392
  385.4 43.6 %collective-permute-start.30 = (f32[8,4,128]{2,1,0:T(4,128)S(1)}, f32[8,4,128]{2,1,0:T(4,128)S(1)}, u32[]{:S(2)}, u32[]{:S(2)}) collective-permute-start(f32[8,4,128]{2,1,0:T(4,128)S(1)} %get-tuple-element.136.refs_8_), channel_id=1, source_target_pairs={{0,8},{4,12},{8,0},{12,4},{1,9},{5,13},{9,1},{13,5},{2,10},{6,14},... | collective-permute-start | bytes 49160 | tf_op jit(solution)/shard_map/ppermute | solution.py:392
  413.1 17.4 %collective-permute-start.29 = (f32[8,4,128]{2,1,0:T(4,128)S(1)}, f32[8,4,128]{2,1,0:T(4,128)S(1)}, u32[]{:S(2)}, u32[]{:S(2)}) collective-permute-start(f32[8,4,128]{2,1,0:T(4,128)S(1)} %get-tuple-element.136.refs_8_), channel_id=1, source_target_pairs={{0,4},{4,8},{8,12},{12,0},{1,5},{5,9},{9,13},{13,1},{2,6},{6,10},{... | collective-permute-start | bytes 49160 | tf_op jit(solution)/shard_map/ppermute | solution.py:392
  429.0 3.7 collective-permute-start.34
  430.5 4.8 collective-permute-start.33
  432.8 5.5 collective-permute-start.32
  481.3 12.6 %collective-permute-start.35 = (bf16[8,128,256]{2,1,0:T(8,128)(2,1)S(1)}, bf16[8,128,256]{2,1,0:T(8,128)(2,1)S(1)}, u32[]{:S(2)}, u32[]{:S(2)}) collective-permute-start(bf16[8,128,256]{2,1,0:T(8,128)(2,1)S(1)} %get-tuple-element.48), channel_id=1, source_target_pairs={{0,12},{4,0},{8,4},{12,8},{1,13},{5,1},{9,5},{13,9},{2,14},{6,2},{... | collective-permute-start | bytes 1572872 | tf_op jit(solution)/shard_map/ppermute | solution.py:392
  481.5 45.5 %collective-permute-start.36 = (bf16[8,128,256]{2,1,0:T(8,128)(2,1)S(1)}, bf16[8,128,256]{2,1,0:T(8,128)(2,1)S(1)}, u32[]{:S(2)}, u32[]{:S(2)}) collective-permute-start(bf16[8,128,256]{2,1,0:T(8,128)(2,1)S(1)} %get-tuple-element.49), channel_id=1, source_target_pairs={{0,8},{4,12},{8,0},{12,4},{1,9},{5,13},{9,1},{13,5},{2,10},{6,14},... | collective-permute-start | bytes 1572872 | tf_op jit(solution)/shard_map/ppermute | solution.py:392
  485.0 42.1 %collective-permute-start.37 = (bf16[8,128,256]{2,1,0:T(8,128)(2,1)S(1)}, bf16[8,128,256]{2,1,0:T(8,128)(2,1)S(1)}, u32[]{:S(2)}, u32[]{:S(2)}) collective-permute-start(bf16[8,128,256]{2,1,0:T(8,128)(2,1)S(1)} %get-tuple-element.50), channel_id=1, source_target_pairs={{0,4},{4,8},{8,12},{12,0},{1,5},{5,9},{9,13},{13,1},{2,6},{6,10},{... | collective-permute-start | bytes 1572872 | tf_op jit(solution)/shard_map/ppermute | solution.py:392
  527.8 2.7 collective-permute-start.38
  531.0 25.3 %collective-permute-start.39 = (bf16[4,128,1024]{2,1,0:T(8,128)(2,1)S(1)}, bf16[4,128,1024]{2,1,0:T(8,128)(2,1)S(1)}, u32[]{:S(2)}, u32[]{:S(2)}) collective-permute-start(bf16[4,128,1024]{2,1,0:T(8,128)(2,1)S(1)} %add_convert_fusion.1), channel_id=1, source_target_pairs={{0,2},{1,3},{2,0},{3,1},{4,6},{5,7},{6,4},{7,5},{8,10},{9,11},{10,... | collective-permute-start | bytes 3145736 | tf_op jit(solution)/shard_map/ppermute | solution.py:408
  559.8 5.9 collective-permute-start.40
  574.5 19.4 %collective-permute-start.41 = (bf16[8,80,512]{2,1,0:T(8,128)(2,1)S(1)}, bf16[8,80,512]{2,1,0:T(8,128)(2,1)S(1)}, u32[]{:S(2)}, u32[]{:S(2)}) collective-permute-start(bf16[8,80,512]{2,1,0:T(8,128)(2,1)S(1)} %get-tuple-element.54), channel_id=1, source_target_pairs={{4,0},{8,4},{12,8},{5,1},{9,5},{13,9},{6,2},{10,6},{14,10},{7,3},{... | collective-permute-start | bytes 1966088 | tf_op jit(solution)/shard_map/ppermute | solution.py:636
  598.6 190.8 %reduce-scatter.2.cloned.1.call-start = ((), (), s32[]{:S(2)}) async-start(), calls=%async_computation.1 | async-start | bytes 20971520 | tf_op jit(solution)/shard_map/reduce_scatter | solution.py:613
  618.2 2.7 collective-permute-start.42
  621.9 25.3 %collective-permute-start.43 = (bf16[4,128,1024]{2,1,0:T(8,128)(2,1)S(1)}, bf16[4,128,1024]{2,1,0:T(8,128)(2,1)S(1)}, u32[]{:S(2)}, u32[]{:S(2)}) collective-permute-start(bf16[4,128,1024]{2,1,0:T(8,128)(2,1)S(1)} %add_convert_fusion), channel_id=1, source_target_pairs={{0,2},{1,3},{2,0},{3,1},{4,6},{5,7},{6,4},{7,5},{8,10},{9,11},{10,... | collective-permute-start | bytes 3145736 | tf_op jit(solution)/shard_map/ppermute | solution.py:408
  650.0 33.8 %collective-permute-start.44 = (f32[4,128,1024]{2,1,0:T(8,128)}, f32[4,128,1024]{2,1,0:T(8,128)}, u32[]{:S(2)}, u32[]{:S(2)}) collective-permute-start(f32[4,128,1024]{2,1,0:T(8,128)} %get-tuple-element.134), channel_id=1, source_target_pairs={{0,1},{1,0},{2,3},{3,2},{4,5},{5,4},{6,7},{7,6},{8,9},{9,8},{10,11... | collective-permute-start | bytes 6291464 | tf_op jit(solution)/shard_map/ppermute | solution.py:396
  654.9 2.7 collective-permute-start.21
  655.0 3.6 collective-permute-start.45
  (90 other events, 1102.4 us)
Sparse Core Ops, SparseCore 0:
  598.7 175.7 all-reduce.4
Sparse Core Ops, SparseCore 1:
  615.7 129.3 reduce-scatter.1

commit v2 on v1

v2 whole, which is shorter than its diff:
```python
import functools

import jax
import jax.numpy as jnp
from jax import lax
from jax.experimental import pallas as pl
from jax.experimental.pallas import tpu as pltpu
from jax.sharding import PartitionSpec as P

HEAD_DIM = 64
HALO = 80
SOURCE_TILE = 512
FFN_TILE = 512
EXTRA = 16
VMEM_LIMIT = 40 * 2**20
VMEM_MOST = 56 * 2**20

epsilon = 1e-05
negative = -1e30
floor = -1e20
log2e = 1.4426950408889634
to_base2 = log2e * HEAD_DIM**-0.5
bf16 = jnp.bfloat16
f32 = jnp.float32


def forward_mul(left, right):
    return jnp.einsum("rti,ij->rtj", left, right, preferred_element_type=f32)


def backward_mul(left, right):
    return jnp.einsum("rtj,ij->rti", left, right, preferred_element_type=f32)


def weight_mul(left, right):
    return jnp.einsum("rti,rtj->ij", left, right, preferred_element_type=f32)


def norm_parts(values):
    centered = values - jnp.mean(values, axis=-1, keepdims=True)
    variance = jnp.mean(centered * centered, axis=-1, keepdims=True)
    scale = lax.rsqrt(variance + epsilon)
    return centered * scale, scale


def norm_back(unit, scale, gain, grad):
    inner = grad * gain
    first = jnp.mean(inner, axis=-1, keepdims=True)
    second = jnp.mean(inner * unit, axis=-1, keepdims=True)
    return (
        scale * (inner - first - unit * second),
        jnp.sum(grad * unit, axis=0),
        jnp.sum(grad, axis=0),
    )


def mul_nt(left, right):
    return lax.dot_general(left, right, (((1,), (1,)), ((), ())), preferred_element_type=f32)


def mul_nn(left, right):
    return lax.dot_general(left, right, (((1,), (0,)), ((), ())), preferred_element_type=f32)


def spread_heads(block, heads):
    if heads == 1:
        return block
    width = block.shape[1]
    lane = lax.broadcasted_iota(jnp.int32, (1, width), 1)
    copies = []
    for head in range(heads):
        inside = (lane >= head * HEAD_DIM) & (lane < (head + 1) * HEAD_DIM)
        copies.append(block * jnp.where(inside, 1.0, 0.0).astype(block.dtype))
    return jnp.concatenate(copies, axis=0)


def tile_lanes(block, heads):
    return jnp.concatenate([block] * heads, axis=1) if heads > 1 else block


def row_of(ref, heads):
    rows = [ref[0, head : head + 1, :] for head in range(heads)]
    return jnp.concatenate(rows, axis=1) if heads > 1 else rows[0]


def store_rows(ref, row, first, heads, count):
    for head in range(heads):
        ref[0, first + head : first + head + 1, :] = row[:, head * count : (head + 1) * count]


def rounded(row):
    return row.astype(bf16).astype(f32)


def pack_rows(ref, lines_ref, rows, width):
    line = 0
    for row in rows:
        for _ in range(3):
            term = rounded(row)
            row = row - term
            for at in range(0, term.shape[1], width):
                lines_ref[line : line + 1, :] = term[:, at : at + width]
                line += 1
    lines_ref[line:, :] = jnp.zeros((EXTRA - line, width), f32)
    ref[0, ref.shape[1] - EXTRA :, :] = lines_ref[...].astype(bf16)


def unpack_rows(ref, lines_ref, total, heads, count):
    width = ref.shape[2]
    lines = heads * count // width
    lines_ref[...] = ref[0, ref.shape[1] - EXTRA :, :].astype(f32)
    rows = []
    for index in range(total):
        pieces = []
        for at in range(lines):
            first = 3 * index * lines + at
            pieces.append(
                lines_ref[first : first + 1, :]
                + lines_ref[first + lines : first + lines + 1, :]
                + lines_ref[first + 2 * lines : first + 2 * lines + 1, :]
            )
        rows.append(jnp.concatenate(pieces, axis=1) if lines > 1 else pieces[0])
    return rows


def head_scale(row, heads, count):
    pieces = [
        jnp.broadcast_to(row[:, head * count : (head + 1) * count], (HEAD_DIM, count))
        for head in range(heads)
    ]
    return jnp.concatenate(pieces, axis=0) if heads > 1 else pieces[0]


def head_products(left, right, heads, count):
    pieces = [
        mul_nn(
            left[head * HEAD_DIM : (head + 1) * HEAD_DIM, :],
            right[:, head * count : (head + 1) * count],
        )
        for head in range(heads)
    ]
    return jnp.concatenate(pieces, axis=0) if heads > 1 else pieces[0]


def cross_forward_kernel(heads, blocks, tile, table_ref, *refs):
    queries = refs[:blocks]
    target_ids, source_ids, keys, values = refs[blocks : blocks + 4]
    mixed = refs[blocks + 4 : 2 * blocks + 4]
    turned, lines, total = refs[2 * blocks + 4 :]
    place = pl.program_id(0)
    count, width = queries[0].shape[1:]
    tiles = keys.shape[1] // tile
    for step in range(tiles):
        turned[step] = values[0, step * tile : (step + 1) * tile, :].T
    for block in range(blocks):
        spread = spread_heads(queries[block][0], heads)
        ids = target_ids[0, block : block + 1, :]
        total[...] = jnp.zeros_like(total)

        def visit(step, carry):
            best, weight = carry
            start = pl.multiple_of(step * tile, tile)
            scores = mul_nt(keys[0, pl.ds(start, tile), :], spread) * to_base2
            allowed = source_ids[0, pl.ds(start, tile), :] == ids
            scores = jnp.where(tile_lanes(allowed, heads), scores, negative)
            fresh = jnp.maximum(best, jnp.max(scores, axis=0, keepdims=True))
            anchor = jnp.maximum(fresh, floor)
            probs = jnp.exp2(scores - anchor)
            fade = jnp.exp2(best - anchor)
            weight = weight * fade + jnp.sum(probs, axis=0, keepdims=True)
            total[...] = total[...] * head_scale(fade, heads, count) + head_products(
                turned[step], probs.astype(bf16), heads, count
            )
            return fresh, weight

        best, weight = lax.fori_loop(
            table_ref[place, 2 * block],
            table_ref[place, 2 * block + 1],
            visit,
            (jnp.full((1, heads * count), negative, f32), jnp.zeros((1, heads * count), f32)),
        )
        some = weight > 0.0
        safe = jnp.where(some, weight, 1.0)
        scaled = total[...] * head_scale(1.0 / safe, heads, count)
        mixed[block][0, :count, :] = scaled.T.astype(bf16)
        sums = jnp.where(some, best + jnp.log2(safe), negative)
        pack_rows(mixed[block], lines.at[block], [sums], width)


def cross_merge_kernel(group, blocks, *refs):
    parts = refs[:blocks]
    weight, mixed, sums, product, lines = refs[blocks:]
    count, width = mixed.shape[1:]
    heads = group // HEAD_DIM
    for index in range(width // group):
        columns = slice(index * group, (index + 1) * group)
        rows = [
            unpack_rows(part.at[:, :, columns], lines.at[at], 1, heads, count)[0]
            for at, part in enumerate(parts)
        ]
        best = functools.reduce(jnp.maximum, rows)
        shares = [jnp.exp2(row - best) for row in rows]
        whole = functools.reduce(jnp.add, shares)
        store_rows(sums, best + jnp.log2(whole), index * heads, heads, count)
        inverse = 1.0 / whole
        total = None
        for part, each in zip(parts, shares):
            scale = head_scale(each * inverse, heads, count).T
            term = part[0, :count, columns].astype(f32) * scale
            total = term if total is None else total + term
        mixed[0, :, columns] = total.astype(bf16)
    product[0] = mul_nn(mixed[0], weight[...])


def cross_prepare_kernel(group, *refs):
    branch, weight, mixed, sums, message, lines = refs
    count, width = mixed.shape[1:]
    heads = group // HEAD_DIM
    grad = mul_nt(branch[0], weight[...]).astype(bf16)
    message[0, :count, :] = grad
    product = (grad.astype(f32) * mixed[0].astype(f32)).T
    for index in range(width // group):
        columns = slice(index * group, (index + 1) * group)
        delta, offset = [], []
        for head in range(index * heads, (index + 1) * heads):
            delta.append(
                jnp.sum(product[head * HEAD_DIM : (head + 1) * HEAD_DIM], axis=0, keepdims=True)
            )
            offset.append(sums[0, head : head + 1, :])
        if heads > 1:
            delta, offset = [jnp.concatenate(delta, axis=1)], [jnp.concatenate(offset, axis=1)]
        pack_rows(message.at[:, :, columns], lines, [offset[0], delta[0]], group)


def cross_backward_kernel(heads, blocks, tile, table_ref, *refs):
    queries = refs[:blocks]
    grads = refs[blocks : 2 * blocks]
    target_ids, source_ids, keys, values = refs[2 * blocks : 2 * blocks + 4]
    query_grads = refs[2 * blocks + 4 : 3 * blocks + 4]
    source_side, turned, lines, key_grad, value_grad, total = refs[3 * blocks + 4 :]
    place = pl.program_id(0)
    count, width = queries[0].shape[1:]
    tiles = keys.shape[1] // tile
    for step in range(tiles):
        turned[step] = keys[0, step * tile : (step + 1) * tile, :].T
    key_grad[...] = jnp.zeros_like(key_grad)
    value_grad[...] = jnp.zeros_like(value_grad)
    for block in range(blocks):
        spread = spread_heads(queries[block][0], heads)
        spread_grad = spread_heads(grads[block][0, :count, :], heads)
        offset, delta = unpack_rows(grads[block], lines.at[block], 2, heads, count)
        ids = target_ids[0, block : block + 1, :]
        total[...] = jnp.zeros_like(total)

        def visit(step, carry):
            start = pl.multiple_of(step * tile, tile)
            span = pl.ds(start, tile)
            scores = mul_nt(keys[0, span, :], spread) * to_base2
            allowed = source_ids[0, span, :] == ids
            probs = jnp.where(tile_lanes(allowed, heads), jnp.exp2(scores - offset), 0.0)
            dprobs = mul_nt(values[0, span, :], spread_grad)
            dscores = (probs * (dprobs - delta)).astype(bf16)
            key_grad[span, :] += mul_nn(dscores, spread)
            value_grad[span, :] += mul_nn(probs.astype(bf16), spread_grad)
            total[...] += head_products(turned[step], dscores, heads, count)
            return carry

        lax.fori_loop(table_ref[place, 2 * block], table_ref[place, 2 * block + 1], visit, 0)
        query_grads[block][0] = (total[...] * HEAD_DIM**-0.5).T.astype(bf16)
    source_side[0] = jnp.concatenate(
        [(key_grad[...] * HEAD_DIM**-0.5).astype(bf16), value_grad[...].astype(bf16)], axis=1
    )


def self_scores(heads, queries, keys, source_ids, ids):
    spread = spread_heads(queries, heads)
    scores = mul_nt(keys, spread) * to_base2
    count = queries.shape[0]
    slots = keys.shape[0]
    key_place = lax.broadcasted_iota(jnp.int32, (slots, count), 0) - (slots - count)
    query_place = lax.broadcasted_iota(jnp.int32, (slots, count), 1)
    allowed = (source_ids == ids) & (key_place <= query_place)
    return spread, scores, tile_lanes(allowed, heads)


def with_halo(halo, own):
    missing = own.shape[0] - halo.shape[0]
    return jnp.concatenate([jnp.zeros((missing, own.shape[1]), own.dtype), halo, own], axis=0)


def self_forward_kernel(heads, *refs):
    queries, keys, values, key_halo, value_halo, target_ids, source_ids, mixed, sums = refs
    count = queries.shape[1]
    every_key = with_halo(key_halo[0], keys[0])
    every_value = with_halo(value_halo[0], values[0])
    _, scores, allowed = self_scores(
        heads, queries[0], every_key, source_ids[0], target_ids[0, 0:1, :]
    )
    scores = jnp.where(allowed, scores, negative)
    best = jnp.max(scores, axis=0, keepdims=True)
    probs = jnp.exp2(scores - best)
    weight = jnp.sum(probs, axis=0, keepdims=True)
    total = head_products(every_value.T, probs.astype(bf16), heads, count)
    mixed[0] = (total * head_scale(1.0 / weight, heads, count)).T.astype(bf16)
    store_rows(sums, best + jnp.log2(weight), 0, heads, count)


def self_backward_kernel(heads, *refs):
    queries, keys, values, key_halo, value_halo, target_ids, source_ids, sums, grads = refs[:9]
    query_grad, key_own, value_own, side = refs[9:]
    count = queries.shape[1]
    every_key = with_halo(key_halo[0], keys[0])
    every_value = with_halo(value_halo[0], values[0])
    spread, scores, allowed = self_scores(
        heads, queries[0], every_key, source_ids[0], target_ids[0, 0:1, :]
    )
    spread_grad = spread_heads(grads[0], heads)
    probs = jnp.where(allowed, jnp.exp2(scores - row_of(sums, heads)), 0.0)
    dprobs = mul_nt(every_value, spread_grad)
    delta = jnp.sum(probs * dprobs, axis=0, keepdims=True)
    dscores = (probs * (dprobs - delta)).astype(bf16)
    key_grad = mul_nn(dscores, spread) * HEAD_DIM**-0.5
    value_grad = mul_nn(probs.astype(bf16), spread_grad)
    total = head_products(every_key.T, dscores, heads, count)
    query_grad[0] = (total * HEAD_DIM**-0.5).T.astype(bf16)
    slots = every_key.shape[0]
    first = slots - count - HALO
    key_own[0] = key_grad[slots - count :, :]
    value_own[0] = value_grad[slots - count :, :]
    side[0] = jnp.concatenate(
        [
            key_grad[first : slots - count, :].astype(bf16),
            value_grad[first : slots - count, :].astype(bf16),
        ],
        axis=1,
    )


def group_width(width, total):
    return width if width % 128 == 0 else total


def cross_call(backward, group, queries, grads, target_ids, source_ids, kv, table):
    blocks = len(queries)
    rows, count, width = queries[0].shape
    slots = kv.shape[1]
    tile = min(SOURCE_TILE, slots)
    heads = group // HEAD_DIM
    token = pl.BlockSpec((1, count, group), lambda i, g, t: (i, 0, g))
    packed = pl.BlockSpec((1, count + EXTRA, group), lambda i, g, t: (i, 0, g))
    in_specs = [token] * blocks
    operands = list(queries)
    if backward:
        in_specs += [packed] * blocks
        operands += list(grads)
    in_specs += [
        pl.BlockSpec((1, blocks, count), lambda i, g, t: (i, 0, 0)),
        pl.BlockSpec((1, slots, 1), lambda i, g, t: (i, 0, 0)),
        pl.BlockSpec((1, slots, group), lambda i, g, t: (i, 0, 2 * g)),
        pl.BlockSpec((1, slots, group), lambda i, g, t: (i, 0, 2 * g + 1)),
    ]
    operands += [target_ids, source_ids, kv, kv]
    scratch = [
        pltpu.VMEM((slots // tile, group, tile), bf16),
        pltpu.VMEM((blocks, EXTRA, group), f32),
    ]
    if backward:
        out_shape = [jax.ShapeDtypeStruct((rows, count, width), bf16)] * blocks
        out_shape += [jax.ShapeDtypeStruct((rows, slots, 2 * width), bf16)]
        out_specs = [token] * blocks + [
            pl.BlockSpec((1, slots, 2 * group), lambda i, g, t: (i, 0, g))
        ]
        scratch += [pltpu.VMEM((slots, group), f32), pltpu.VMEM((slots, group), f32)]
    else:
        out_shape = [jax.ShapeDtypeStruct((rows, count + EXTRA, width), bf16)] * blocks
        out_specs = [packed] * blocks
    scratch += [pltpu.VMEM((group, count), f32)]
    work = rows * slots * blocks * count * width // 2
    return pl.pallas_call(
        functools.partial(
            cross_backward_kernel if backward else cross_forward_kernel, heads, blocks, tile
        ),
        grid_spec=pltpu.PrefetchScalarGridSpec(
            num_scalar_prefetch=1,
            grid=(rows, width // group),
            in_specs=in_specs,
            out_specs=out_specs,
            scratch_shapes=scratch,
        ),
        out_shape=out_shape,
        compiler_params=pltpu.CompilerParams(vmem_limit_bytes=VMEM_MOST),
        cost_estimate=pl.CostEstimate(
            flops=work * (20 if backward else 8),
            bytes_accessed=rows * slots * width * (8 if backward else 4),
            transcendentals=0,
        ),
        name="cross_backward" if backward else "cross_forward",
    )(table, *operands)


def merge_call(group, parts, weight):
    rows, tall, width = parts[0].shape
    count = tall - EXTRA
    depth = weight.shape[1]
    heads = width // HEAD_DIM
    return pl.pallas_call(
        functools.partial(cross_merge_kernel, group, len(parts)),
        grid=(rows,),
        in_specs=[pl.BlockSpec((1, tall, width), lambda i: (i, 0, 0))] * len(parts)
        + [pl.BlockSpec(weight.shape, lambda i: (0, 0))],
        out_specs=[
            pl.BlockSpec((1, count, width), lambda i: (i, 0, 0)),
            pl.BlockSpec((1, heads, count), lambda i: (i, 0, 0)),
            pl.BlockSpec((1, count, depth), lambda i: (i, 0, 0)),
        ],
        out_shape=[
            jax.ShapeDtypeStruct((rows, count, width), bf16),
            jax.ShapeDtypeStruct((rows, heads, count), f32),
            jax.ShapeDtypeStruct((rows, count, depth), f32),
        ],
        scratch_shapes=[pltpu.VMEM((len(parts), EXTRA, group), f32)],
        compiler_params=pltpu.CompilerParams(vmem_limit_bytes=VMEM_LIMIT),
        cost_estimate=pl.CostEstimate(
            flops=2 * rows * count * width * depth,
            bytes_accessed=rows * tall * (width * 8 + depth * 4),
            transcendentals=0,
        ),
        name="cross_merge",
    )(*parts, weight)


def prepare_call(group, branch, weight, mixed, sums):
    rows, count, width = mixed.shape
    depth = branch.shape[2]
    heads = width // HEAD_DIM
    return pl.pallas_call(
        functools.partial(cross_prepare_kernel, group),
        grid=(rows,),
        in_specs=[
            pl.BlockSpec((1, count, depth), lambda i: (i, 0, 0)),
            pl.BlockSpec(weight.shape, lambda i: (0, 0)),
            pl.BlockSpec((1, count, width), lambda i: (i, 0, 0)),
            pl.BlockSpec((1, heads, count), lambda i: (i, 0, 0)),
        ],
        out_specs=pl.BlockSpec((1, count + EXTRA, width), lambda i: (i, 0, 0)),
        out_shape=jax.ShapeDtypeStruct((rows, count + EXTRA, width), bf16),
        scratch_shapes=[pltpu.VMEM((EXTRA, group), f32)],
        compiler_params=pltpu.CompilerParams(vmem_limit_bytes=VMEM_LIMIT),
        cost_estimate=pl.CostEstimate(
            flops=2 * rows * count * width * depth,
            bytes_accessed=rows * count * (width * 6 + depth * 2),
            transcendentals=0,
        ),
        name="cross_prepare",
    )(branch, weight, mixed, sums)


def mul_tn(left, right):
    return lax.dot_general(left, right, (((0,), (0,)), ((), ())), preferred_element_type=f32)


def project_kernel(row, tokens, weight, out):
    out[0] = mul_nn(tokens[0], weight[...]).astype(bf16)


def source_weight_kernel(row, tokens, grad, total):
    @pl.when((pl.program_id(0) == 0) & (pl.program_id(1) == 0))
    def _():
        total[...] = jnp.zeros_like(total)

    total[...] += mul_tn(tokens[0], grad[0])


def source_other_kernel(grad, weight, out):
    out[0] = mul_nt(grad[0], weight[...]).astype(bf16)


def source_own_kernel(grad, weight, across, own, peer):
    width = own.shape[2]
    total = mul_nt(grad[0], weight[...]) + across[0].astype(f32)
    own[0] = total[:, :width]
    peer[0] = total[:, width:].astype(bf16)


def source_call(kernel, row, rows, slots, operands, blocks, outs, name):
    tile = min(FFN_TILE, slots)
    prefetch = row is not None

    def spec(shape, kind):
        if kind == "all":
            return pl.BlockSpec(shape, lambda i, j, *r: (0, 0))
        if kind == "far":
            return pl.BlockSpec((1, tile, shape[2]), lambda i, j, r: (r[0] + i, j, 0))
        return pl.BlockSpec((1, tile, shape[2]), lambda i, j, *r: (i, j, 0))

    count = len(operands)
    return pl.pallas_call(
        kernel,
        grid_spec=pltpu.PrefetchScalarGridSpec(
            num_scalar_prefetch=1 if prefetch else 0,
            grid=(rows, slots // tile),
            in_specs=[spec(each.shape, kind) for each, kind in zip(operands, blocks)],
            out_specs=[spec(each.shape, kind) for each, kind in zip(outs, blocks[count:])],
        ),
        out_shape=outs,
        compiler_params=pltpu.CompilerParams(vmem_limit_bytes=VMEM_MOST),
        cost_estimate=pl.CostEstimate(flops=0, bytes_accessed=0, transcendentals=0),
        name=name,
    )(*([row] if prefetch else []), *operands)


def ffn_forward_kernel(tokens, weight_in, weight_out, down, up, total, slope, rect, down_slope):
    @pl.when(pl.program_id(0) == 0)
    def _():
        value = mul_nn(tokens[...], down[...])
        smooth = 1.0 / (1.0 + jnp.exp(-value))
        low = (value * smooth).astype(bf16)
        rect[...] = low
        down_slope[...] = smooth * (1.0 + value * (1.0 - smooth))
        total[...] = 4.0 * mul_nn(low, up[...])

    gate = mul_nn(tokens[...], weight_in[...])
    normal = 0.5 * (1.0 + lax.erf(gate * 0.5**0.5))
    slope[...] = (normal + gate * jnp.exp(-0.5 * gate * gate) * 0.3989422804014327).astype(bf16)
    total[...] += mul_nn((gate * normal).astype(bf16), weight_out[...])


def ffn_backward_kernel(grad, weight_in, weight_out, down, up, slope, down_slope, total, down_grad):
    @pl.when(pl.program_id(0) == 0)
    def _():
        low = (4.0 * mul_nt(grad[...], up[...]) * down_slope[...]).astype(bf16)
        down_grad[...] = low
        total[...] = mul_nt(low, down[...])

    gate_grad = (mul_nt(grad[...], weight_out[...]) * slope[...].astype(f32)).astype(bf16)
    total[...] += mul_nt(gate_grad, weight_in[...])


def ffn_call(backward, tokens, weight_in, weight_out, down, up, slopes=()):
    count, depth = tokens.shape
    hidden = weight_in.shape[1]
    extra = down.shape[1]
    tile = min(FFN_TILE, hidden)
    whole = lambda shape: pl.BlockSpec(shape, lambda j: (0, 0))
    across = pl.BlockSpec((count, tile), lambda j: (0, j))
    in_specs = [
        whole((count, depth)),
        pl.BlockSpec((depth, tile), lambda j: (0, j)),
        pl.BlockSpec((tile, depth), lambda j: (j, 0)),
        whole((depth, extra)),
        whole((extra, depth)),
    ]
    out_shape = [jax.ShapeDtypeStruct((count, depth), f32)]
    out_specs = [whole((count, depth))]
    if backward:
        in_specs += [across, whole((count, extra))]
        out_shape += [jax.ShapeDtypeStruct((count, extra), bf16)]
        out_specs += [whole((count, extra))]
    else:
        out_shape += [
            jax.ShapeDtypeStruct((count, hidden), bf16),
            jax.ShapeDtypeStruct((count, extra), bf16),
            jax.ShapeDtypeStruct((count, extra), f32),
        ]
        out_specs += [across, whole((count, extra)), whole((count, extra))]
    return pl.pallas_call(
        ffn_backward_kernel if backward else ffn_forward_kernel,
        grid=(hidden // tile,),
        in_specs=in_specs,
        out_specs=out_specs,
        out_shape=out_shape,
        compiler_params=pltpu.CompilerParams(vmem_limit_bytes=VMEM_LIMIT),
        cost_estimate=pl.CostEstimate(
            flops=4 * count * hidden * depth,
            bytes_accessed=4 * hidden * depth,
            transcendentals=0,
        ),
        name="ffn_backward" if backward else "ffn_forward",
    )(tokens, weight_in, weight_out, down, up, *slopes)


def self_call(backward, group, qkv, halo, extra, target_ids, source_ids):
    rows, count = qkv.shape[:2]
    width = qkv.shape[2] // 3
    groups = width // group
    heads = group // HEAD_DIM
    in_specs = [
        pl.BlockSpec((1, count, group), lambda i, g, at=at: (i, 0, 3 * g + at)) for at in range(3)
    ]
    in_specs += [
        pl.BlockSpec((1, HALO, group), lambda i, g, at=at: (i, 0, 2 * g + at)) for at in range(2)
    ]
    token = pl.BlockSpec((1, count, group), lambda i, g: (i, 0, g))
    stat = pl.BlockSpec((1, None, heads, count), lambda i, g: (i, g, 0, 0))
    in_specs += [
        pl.BlockSpec((1, 1, count), lambda i, g: (i, 0, 0)),
        pl.BlockSpec((1, 2 * count, 1), lambda i, g: (i, 0, 0)),
    ]
    operands = [qkv, qkv, qkv, halo, halo, target_ids, source_ids]
    token_shape = (rows, count, width)
    if backward:
        in_specs += [stat, token]
        operands += list(extra)
        out_shape = [
            jax.ShapeDtypeStruct(token_shape, bf16),
            jax.ShapeDtypeStruct(token_shape, f32),
            jax.ShapeDtypeStruct(token_shape, f32),
            jax.ShapeDtypeStruct((rows, HALO, 2 * width), bf16),
        ]
        out_specs = [
            token,
            token,
            token,
            pl.BlockSpec((1, HALO, 2 * group), lambda i, g: (i, 0, g)),
        ]
    else:
        out_shape = [
            jax.ShapeDtypeStruct(token_shape, bf16),
            jax.ShapeDtypeStruct((rows, groups, heads, count), f32),
        ]
        out_specs = [token, stat]
    work = rows * count * count * width
    return pl.pallas_call(
        functools.partial(self_backward_kernel if backward else self_forward_kernel, heads),
        grid=(rows, groups),
        in_specs=in_specs,
        out_specs=out_specs,
        out_shape=out_shape,
        compiler_params=pltpu.CompilerParams(vmem_limit_bytes=VMEM_LIMIT),
        cost_estimate=pl.CostEstimate(
            flops=work * (40 if backward else 16),
            bytes_accessed=rows * count * width * 12,
            transcendentals=0,
        ),
        name="self_backward" if backward else "self_forward",
    )(*operands)


def send_blk(array, distance, size):
    return lax.ppermute(array, "blk", [(i, (i + distance) % size) for i in range(size)])


def send_sibling(array, size):
    return lax.ppermute(array, "tensor", [(i, i ^ 1) for i in range(size)])


def send_outer(array, distance, size):
    return lax.ppermute(array, "tensor", [(i, (i + 2 * distance) % size) for i in range(size)])


def tie(token, *arrays):
    if token is None:
        return arrays
    return lax.optimization_barrier((token, *arrays))[1:]


def sum_grid(value, first=(), others_of=lambda first: ()):
    groups, blocks = lax.axis_size("dp"), lax.axis_size("blk")
    group, place = lax.axis_index("dp"), lax.axis_index("blk")
    depth, width = value.shape

    def send_dp(array, step):
        return lax.ppermute(array, "dp", [(i, (i + step) % groups) for i in range(groups)])

    def reduce_over(array, index, size, send):
        many = array.shape[0] // size
        mine = lax.dynamic_slice_in_dim(array, index * many, many, 0)
        for step in range(1, size):
            to = lax.rem(index + step, size)
            other = lax.dynamic_slice_in_dim(array, to * many, many, 0)
            mine = mine + send(other.astype(bf16), step).astype(f32)
        return mine

    def gather_over(array, index, size, send):
        many = array.shape[0]
        whole = jnp.zeros((many * size, width), array.dtype)
        whole = lax.dynamic_update_slice_in_dim(whole, array, index * many, 0)
        for step in range(1, size):
            source = lax.rem(index - step + size, size)
            whole = lax.dynamic_update_slice_in_dim(whole, send(array, step), source * many, 0)
        return whole

    def over_blk(array, step):
        return send_blk(array, step, blocks)

    total = reduce_over(value, group, groups, send_dp)
    total, first = lax.optimization_barrier((total, first))
    others = others_of(first)
    total = reduce_over(total, place, blocks, over_blk).astype(bf16)
    total = gather_over(total, place, blocks, over_blk)
    total, others = lax.optimization_barrier((total, others))
    return gather_over(total, group, groups, send_dp), others


def sum_small(value):
    groups, blocks = lax.axis_size("dp"), lax.axis_size("blk")
    total = value
    for step in range(1, groups):
        total = total + lax.ppermute(
            value, "dp", [(i, (i + step) % groups) for i in range(groups)]
        )
    value = total
    for step in range(1, blocks):
        total = total + send_blk(value, step, blocks)
    return total


def on_device(
    target,
    source,
    target_segments,
    source_segments,
    self_query,
    self_key,
    self_value,
    self_output,
    cross_query,
    cross_key,
    cross_value,
    cross_output,
    ffn_in,
    ffn_out,
    adapter_down,
    adapter_up,
    first_gain,
    first_shift,
    second_gain,
    second_shift,
    third_gain,
    third_shift,
    out_cotangent,
):
    rows, count, depth = target.shape
    slots = source.shape[1]
    width = self_query.shape[1]
    extra = adapter_up.shape[0]
    blocks = lax.axis_size("blk")
    lanes = lax.axis_size("tensor")
    place = lax.axis_index("blk")
    lane = lax.axis_index("tensor")
    core = lax.rem(lane, 2)
    chip = lane // 2
    chips = lanes // 2
    many = rows // chips
    half = many * count // 2
    tile = min(SOURCE_TILE, slots)
    wide = width * chips
    group = group_width(width, wide)
    groups = range(wide // group)

    def over_blk(array):
        return [array] + [send_blk(array, step, blocks) for step in range(1, blocks)]

    def back_blk(arrays):
        return [arrays[0]] + [send_blk(arrays[step], -step, blocks) for step in range(1, blocks)]

    def over_chips(array):
        return [array] + [send_outer(array, step, lanes) for step in range(1, chips)]

    def home_chips(arrays):
        total = arrays[0]
        for step in range(1, chips):
            total = total + send_outer(arrays[step].astype(bf16), -step, lanes).astype(f32)
        return total

    def packed_over_chips(*arrays):
        flat = jnp.concatenate([each.reshape(-1, depth) for each in arrays], axis=0)
        lists = [[each] for each in arrays]
        for step in range(1, chips):
            far = send_outer(flat, step, lanes)
            at = 0
            for each, gathered in zip(arrays, lists):
                size = each.size // depth
                gathered.append(far[at : at + size].reshape(each.shape))
                at += size
        return lists

    def chip_rows(array, step):
        at = lax.rem(chip + step, chips) * many
        return lax.dynamic_slice_in_dim(array, at, many, 0)

    def core_half(array):
        flat = array.reshape(many * count, array.shape[-1])
        return lax.dynamic_slice_in_dim(flat, core * half, half, 0)

    def share(mine):
        other = send_sibling(mine, lanes)
        first_one = core == 0
        both = [jnp.where(first_one, mine, other), jnp.where(first_one, other, mine)]
        return jnp.concatenate(both, axis=0).reshape(many, count, mine.shape[-1])

    def reduced(part):
        flat = part.reshape(many * count, part.shape[-1])
        other = lax.dynamic_slice_in_dim(flat, (1 - core) * half, half, 0).astype(bf16)
        return core_half(part) + send_sibling(other, lanes).astype(f32)

    def total_of(multiply, lefts, rights):
        return functools.reduce(jnp.add, [multiply(a, b) for a, b in zip(lefts, rights)])

    def by_group(*lists):
        joined = [jnp.concatenate(each, axis=-1) for each in lists]
        pieces = [
            each[..., at * group : (at + 1) * group] for at in groups for each in joined
        ]
        return jnp.concatenate(pieces, axis=-1)

    def ungroup(array, kinds):
        return [
            jnp.concatenate(
                [
                    array[..., (at * kinds + kind) * group : (at * kinds + kind + 1) * group]
                    for at in groups
                ],
                axis=-1,
            )
            for kind in range(kinds)
        ]

    def lane_columns(array):
        return [array[..., at * width : (at + 1) * width] for at in range(chips)]

    far_ids = over_blk(chip_rows(target_segments, 0))
    target_ids = jnp.stack(far_ids, axis=1)
    first_row = (chip * many).astype(jnp.int32).reshape(1)
    source_segments = chip_rows(source_segments, 0)
    tiles = source_segments.reshape(many, slots // tile, tile)
    table = jnp.stack(
        [
            jnp.sum(tiles[:, None, :, -1] < target_ids[:, :, :1], axis=-1, dtype=jnp.int32),
            jnp.sum(tiles[:, None, :, 0] <= target_ids[:, :, -1:], axis=-1, dtype=jnp.int32),
        ],
        axis=-1,
    ).reshape(many, 2 * blocks)
    source_ids = source_segments[:, :, None]
    halo_ids = jnp.where(place == 0, -1, far_ids[-1 + min(blocks, 2)][:, count - HALO :])
    self_ids = jnp.concatenate(
        [jnp.full((many, count - HALO), -1, jnp.int32), halo_ids, far_ids[0]], axis=1
    )[:, :, None]
    own_ids = target_ids[:, :1]

    qkv_weight = jnp.concatenate([self_query, self_key, self_value], axis=1)
    all_tokens = jnp.concatenate([chip_rows(target, step) for step in range(chips)], axis=0)
    tokens = all_tokens[:many]
    target_mine = core_half(tokens)
    flat_cotangent = out_cotangent.reshape(rows * count, depth)
    cotangent = lax.dynamic_slice_in_dim(
        flat_cotangent, chip * many * count + core * half, half, 0
    )
    self_outputs = over_chips(self_output)
    every = forward_mul(all_tokens, qkv_weight).astype(bf16)
    qkv = [every[:many]] + [
        send_outer(every[step * many : (step + 1) * many], step, lanes)
        for step in range(1, chips)
    ]
    arrived = qkv[-1]
    qkv = by_group(*[[each[..., at * width : (at + 1) * width] for each in qkv] for at in range(3)])
    halo = jnp.concatenate(
        [
            qkv[:, count - HALO :, (3 * at + 1) * group : (3 * at + 3) * group]
            for at in groups
        ],
        axis=2,
    )
    halo = send_blk(halo, 1, blocks)
    cross_queries = over_chips(tie(arrived, cross_query)[0])
    halo, cross_queries, self_outputs = lax.optimization_barrier(
        (halo, cross_queries, self_outputs)
    )

    self_low, self_sums = self_call(False, group, qkv, halo, (), own_ids, self_ids)
    self_outputs = jnp.concatenate(self_outputs, axis=0)
    first_in = target_mine.astype(f32) + reduced(forward_mul(self_low, self_outputs))
    first_unit, first_scale = norm_parts(first_in)
    first = first_unit * first_gain + first_shift
    first_low = share(first.astype(bf16))

    cross_queries = jnp.concatenate(cross_queries, axis=1)
    cross_q = forward_mul(first_low, cross_queries).astype(bf16)
    far_q = over_blk(cross_q)
    near_kv = tie(cross_q, jnp.concatenate([cross_key, cross_value], axis=1))[0]
    kv_weights = over_chips(near_kv)
    kv_weight = by_group(
        [each[:, :width] for each in kv_weights], [each[:, width:] for each in kv_weights]
    )
    (kv,) = source_call(
        project_kernel,
        first_row,
        many,
        slots,
        (source, kv_weight),
        ("far", "all", "near"),
        [jax.ShapeDtypeStruct((many, slots, 2 * wide), bf16)],
        "source_project",
    )
    near = tie(kv_weights[-1], cross_output, ffn_in, adapter_down)
    cross_outputs, ffn_ins = packed_over_chips(*near[:2])
    downs = over_chips(near[2])
    visited = cross_call(False, group, far_q, (), target_ids, source_ids, kv, table)
    back = back_blk(visited)
    ffn_outs, ups = packed_over_chips(*tie(visited[0], ffn_out, adapter_up))
    back, cross_outputs, ffn_ins, downs = lax.optimization_barrier(
        (back, cross_outputs, ffn_ins, downs)
    )
    cross_outputs = jnp.concatenate(cross_outputs, axis=0)
    down_weight = jnp.concatenate(downs, axis=1)
    ffn_in_weight = jnp.concatenate(ffn_ins, axis=1)
    ffn_out_weight = jnp.concatenate(ffn_outs, axis=0)
    up_weight = jnp.concatenate(ups, axis=0)
    cross_low, cross_sums, branch = merge_call(group, back, cross_outputs)
    second_in = first + reduced(branch)
    second_unit, second_scale = norm_parts(second_in)
    second = second_unit * second_gain + second_shift
    second_low = share(second.astype(bf16))

    ffn_weights = (ffn_in_weight, ffn_out_weight, down_weight, up_weight)
    branch, gate_slope, rectified, down_slope = ffn_call(
        False, second_low.reshape(many * count, depth), *ffn_weights
    )
    third_in = second + reduced(branch)
    third_unit, third_scale = norm_parts(third_in)
    result = (third_unit * third_gain + third_shift).astype(bf16)
    third_grad, third_gain_grad, third_shift_grad = norm_back(
        third_unit, third_scale, third_gain, cotangent.astype(f32)
    )
    branch_grad = share(third_grad.astype(bf16))

    branch, down_grad = ffn_call(
        True, branch_grad.reshape(many * count, depth), *ffn_weights, (gate_slope, down_slope)
    )
    second_grad = third_grad + reduced(branch)
    cross_grad, second_gain_grad, second_shift_grad = norm_back(
        second_unit, second_scale, second_gain, second_grad
    )
    cross_branch = share(cross_grad.astype(bf16))

    message = prepare_call(group, cross_branch, cross_outputs, cross_low, cross_sums)
    far_grads = over_blk(message)
    early = [
        jnp.concatenate(
            [
                4.0 * weight_mul(branch_grad, up),
                weight_mul(second_low, down),
                weight_mul(cross_branch, low),
            ],
            axis=1,
        )
        for up, down, low in zip(
            *[
                [
                    each.reshape(many, count, -1)[..., at * extra : (at + 1) * extra]
                    for at in range(chips)
                ]
                for each in (rectified, down_grad)
            ],
            lane_columns(cross_low),
        )
    ]
    early = home_chips(early)
    results = over_chips(tie(message, result)[0])
    far_grads, early, results = lax.optimization_barrier((far_grads, early, results))
    visited = cross_call(True, group, far_q, far_grads, target_ids, source_ids, kv, table)
    kv_grad = visited[blocks]
    back = back_blk(visited[:blocks])
    qkv_weights = over_chips(tie(kv_grad, qkv_weight)[0])
    (kv_grad_now,) = tie(back[min(1, blocks - 1)], kv_grad)

    def owner_rows(parity):
        owners = [lax.rem(chip + step, chips) * 2 + parity for step in range(chips)]
        rows_of = [
            lax.dynamic_slice_in_dim(kv_weight, owner * width, width, 0) for owner in owners
        ]
        return jnp.concatenate(rows_of, axis=0)

    (kv_weight_grad,) = source_call(
        source_weight_kernel,
        first_row,
        many,
        slots,
        (source, kv_grad_now),
        ("far", "near", "all"),
        [jax.ShapeDtypeStruct((depth, 2 * wide), f32)],
        "source_weight",
    )
    middle = [
        jnp.concatenate(each, axis=1)
        for each in zip(*[lane_columns(each) for each in ungroup(kv_weight_grad, 2)])
    ]
    (across,) = source_call(
        source_other_kernel,
        None,
        many,
        slots,
        (kv_grad_now, owner_rows(1 - core)),
        ("near", "all", "near"),
        [jax.ShapeDtypeStruct((many, slots, wide), bf16)],
        "source_other",
    )
    back, qkv_weights, middle, across = lax.optimization_barrier(
        (back, qkv_weights, middle, across)
    )
    cross_q_low = functools.reduce(jnp.add, [part.astype(f32) for part in back]).astype(bf16)
    first_grad = cross_grad + reduced(backward_mul(cross_q_low, cross_queries))
    self_grad, first_gain_grad, first_shift_grad = norm_back(
        first_unit, first_scale, first_gain, first_grad
    )
    middle = home_chips(list(tie(cross_q_low, *middle)))
    self_branch = share(self_grad.astype(bf16))

    mixed_grad = backward_mul(self_branch, self_outputs).astype(bf16)
    q_grad, key_own, value_own, side = self_call(
        True, group, qkv, halo, (self_sums, mixed_grad), own_ids, self_ids
    )
    side = lax.ppermute(side, "blk", [(i, i - 1) for i in range(1, blocks)])
    (middle,) = tie(q_grad, jnp.concatenate([early, middle], axis=1).astype(bf16))
    middle = lax.psum(middle, ("dp", "blk"))
    across = send_sibling(across, lanes)
    vector = jnp.stack(
        [
            first_gain_grad,
            first_shift_grad,
            second_gain_grad,
            second_shift_grad,
            third_gain_grad,
            third_shift_grad,
        ]
    )
    portion = depth // lanes
    lines = 6 * portion // (2 * width)
    below = 16 * lax.axis_size("dp") * blocks

    def vector_rows(step):
        owner = lax.rem(chip - step + chips, chips) * 2 + core
        piece = lax.dynamic_slice_in_dim(vector, owner * portion, portion, 1)
        return jnp.pad(piece.reshape(lines, 2 * width), ((0, below - lines), (0, 0)))

    vector, late_branch, late_low = tie(q_grad, vector, self_branch, first_low)
    vector = vector + send_sibling(vector, lanes)
    late = [
        jnp.concatenate([jnp.concatenate(each, axis=1), vector_rows(step)], axis=0)
        for step, each in enumerate(
            zip(
                lane_columns(weight_mul(late_branch, self_low)),
                lane_columns(weight_mul(late_low, cross_q_low)),
            )
        )
    ]
    late = home_chips(late)
    after = ((0, 0), (count - HALO, 0), (0, 0))
    key_side, value_side = [jnp.pad(each.astype(f32), after) for each in ungroup(side, 2)]
    key_grad = (key_own + key_side).astype(bf16)
    value_grad = (value_own + value_side).astype(bf16)
    qkv_grad = [
        jnp.concatenate(each, axis=2)
        for each in zip(lane_columns(q_grad), lane_columns(key_grad), lane_columns(value_grad))
    ]
    home = [qkv_grad[0]] + [
        send_outer(qkv_grad[step], -step, lanes) for step in range(1, chips)
    ]
    self_qkv_grad = weight_mul(all_tokens, jnp.concatenate(home, axis=0))
    source_own, source_peer = source_call(
        source_own_kernel,
        None,
        many,
        slots,
        (tie(home[-1], kv_grad)[0], owner_rows(core), across),
        ("near", "all", "near", "near", "near"),
        [
            jax.ShapeDtypeStruct((many, slots, width), f32),
            jax.ShapeDtypeStruct((many, slots, wide - width), bf16),
        ],
        "source_own",
    )

    def source_sends(first):
        own, peer = first
        far = [
            send_outer(peer[:, :, (step - 1) * width : step * width], step, lanes)
            for step in range(1, chips)
        ]
        return middle, [own] + far

    late, (middle, source_parts) = sum_grid(
        tie(self_qkv_grad, late)[0], (source_own, source_peer), source_sends
    )
    (self_grad, *qkv_grad) = tie(self_qkv_grad, self_grad, *qkv_grad)
    target_grad = self_grad + reduced(total_of(backward_mul, qkv_grad, qkv_weights))
    target_grads = over_chips(lax.optimization_barrier(target_grad.astype(bf16)))

    def everywhere(pieces, dtype):
        whole = jnp.zeros((rows * count, depth), dtype)
        for step, piece in enumerate(pieces):
            first_at = lax.rem(chip - step + chips, chips) * many * count
            other = send_sibling(piece, lanes)
            whole = lax.dynamic_update_slice_in_dim(
                whole, piece.astype(dtype), first_at + core * half, 0
            )
            whole = lax.dynamic_update_slice_in_dim(
                whole, other.astype(dtype), first_at + (1 - core) * half, 0
            )
        return whole.reshape(rows, count, depth)

    last, _ = sum_grid(self_qkv_grad)
    source_grad = jnp.zeros((rows, slots, width), f32)
    for step, part in enumerate(source_parts):
        at = lax.rem(chip - step + chips, chips) * many
        source_grad = lax.dynamic_update_slice_in_dim(source_grad, part.astype(f32), at, 0)
    vector = late[depth : depth + lines].astype(f32).reshape(6, portion)
    late = late[:depth]

    def columns(array, first, size):
        return array[:, first : first + size].astype(f32)

    return (
        everywhere(results, bf16),
        everywhere(target_grads, f32),
        source_grad,
        columns(last, 0, width),
        columns(last, width, width),
        columns(last, 2 * width, width),
        columns(late, 0, width).T,
        columns(late, width, width),
        columns(middle, 2 * extra + width, width),
        columns(middle, 2 * extra + 2 * width, width),
        columns(middle, 2 * extra, width).T,
        columns(middle, extra, extra),
        columns(middle, 0, extra).T,
        vector[0],
        vector[1],
        vector[2],
        vector[3],
        vector[4],
        vector[5],
    )


def solution(mesh):
    return jax.shard_map(
        on_device,
        mesh=mesh,
        in_specs=(
            P("dp", "blk", None),
            P("dp", "blk", None),
            P("dp", "blk"),
            P("dp", "blk"),
            P(None, "tensor"),
            P(None, "tensor"),
            P(None, "tensor"),
            P("tensor", None),
            P(None, "tensor"),
            P(None, "tensor"),
            P(None, "tensor"),
            P("tensor", None),
            P(None, "tensor"),
            P("tensor", None),
            P(None, "tensor"),
            P("tensor", None),
            P(),
            P(),
            P(),
            P(),
            P(),
            P(),
            P("dp", "blk", None),
        ),
        out_specs=(
            P("dp", "blk", None),
            P("dp", "blk", None),
            P("dp", "blk", "tensor"),
            P(None, "tensor"),
            P(None, "tensor"),
            P(None, "tensor"),
            P("tensor", None),
            P(None, "tensor"),
            P(None, "tensor"),
            P(None, "tensor"),
            P("tensor", None),
            P(None, "tensor"),
            P("tensor", None),
            P("tensor"),
            P("tensor"),
            P("tensor"),
            P("tensor"),
            P("tensor"),
            P("tensor"),
        ),
        check_vma=False,
    )
```

time: 814 us -> 675 us (0.83)
  waiting for transfers between devices: 407 us -> 249 us
  Pallas kernels: 75.6 us -> 147 us
  matrix products: 86.6 us -> 29 us
  starting transfers between devices: 76.5 us -> 114 us
  blocking collectives: 24.6 us -> 0 us
    ppermute x25 -> x28, waiting for transfers between devices: 160 us -> 53.5 us  [send_blk(): lax.ppermute(array, 'blk', [(i, (i + distance) % size) for i in range(siz...]
    psum x1, waiting for transfers between devices: 87.4 us -> 0.02 us  [on_device(): middle = lax.psum(middle, ('dp', 'blk'))]
    pallas_call x0 -> x8, Pallas kernels: none -> 74.5 us  [the longest x4 52.2 us: source_call(): pl.pallas_call(kernel, grid_spec=pltpu.PrefetchScalarGridSpec(num_scalar_...]
    ppermute x7 -> x20, waiting for transfers between devices: 137 us -> 184 us  [the longest x15 153 us: send_outer(): lax.ppermute(array, 'tensor', [(i, (i + 2 * distance) % size) for i in ra...]
    ppermute x25 -> x28, starting transfers between devices: 64.2 us -> 89.2 us  [send_blk(): lax.ppermute(array, 'blk', [(i, (i + distance) % size) for i in range(siz...]
    psum x1 -> x0, blocking collectives: 24.6 us -> none  [on_device(): vector = lax.psum(vector, ('dp', 'blk'))]
    dot_general x13 -> x3, matrix products: 31.8 us -> 9.15 us  [forward_mul(): return jnp.einsum('rti,ij->rtj', left, right, preferred_element_type=f32)]
    dot_general x13 -> x4, matrix products: 29.4 us -> 9.44 us  [backward_mul(): return jnp.einsum('rtj,ij->rti', left, right, preferred_element_type=f32)]
  transfers between devices with their start and end apart: 48 -> 66, of which waited for: 29 -> 31; matrix products, arithmetic and copies ran while one was open for 14% -> 12% of each run, Pallas kernels for 0% -> 14%
where the time goes in v2:
time: 675 us; the launch traced here: 672 us
  waiting for transfers between devices  249 us (37%)
  Pallas kernels  147 us (22%)
  starting transfers between devices  114 us (17%)
  local copies, waits for them, and re-layouts  63.3 us (9%)
  other arithmetic  53.4 us (8%)
  matrix products  29 us (4%)
  between operations  16.3 us (2%)
    ppermute x15, waiting for transfers between devices, send_outer(): lax.ppermute(array, 'tensor', [(i, (i + 2 * distance) % size) for i in ra...  153 us
    ppermute x28, starting transfers between devices, send_blk(): lax.ppermute(array, 'blk', [(i, (i + distance) % size) for i in range(siz...  89.2 us
    pallas_call x2, Pallas kernels, cross_call(): pl.pallas_call(functools.partial(cross_backward_kernel if backward else c...  59.8 us
    ppermute x28, waiting for transfers between devices, send_blk(): lax.ppermute(array, 'blk', [(i, (i + distance) % size) for i in range(siz...  53.5 us
    pallas_call x4, Pallas kernels, source_call(): pl.pallas_call(kernel, grid_spec=pltpu.PrefetchScalarGridSpec(num_scalar_...  52.2 us
    unnamed x169, local copies, waits for them, and re-layouts  28.4 us
    ppermute x1, waiting for transfers between devices, on_device(): side = lax.ppermute(side, 'blk', [(i, i - 1) for i in range(1, blocks)])  21.3 us
    ppermute x15, starting transfers between devices, send_outer(): lax.ppermute(array, 'tensor', [(i, (i + 2 * distance) % size) for i in ra...  18.2 us
  transfers between devices with their start and end apart: 66, of which 31 were waited for; matrix products, arithmetic and copies ran while one was open for 12% of the time, Pallas kernels for 14%

profile of v2, /device:TPU:0, one launch (start us, length us, event | category | flops | bytes accessed | tf_op | source)
XLA Modules:
  0.0 672.0 jit_solution(18398083515881765439)
XLA Ops:
  14.0 3.9 convolution_convert_fusion
  18.9 2.9 collective-permute-start
  24.1 16.1 %collective-permute-done = bf16[4,128,768]{2,1,0:T(8,128)(2,1)S(1)} collective-permute-done((bf16[4,128,768]{2,1,0:T(8,128)(2,1)S(1)}, bf16[4,128,768]{2,1,0:T(8,128)(2,1)S(1)}, u32[]{:S(2)}, u32[]{:S(2)}) %collective-permute-start) | collective-permute-done | bytes 786464 | tf_op jit(solution)/shard_map/ppermute | solution.py:648
  47.0 4.6 collective-permute-done.3
  51.6 10.4 %collective-permute-done.2 = bf16[1024,256]{1,0:T(8,128)(2,1)} collective-permute-done((bf16[1024,256]{1,0:T(8,128)(2,1)}, bf16[1024,256]{1,0:T(8,128)(2,1)}, u32[]{:S(2)}, u32[]{:S(2)}) %collective-permute-start.2) | collective-permute-done | bytes 524320 | tf_op jit(solution)/shard_map/ppermute | solution.py:648
  62.0 5.4 self_forward.1
  80.7 3.1 convolution_convert_fusion.2.refs_0_
  96.1 13.5 %collective-permute-done.12 = bf16[1024,512]{1,0:T(8,128)(2,1)} collective-permute-done((bf16[1024,512]{1,0:T(8,128)(2,1)}, bf16[1024,512]{1,0:T(8,128)(2,1)}, u32[]{:S(2)}, u32[]{:S(2)}) %collective-permute-start.12) | collective-permute-done | bytes 1048608 | tf_op jit(solution)/shard_map/ppermute | solution.py:648
  109.6 3.4 pad_maximum_fusion.1
  119.6 14.2 %source_project.1.refs_6_.refs_7_.refs_10_.refs_11_ = bf16[4,1024,1024]{2,1,0:T(8,128)(2,1)} custom-call(s32[1]{0:T(128)} %bitcast.19.row, bf16[8,1024,1024]{2,1,0:T(8,128)(2,1)} %tokens.3, bf16[1024,1024]{1,0:T(8,128)(2,1)} %copy-done.29), custom_call_target="tpu_custom_call" | custom-call | tf_op jit(solution)/shard_map/source_project/pallas_call | solution.py:497
  133.9 26.4 %cross_forward.1 = (bf16[4,144,512]{2,1,0:T(8,128)(2,1)}, bf16[4,144,512]{2,1,0:T(8,128)(2,1)}, bf16[4,144,512]{2,1,0:T(8,128)(2,1)}, bf16[4,144,512]{2,1,0:T(8,128)(2,1)}) custom-call(s32[4,8]{1,0:T(4,128)} %copy.231.table_ref, bf16[4,128,512]{2,1,0:T(8,128)(2,1)} %convolution_convert_fusion.2.refs_0_, bf16[4,128,512]{2,1,0:T(8,128)(2,1)} %collective-permute-done.9.refs_1_, ...), custom_call_target="tpu_custom_call" | custom-call | flops 4294967296 | bytes 8388608 | tf_op jit(solution)/shard_map/cross_forward/pallas_call | solution.py:379
  162.2 10.1 %collective-permute-start.14 = (bf16[4,144,512]{2,1,0:T(8,128)(2,1)S(1)}, bf16[4,144,512]{2,1,0:T(8,128)(2,1)S(1)}, u32[]{:S(2)}, u32[]{:S(2)}) collective-permute-start(bf16[4,144,512]{2,1,0:T(8,128)(2,1)S(1)} %copy-done.78), channel_id=1, source_target_pairs={{0,8},{4,12},{8,0},{12,4},{1,9},{5,13},{9,1},{13,5},{2,10},{6,14},... | collective-permute-start | bytes 1769480 | tf_op jit(solution)/shard_map/ppermute | solution.py:640
  177.8 49.9 %collective-permute-done.17 = bf16[1024,128]{1,0:T(8,128)(2,1)S(1)} collective-permute-done((bf16[1024,128]{1,0:T(8,128)(2,1)S(1)}, bf16[1024,128]{1,0:T(8,128)(2,1)S(1)}, u32[]{:S(2)}, u32[]{:S(2)}) %collective-permute-start.17) | collective-permute-done | bytes 262176 | tf_op jit(solution)/shard_map/ppermute | solution.py:648
  238.6 8.9 %ffn_forward.1 = (f32[512,1024]{1,0:T(8,128)S(1)}, bf16[512,2048]{1,0:T(8,128)(2,1)S(1)}, bf16[512,256]{1,0:T(8,128)(2,1)S(1)}, f32[512,256]{1,0:T(8,128)S(1)}) custom-call(bf16[512,1024]{1,0:T(8,128)(2,1)S(1)} %pad_maximum_fusion.10.tokens, bf16[1024,2048]{1,0:T(8,128)(2,1)S(1)} %constant_dynamic-update-slice_fusion.7.weight_in, ...), custom_call_target="tpu_custom_call" | custom-call | flops 4294967296 | bytes 8388608 | tf_op jit(solution)/shard_map/ffn_forward/pallas_call | solution.py:566
  259.6 8.4 %ffn_backward.1 = (f32[512,1024]{1,0:T(8,128)S(1)}, bf16[512,256]{1,0:T(8,128)(2,1)S(1)}) custom-call(bf16[512,1024]{1,0:T(8,128)(2,1)S(1)} %pad_maximum_fusion.11.grad, bf16[1024,2048]{1,0:T(8,128)(2,1)S(1)} %copy-done.12, bf16[2048,1024]{1,0:T(8,128)(2,1)} %pad_maximum_fusion.weight_out, bf16[1024,256]{1,0:T(8,128)(2,1)S(1)} %copy-done.20, ...), custom_call_target="tpu_custom_call" | custom-call | flops 4294967296 | bytes 8388608 | tf_op jit(solution)/shard_map/ffn_backward/pallas_call | solution.py:566
  287.2 14.1 %collective-permute-done.28 = bf16[1024,512]{1,0:T(8,128)(2,1)S(1)} collective-permute-done((bf16[1024,512]{1,0:T(8,128)(2,1)S(1)}, bf16[1024,512]{1,0:T(8,128)(2,1)S(1)}, u32[]{:S(2)}, u32[]{:S(2)}) %collective-permute-start.28) | collective-permute-done | bytes 1048608 | tf_op jit(solution)/shard_map/ppermute | solution.py:648
  302.6 9.5 %collective-permute-done.29 = bf16[256,1024]{1,0:T(8,128)(2,1)S(1)} collective-permute-done((bf16[256,1024]{1,0:T(8,128)(2,1)S(1)}, bf16[256,1024]{1,0:T(8,128)(2,1)S(1)}, u32[]{:S(2)}, u32[]{:S(2)}) %collective-permute-start.29) | collective-permute-done | bytes 524320 | tf_op jit(solution)/shard_map/ppermute | solution.py:648
  312.0 10.7 %collective-permute-done.26.refs_6_ = bf16[4,144,512]{2,1,0:T(8,128)(2,1)S(1)} collective-permute-done((bf16[4,144,512]{2,1,0:T(8,128)(2,1)S(1)}, bf16[4,144,512]{2,1,0:T(8,128)(2,1)S(1)}, u32[]{:S(2)}, u32[]{:S(2)}) %collective-permute-start.26) | collective-permute-done | bytes 589856 | tf_op jit(solution)/shard_map/ppermute | solution.py:640
  324.4 33.4 %cross_backward.1 = (bf16[4,128,512]{2,1,0:T(8,128)(2,1)}, bf16[4,128,512]{2,1,0:T(8,128)(2,1)}, bf16[4,128,512]{2,1,0:T(8,128)(2,1)}, bf16[4,128,512]{2,1,0:T(8,128)(2,1)}, bf16[4,1024,1024]{2,1,0:T(8,128)(2,1)}) custom-call(s32[4,8]{1,0:T(4,128)} %copy.231.table_ref, bf16[4,128,512]{2,1,0:T(8,128)(2,1)} %convolution_convert_fusion.2.refs_0_, ...), custom_call_target="tpu_custom_call" | custom-call | flops 10737418240 | bytes 16777216 | tf_op jit(solution)/shard_map/cross_backward/pallas_call | solution.py:379
  357.9 11.5 %collective-permute-start.32 = (bf16[4,128,512]{2,1,0:T(8,128)(2,1)}, bf16[4,128,512]{2,1,0:T(8,128)(2,1)S(1)}, u32[]{:S(2)}, u32[]{:S(2)}) collective-permute-start(bf16[4,128,512]{2,1,0:T(8,128)(2,1)} %get-tuple-element.149), channel_id=1, source_target_pairs={{0,12},{4,0},{8,4},{12,8},{1,13},{5,1},{9,5},{13,9},{2,14},{6,2},{... | collective-permute-start | bytes 1572872 | tf_op jit(solution)/shard_map/ppermute | solution.py:640
  369.4 6.6 collective-permute-start.33
  376.0 2.7 constant_dynamic-slice_fusion.1
  379.8 6.8 %collective-permute-done.32 = bf16[4,128,512]{2,1,0:T(8,128)(2,1)S(1)} collective-permute-done((bf16[4,128,512]{2,1,0:T(8,128)(2,1)}, bf16[4,128,512]{2,1,0:T(8,128)(2,1)S(1)}, u32[]{:S(2)}, u32[]{:S(2)}) %collective-permute-start.32) | collective-permute-done | bytes 524320 | tf_op jit(solution)/shard_map/ppermute | solution.py:640
  386.6 15.3 %source_weight.1 = f32[1024,1024]{1,0:T(8,128)} custom-call(s32[1]{0:T(128)} %bitcast.19.row, bf16[8,1024,1024]{2,1,0:T(8,128)(2,1)} %tokens.3, bf16[4,1024,1024]{2,1,0:T(8,128)(2,1)} %get-tuple-element.172.grad), custom_call_target="tpu_custom_call" | custom-call | tf_op jit(solution)/shard_map/source_weight/pallas_call | solution.py:497
  405.2 10.7 %source_other.1 = bf16[4,1024,512]{2,1,0:T(8,128)(2,1)} custom-call(bf16[4,1024,1024]{2,1,0:T(8,128)(2,1)} %get-tuple-element.172.grad, bf16[512,1024]{1,0:T(8,128)(2,1)} %pad_maximum_fusion.14.weight), custom_call_target="tpu_custom_call" | custom-call | tf_op jit(solution)/shard_map/source_other/pallas_call | solution.py:497
  415.9 5.6 collective-permute-done.33
  443.7 7.6 %self_backward.1 = (bf16[4,128,512]{2,1,0:T(8,128)(2,1)S(1)}, f32[4,128,512]{2,1,0:T(8,128)S(1)}, f32[4,128,512]{2,1,0:T(8,128)S(1)}, bf16[4,80,1024]{2,1,0:T(8,128)(2,1)S(1)}) custom-call(bf16[4,128,1536]{2,1,0:T(8,128)(2,1)S(1)} %pad_maximum_fusion.5.refs_0_.refs_1_.refs_2_, bf16[4,128,1536]{2,1,0:T(8,128)(2,1)S(1)} %pad_maximum_fusion.5.refs_0_.refs_1_.refs_2_, ...), custom_call_target="tpu_custom_call" | custom-call | flops 1342177280 | bytes 3145728 | tf_op jit(solution)/shard_map/self_backward/pallas_call | solution.py:623
  458.3 7.0 %collective-permute-done.54 = bf16[1024,512]{1,0:T(8,128)(2,1)} collective-permute-done((bf16[1024,512]{1,0:T(8,128)(2,1)S(1)}, bf16[1024,512]{1,0:T(8,128)(2,1)}, u32[]{:S(2)}, u32[]{:S(2)}) %collective-permute-start.54) | collective-permute-done | bytes 1048608 | tf_op jit(solution)/shard_map/ppermute | solution.py:648
  466.9 21.3 %collective-permute-done.38 = bf16[4,80,1024]{2,1,0:T(8,128)(2,1)S(1)} collective-permute-done((bf16[4,80,1024]{2,1,0:T(8,128)(2,1)S(1)}, bf16[4,80,1024]{2,1,0:T(8,128)(2,1)S(1)}, u32[]{:S(2)}, u32[]{:S(2)}) %collective-permute-start.38) | collective-permute-done | bytes 655392 | tf_op jit(solution)/shard_map/ppermute | solution.py:1013
  499.2 12.4 %collective-permute-done.39 = bf16[4,128,768]{2,1,0:T(8,128)(2,1)} collective-permute-done((bf16[4,128,768]{2,1,0:T(8,128)(2,1)}, bf16[4,128,768]{2,1,0:T(8,128)(2,1)}, u32[]{:S(2)}, u32[]{:S(2)}) %collective-permute-start.39) | collective-permute-done | bytes 786464 | tf_op jit(solution)/shard_map/ppermute | solution.py:648
  511.7 3.4 convolution_bitcast_fusion
  515.3 2.7 fusion.9
  518.0 2.6 convolution_add_fusion
  520.8 15.2 %collective-permute-done.45 = bf16[1152,512]{1,0:T(8,128)(2,1)S(1)} collective-permute-done((bf16[1152,512]{1,0:T(8,128)(2,1)}, bf16[1152,512]{1,0:T(8,128)(2,1)S(1)}, u32[]{:S(2)}, u32[]{:S(2)}) %collective-permute-start.45) | collective-permute-done | bytes 1179680 | tf_op jit(solution)/shard_map/ppermute | solution.py:648
  541.2 9.9 %collective-permute-done.46 = bf16[576,512]{1,0:T(8,128)(2,1)S(1)} collective-permute-done((bf16[576,512]{1,0:T(8,128)(2,1)S(1)}, bf16[576,512]{1,0:T(8,128)(2,1)S(1)}, u32[]{:S(2)}, u32[]{:S(2)}) %collective-permute-start.46) | collective-permute-done | bytes 589856 | tf_op jit(solution)/shard_map/ppermute | solution.py:663
  551.6 3.3 collective-permute-start.59
  556.1 10.0 %collective-permute-done.58 = bf16[128,768]{1,0:T(8,128)(2,1)S(1)} collective-permute-done((bf16[128,768]{1,0:T(8,128)(2,1)S(1)}, bf16[128,768]{1,0:T(8,128)(2,1)S(1)}, u32[]{:S(2)}, u32[]{:S(2)}) %collective-permute-start.58) | collective-permute-done | bytes 196640 | tf_op jit(solution)/shard_map/ppermute | solution.py:640
  566.3 6.0 collective-permute-start.60
  574.8 12.0 %source_own.1 = (f32[4,1024,256]{2,1,0:T(8,128)}, bf16[4,1024,256]{2,1,0:T(8,128)(2,1)}) custom-call(bf16[4,1024,1024]{2,1,0:T(8,128)(2,1)} %get-tuple-element.172.grad, bf16[512,1024]{1,0:T(8,128)(2,1)} %pad_maximum_fusion.16.weight, bf16[4,1024,512]{2,1,0:T(8,128)(2,1)} %collective-permute-done.47.across), custom_call_target="tpu_custom_call" | custom-call | tf_op jit(solution)/shard_map/source_own/pallas_call | solution.py:497
  587.8 6.7 collective-permute-done.61
  596.2 18.7 %collective-permute-start.48 = (bf16[144,512]{1,0:T(8,128)(2,1)S(1)}, bf16[144,512]{1,0:T(8,128)(2,1)S(1)}, u32[]{:S(2)}, u32[]{:S(2)}) collective-permute-start(bf16[144,512]{1,0:T(8,128)(2,1)S(1)} %get-tuple-element.354), channel_id=1, source_target_pairs={{0,4},{4,8},{8,12},{12,0},{1,5},{5,9},{9,13},{13,1},{2,6},{6,10},{... | collective-permute-start | bytes 442376 | tf_op jit(solution)/shard_map/ppermute | solution.py:640
  619.2 4.8 collective-permute-done.49
  624.3 3.5 collective-permute-start.51
  627.8 3.4 collective-permute-start.52
  635.5 4.6 collective-permute-done.52
  640.3 2.9 convert_bitcast_fusion
  650.1 4.1 broadcast_in_dim.30
  656.6 4.0 convert_dynamic-update-slice_fusion
  (439 shorter events, 181.5 us)
Async XLA Ops:
  7.2 633.1 %all-reduce.6.cloned.1.call-start = ((), (), s32[]{:S(2)}) async-start(), calls=%async_computation | async-start | bytes 4194304 | tf_op jit(solution)/shard_map/psum | solution.py:1015
  18.9 21.3 %collective-permute-start = (bf16[4,128,768]{2,1,0:T(8,128)(2,1)S(1)}, bf16[4,128,768]{2,1,0:T(8,128)(2,1)S(1)}, u32[]{:S(2)}, u32[]{:S(2)}) collective-permute-start(bf16[4,128,768]{2,1,0:T(8,128)(2,1)S(1)} %get-tuple-element.351), channel_id=1, source_target_pairs={{0,2},{1,3},{2,0},{3,1},{4,6},{5,7},{6,4},{7,5},{8,10},{9,11},{10,... | collective-permute-start | bytes 2359304 | tf_op jit(solution)/shard_map/ppermute | solution.py:648
  21.9 29.7 %collective-permute-start.3 = (bf16[256,1024]{1,0:T(8,128)(2,1)}, bf16[256,1024]{1,0:T(8,128)(2,1)}, u32[]{:S(2)}, u32[]{:S(2)}) collective-permute-start(bf16[256,1024]{1,0:T(8,128)(2,1)} %param.30), channel_id=1, source_target_pairs={{0,2},{1,3},{2,0},{3,1},{4,6},{5,7},{6,4},{7,5},{8,10},{9,11},{10,... | collective-permute-start | bytes 1572872 | tf_op jit(solution)/shard_map/ppermute | solution.py:648
  21.9 23.0 %collective-permute-start.4 = (s32[4,128]{1,0:T(4,128)S(1)}, s32[4,128]{1,0:T(4,128)S(1)}, u32[]{:S(2)}, u32[]{:S(2)}) collective-permute-start(s32[4,128]{1,0:T(4,128)S(1)} %constant_dynamic-slice_fusion.7), channel_id=1, source_target_pairs={{0,4},{4,8},{8,12},{12,0},{1,5},{5,9},{9,13},{13,1},{2,6},{6,10},{... | collective-permute-start | bytes 6152 | tf_op jit(solution)/shard_map/ppermute | solution.py:640
  41.2 20.8 %collective-permute-start.1 = (bf16[4,80,1024]{2,1,0:T(8,128)(2,1)S(1)}, bf16[4,80,1024]{2,1,0:T(8,128)(2,1)S(1)}, u32[]{:S(2)}, u32[]{:S(2)}) collective-permute-start(bf16[4,80,1024]{2,1,0:T(8,128)(2,1)S(1)} %pad_maximum_fusion.19), channel_id=1, source_target_pairs={{0,4},{4,8},{8,12},{12,0},{1,5},{5,9},{9,13},{13,1},{2,6},{6,10},{... | collective-permute-start | bytes 1966088 | tf_op jit(solution)/shard_map/ppermute | solution.py:640
  43.4 18.6 %collective-permute-start.2 = (bf16[1024,256]{1,0:T(8,128)(2,1)}, bf16[1024,256]{1,0:T(8,128)(2,1)}, u32[]{:S(2)}, u32[]{:S(2)}) collective-permute-start(bf16[1024,256]{1,0:T(8,128)(2,1)} %param.31), channel_id=1, source_target_pairs={{0,2},{1,3},{2,0},{3,1},{4,6},{5,7},{6,4},{7,5},{8,10},{9,11},{10,... | collective-permute-start | bytes 1572872 | tf_op jit(solution)/shard_map/ppermute | solution.py:648
  83.8 25.8 %collective-permute-start.12 = (bf16[1024,512]{1,0:T(8,128)(2,1)}, bf16[1024,512]{1,0:T(8,128)(2,1)}, u32[]{:S(2)}, u32[]{:S(2)}) collective-permute-start(bf16[1024,512]{1,0:T(8,128)(2,1)} %pad_maximum_fusion.9), channel_id=1, source_target_pairs={{0,2},{1,3},{2,0},{3,1},{4,6},{5,7},{6,4},{7,5},{8,10},{9,11},{10,... | collective-permute-start | bytes 3145736 | tf_op jit(solution)/shard_map/ppermute | solution.py:648
  92.2 41.7 %collective-permute-start.10 = (bf16[4,128,512]{2,1,0:T(8,128)(2,1)}, bf16[4,128,512]{2,1,0:T(8,128)(2,1)}, u32[]{:S(2)}, u32[]{:S(2)}) collective-permute-start(bf16[4,128,512]{2,1,0:T(8,128)(2,1)} %convolution_convert_fusion.2.refs_0_), channel_id=1, source_target_pairs={{0,8},{4,12},{8,0},{12,4},{1,9},{5,13},{9,1},{13,5},{2,10},{6,14},... | collective-permute-start | bytes 1572872 | tf_op jit(solution)/shard_map/ppermute | solution.py:640
  93.9 40.0 %collective-permute-start.11 = (bf16[4,128,512]{2,1,0:T(8,128)(2,1)}, bf16[4,128,512]{2,1,0:T(8,128)(2,1)}, u32[]{:S(2)}, u32[]{:S(2)}) collective-permute-start(bf16[4,128,512]{2,1,0:T(8,128)(2,1)} %convolution_convert_fusion.2.refs_0_), channel_id=1, source_target_pairs={{0,12},{4,0},{8,4},{12,8},{1,13},{5,1},{9,5},{13,9},{2,14},{6,2},{... | collective-permute-start | bytes 1572872 | tf_op jit(solution)/shard_map/ppermute | solution.py:640
  96.1 37.8 %collective-permute-start.9 = (bf16[4,128,512]{2,1,0:T(8,128)(2,1)}, bf16[4,128,512]{2,1,0:T(8,128)(2,1)}, u32[]{:S(2)}, u32[]{:S(2)}) collective-permute-start(bf16[4,128,512]{2,1,0:T(8,128)(2,1)} %convolution_convert_fusion.2.refs_0_), channel_id=1, source_target_pairs={{0,4},{4,8},{8,12},{12,0},{1,5},{5,9},{9,13},{13,1},{2,6},{6,10},{... | collective-permute-start | bytes 1572872 | tf_op jit(solution)/shard_map/ppermute | solution.py:640
  113.0 60.1 %collective-permute-start.16 = (bf16[1280,1024]{1,0:T(8,128)(2,1)}, bf16[1280,1024]{1,0:T(8,128)(2,1)}, u32[]{:S(2)}, u32[]{:S(2)}) collective-permute-start(bf16[1280,1024]{1,0:T(8,128)(2,1)} %pad_maximum_fusion.1), channel_id=1, source_target_pairs={{0,2},{1,3},{2,0},{3,1},{4,6},{5,7},{6,4},{7,5},{8,10},{9,11},{10,... | collective-permute-start | bytes 7864328 | tf_op jit(solution)/shard_map/ppermute | solution.py:648
  160.6 70.0 %collective-permute-start.20 = (bf16[1152,1024]{1,0:T(8,128)(2,1)S(1)}, bf16[1152,1024]{1,0:T(8,128)(2,1)S(1)}, u32[]{:S(2)}, u32[]{:S(2)}) collective-permute-start(bf16[1152,1024]{1,0:T(8,128)(2,1)S(1)} %pad_maximum_fusion.2), channel_id=1, source_target_pairs={{0,2},{1,3},{2,0},{3,1},{4,6},{5,7},{6,4},{7,5},{8,10},{9,11},{10,... | collective-permute-start | bytes 7077896 | tf_op jit(solution)/shard_map/ppermute | solution.py:648
  161.4 66.3 %collective-permute-start.13 = (bf16[4,144,512]{2,1,0:T(8,128)(2,1)S(1)}, bf16[4,144,512]{2,1,0:T(8,128)(2,1)S(1)}, u32[]{:S(2)}, u32[]{:S(2)}) collective-permute-start(bf16[4,144,512]{2,1,0:T(8,128)(2,1)S(1)} %copy-done.79), channel_id=1, source_target_pairs={{0,12},{4,0},{8,4},{12,8},{1,13},{5,1},{9,5},{13,9},{2,14},{6,2},{... | collective-permute-start | bytes 1769480 | tf_op jit(solution)/shard_map/ppermute | solution.py:640
  162.2 65.5 %collective-permute-start.14 = (bf16[4,144,512]{2,1,0:T(8,128)(2,1)S(1)}, bf16[4,144,512]{2,1,0:T(8,128)(2,1)S(1)}, u32[]{:S(2)}, u32[]{:S(2)}) collective-permute-start(bf16[4,144,512]{2,1,0:T(8,128)(2,1)S(1)} %copy-done.78), channel_id=1, source_target_pairs={{0,8},{4,12},{8,0},{12,4},{1,9},{5,13},{9,1},{13,5},{2,10},{6,14},... | collective-permute-start | bytes 1769480 | tf_op jit(solution)/shard_map/ppermute | solution.py:640
  172.4 55.4 %collective-permute-start.15 = (bf16[4,144,512]{2,1,0:T(8,128)(2,1)S(1)}, bf16[4,144,512]{2,1,0:T(8,128)(2,1)S(1)}, u32[]{:S(2)}, u32[]{:S(2)}) collective-permute-start(bf16[4,144,512]{2,1,0:T(8,128)(2,1)S(1)} %copy-done.77), channel_id=1, source_target_pairs={{0,4},{4,8},{8,12},{12,0},{1,5},{5,9},{9,13},{13,1},{2,6},{6,10},{... | collective-permute-start | bytes 1769480 | tf_op jit(solution)/shard_map/ppermute | solution.py:640
  173.1 54.6 %collective-permute-start.17 = (bf16[1024,128]{1,0:T(8,128)(2,1)S(1)}, bf16[1024,128]{1,0:T(8,128)(2,1)S(1)}, u32[]{:S(2)}, u32[]{:S(2)}) collective-permute-start(bf16[1024,128]{1,0:T(8,128)(2,1)S(1)} %copy-done.65), channel_id=1, source_target_pairs={{0,2},{1,3},{2,0},{3,1},{4,6},{5,7},{6,4},{7,5},{8,10},{9,11},{10,... | collective-permute-start | bytes 786440 | tf_op jit(solution)/shard_map/ppermute | solution.py:648
  275.3 26.1 %collective-permute-start.28 = (bf16[1024,512]{1,0:T(8,128)(2,1)S(1)}, bf16[1024,512]{1,0:T(8,128)(2,1)S(1)}, u32[]{:S(2)}, u32[]{:S(2)}) collective-permute-start(bf16[1024,512]{1,0:T(8,128)(2,1)S(1)} %pad_maximum_fusion.13), channel_id=1, source_target_pairs={{0,2},{1,3},{2,0},{3,1},{4,6},{5,7},{6,4},{7,5},{8,10},{9,11},{10,... | collective-permute-start | bytes 3145736 | tf_op jit(solution)/shard_map/ppermute | solution.py:648
  280.1 31.9 %collective-permute-start.25 = (bf16[4,144,512]{2,1,0:T(8,128)(2,1)S(1)}, bf16[4,144,512]{2,1,0:T(8,128)(2,1)S(1)}, u32[]{:S(2)}, u32[]{:S(2)}) collective-permute-start(bf16[4,144,512]{2,1,0:T(8,128)(2,1)S(1)} %cross_prepare.1.refs_4_), channel_id=1, source_target_pairs={{0,4},{4,8},{8,12},{12,0},{1,5},{5,9},{9,13},{13,1},{2,6},{6,10},{... | collective-permute-start | bytes 1769480 | tf_op jit(solution)/shard_map/ppermute | solution.py:640
  281.7 41.0 %collective-permute-start.26 = (bf16[4,144,512]{2,1,0:T(8,128)(2,1)S(1)}, bf16[4,144,512]{2,1,0:T(8,128)(2,1)S(1)}, u32[]{:S(2)}, u32[]{:S(2)}) collective-permute-start(bf16[4,144,512]{2,1,0:T(8,128)(2,1)S(1)} %cross_prepare.1.refs_4_), channel_id=1, source_target_pairs={{0,8},{4,12},{8,0},{12,4},{1,9},{5,13},{9,1},{13,5},{2,10},{6,14},... | collective-permute-start | bytes 1769480 | tf_op jit(solution)/shard_map/ppermute | solution.py:640
  284.3 38.4 %collective-permute-start.27 = (bf16[4,144,512]{2,1,0:T(8,128)(2,1)S(1)}, bf16[4,144,512]{2,1,0:T(8,128)(2,1)S(1)}, u32[]{:S(2)}, u32[]{:S(2)}) collective-permute-start(bf16[4,144,512]{2,1,0:T(8,128)(2,1)S(1)} %cross_prepare.1.refs_4_), channel_id=1, source_target_pairs={{0,12},{4,0},{8,4},{12,8},{1,13},{5,1},{9,5},{13,9},{2,14},{6,2},{... | collective-permute-start | bytes 1769480 | tf_op jit(solution)/shard_map/ppermute | solution.py:640
  285.7 26.4 %collective-permute-start.29 = (bf16[256,1024]{1,0:T(8,128)(2,1)S(1)}, bf16[256,1024]{1,0:T(8,128)(2,1)S(1)}, u32[]{:S(2)}, u32[]{:S(2)}) collective-permute-start(bf16[256,1024]{1,0:T(8,128)(2,1)S(1)} %get-tuple-element.141), channel_id=1, source_target_pairs={{0,2},{1,3},{2,0},{3,1},{4,6},{5,7},{6,4},{7,5},{8,10},{9,11},{10,... | collective-permute-start | bytes 1572872 | tf_op jit(solution)/shard_map/ppermute | solution.py:648
  357.8 63.6 %collective-permute-start.35 = (bf16[1024,768]{1,0:T(8,128)(2,1)}, bf16[1024,768]{1,0:T(8,128)(2,1)}, u32[]{:S(2)}, u32[]{:S(2)}) collective-permute-start(bf16[1024,768]{1,0:T(8,128)(2,1)} %constant_dynamic-update-slice_fusion), channel_id=1, source_target_pairs={{0,2},{1,3},{2,0},{3,1},{4,6},{5,7},{6,4},{7,5},{8,10},{9,11},{10,... | collective-permute-start | bytes 4718600 | tf_op jit(solution)/shard_map/ppermute | solution.py:648
  357.9 28.7 %collective-permute-start.32 = (bf16[4,128,512]{2,1,0:T(8,128)(2,1)}, bf16[4,128,512]{2,1,0:T(8,128)(2,1)S(1)}, u32[]{:S(2)}, u32[]{:S(2)}) collective-permute-start(bf16[4,128,512]{2,1,0:T(8,128)(2,1)} %get-tuple-element.149), channel_id=1, source_target_pairs={{0,12},{4,0},{8,4},{12,8},{1,13},{5,1},{9,5},{13,9},{2,14},{6,2},{... | collective-permute-start | bytes 1572872 | tf_op jit(solution)/shard_map/ppermute | solution.py:640
  369.4 52.1 %collective-permute-start.33 = (bf16[4,128,512]{2,1,0:T(8,128)(2,1)}, bf16[4,128,512]{2,1,0:T(8,128)(2,1)S(1)}, u32[]{:S(2)}, u32[]{:S(2)}) collective-permute-start(bf16[4,128,512]{2,1,0:T(8,128)(2,1)} %get-tuple-element.150), channel_id=1, source_target_pairs={{0,8},{4,12},{8,0},{12,4},{1,9},{5,13},{9,1},{13,5},{2,10},{6,14},... | collective-permute-start | bytes 1572872 | tf_op jit(solution)/shard_map/ppermute | solution.py:640
  376.0 45.5 %collective-permute-start.34 = (bf16[4,128,512]{2,1,0:T(8,128)(2,1)}, bf16[4,128,512]{2,1,0:T(8,128)(2,1)}, u32[]{:S(2)}, u32[]{:S(2)}) collective-permute-start(bf16[4,128,512]{2,1,0:T(8,128)(2,1)} %get-tuple-element.151), channel_id=1, source_target_pairs={{0,4},{4,8},{8,12},{12,0},{1,5},{5,9},{9,13},{13,1},{2,6},{6,10},{... | collective-permute-start | bytes 1572872 | tf_op jit(solution)/shard_map/ppermute | solution.py:640
  439.8 25.5 %collective-permute-start.54 = (bf16[1024,512]{1,0:T(8,128)(2,1)S(1)}, bf16[1024,512]{1,0:T(8,128)(2,1)}, u32[]{:S(2)}, u32[]{:S(2)}) collective-permute-start(bf16[1024,512]{1,0:T(8,128)(2,1)S(1)} %copy-done.56), channel_id=1, source_target_pairs={{0,2},{1,3},{2,0},{3,1},{4,6},{5,7},{6,4},{7,5},{8,10},{9,11},{10,... | collective-permute-start | bytes 3145736 | tf_op jit(solution)/shard_map/ppermute | solution.py:648
  440.2 134.6 %collective-permute-start.47 = (bf16[4,1024,512]{2,1,0:T(8,128)(2,1)}, bf16[4,1024,512]{2,1,0:T(8,128)(2,1)}, u32[]{:S(2)}, u32[]{:S(2)}) collective-permute-start(bf16[4,1024,512]{2,1,0:T(8,128)(2,1)} %source_other.1), channel_id=1, source_target_pairs={{0,1},{1,0},{2,3},{3,2},{4,5},{5,4},{6,7},{7,6},{8,9},{9,8},{10,11... | collective-permute-start | bytes 12582920 | tf_op jit(solution)/shard_map/ppermute | solution.py:644
  451.3 36.9 %collective-permute-start.38 = (bf16[4,80,1024]{2,1,0:T(8,128)(2,1)S(1)}, bf16[4,80,1024]{2,1,0:T(8,128)(2,1)S(1)}, u32[]{:S(2)}, u32[]{:S(2)}) collective-permute-start(bf16[4,80,1024]{2,1,0:T(8,128)(2,1)S(1)} %get-tuple-element.161), channel_id=1, source_target_pairs={{4,0},{8,4},{12,8},{5,1},{9,5},{13,9},{6,2},{10,6},{14,10},{7,3},{... | collective-permute-start | bytes 1966088 | tf_op jit(solution)/shard_map/ppermute | solution.py:1013
  457.2 39.1 %collective-permute-start.44 = (f32[6,1024]{1,0:T(8,128)S(1)}, f32[6,1024]{1,0:T(8,128)S(1)}, u32[]{:S(2)}, u32[]{:S(2)}) collective-permute-start(f32[6,1024]{1,0:T(8,128)S(1)} %stack.59), channel_id=1, source_target_pairs={{0,1},{1,0},{2,3},{3,2},{4,5},{5,4},{6,7},{7,6},{8,9},{9,8},{10,11... | collective-permute-start | bytes 73736 | tf_op jit(solution)/shard_map/ppermute | solution.py:644
  491.0 20.7 %collective-permute-start.39 = (bf16[4,128,768]{2,1,0:T(8,128)(2,1)}, bf16[4,128,768]{2,1,0:T(8,128)(2,1)}, u32[]{:S(2)}, u32[]{:S(2)}) collective-permute-start(bf16[4,128,768]{2,1,0:T(8,128)(2,1)} %pad_maximum_fusion.18), channel_id=1, source_target_pairs={{0,2},{1,3},{2,0},{3,1},{4,6},{5,7},{6,4},{7,5},{8,10},{9,11},{10,... | collective-permute-start | bytes 2359304 | tf_op jit(solution)/shard_map/ppermute | solution.py:648
  497.5 38.5 %collective-permute-start.45 = (bf16[1152,512]{1,0:T(8,128)(2,1)}, bf16[1152,512]{1,0:T(8,128)(2,1)S(1)}, u32[]{:S(2)}, u32[]{:S(2)}) collective-permute-start(bf16[1152,512]{1,0:T(8,128)(2,1)} %fusion.21), channel_id=1, source_target_pairs={{0,2},{1,3},{2,0},{3,1},{4,6},{5,7},{6,4},{7,5},{8,10},{9,11},{10,... | collective-permute-start | bytes 3538952 | tf_op jit(solution)/shard_map/ppermute | solution.py:648
  515.2 23.6 %collective-permute-start.56 = (bf16[512,768]{1,0:T(8,128)(2,1)S(1)}, bf16[512,768]{1,0:T(8,128)(2,1)S(1)}, u32[]{:S(2)}, u32[]{:S(2)}) collective-permute-start(bf16[512,768]{1,0:T(8,128)(2,1)S(1)} %dynamic-slice_convert_fusion), channel_id=1, source_target_pairs={{0,16},{16,0},{1,17},{17,1},{2,18},{18,2},{3,19},{19,3},{4,20},{20... | collective-permute-start | bytes 2359304 | tf_op jit(solution)/shard_map/ppermute | solution.py:663
  520.7 15.9 %collective-permute-start.40 = (bf16[256,1024]{1,0:T(8,128)(2,1)S(1)}, bf16[256,1024]{1,0:T(8,128)(2,1)S(1)}, u32[]{:S(2)}, u32[]{:S(2)}) collective-permute-start(bf16[256,1024]{1,0:T(8,128)(2,1)S(1)} %dynamic-slice_convert_fusion.2), channel_id=1, source_target_pairs={{0,1},{1,0},{2,3},{3,2},{4,5},{5,4},{6,7},{7,6},{8,9},{9,8},{10,11... | collective-permute-start | bytes 1572872 | tf_op jit(solution)/shard_map/ppermute | solution.py:644
  536.5 14.7 %collective-permute-start.46 = (bf16[576,512]{1,0:T(8,128)(2,1)S(1)}, bf16[576,512]{1,0:T(8,128)(2,1)S(1)}, u32[]{:S(2)}, u32[]{:S(2)}) collective-permute-start(bf16[576,512]{1,0:T(8,128)(2,1)S(1)} %dynamic-slice_convert_fusion.1), channel_id=1, source_target_pairs={{0,16},{16,0},{1,17},{17,1},{2,18},{18,2},{3,19},{19,3},{4,20},{20... | collective-permute-start | bytes 1769480 | tf_op jit(solution)/shard_map/ppermute | solution.py:663
  536.9 36.5 %collective-permute-start.41 = (bf16[256,1024]{1,0:T(8,128)(2,1)S(1)}, bf16[256,1024]{1,0:T(8,128)(2,1)S(1)}, u32[]{:S(2)}, u32[]{:S(2)}) collective-permute-start(bf16[256,1024]{1,0:T(8,128)(2,1)S(1)} %add_convert_fusion.1), channel_id=1, source_target_pairs={{0,1},{1,0},{2,3},{3,2},{4,5},{5,4},{6,7},{7,6},{8,9},{9,8},{10,11... | collective-permute-start | bytes 1572872 | tf_op jit(solution)/shard_map/ppermute | solution.py:644
  536.9 37.7 %collective-permute-start.42 = (bf16[256,1024]{1,0:T(8,128)(2,1)S(1)}, bf16[256,1024]{1,0:T(8,128)(2,1)S(1)}, u32[]{:S(2)}, u32[]{:S(2)}) collective-permute-start(bf16[256,1024]{1,0:T(8,128)(2,1)S(1)} %add_convert_fusion.1), channel_id=1, source_target_pairs={{0,2},{1,3},{2,0},{3,1},{4,6},{5,7},{6,4},{7,5},{8,10},{9,11},{10,... | collective-permute-start | bytes 1572872 | tf_op jit(solution)/shard_map/ppermute | solution.py:648
  539.0 12.6 %collective-permute-start.57 = (bf16[128,768]{1,0:T(8,128)(2,1)S(1)}, bf16[128,768]{1,0:T(8,128)(2,1)S(1)}, u32[]{:S(2)}, u32[]{:S(2)}) collective-permute-start(bf16[128,768]{1,0:T(8,128)(2,1)S(1)} %get-tuple-element.347), channel_id=1, source_target_pairs={{0,4},{4,8},{8,12},{12,0},{1,5},{5,9},{9,13},{13,1},{2,6},{6,10},{... | collective-permute-start | bytes 589832 | tf_op jit(solution)/shard_map/ppermute | solution.py:640
  551.2 15.0 %collective-permute-start.58 = (bf16[128,768]{1,0:T(8,128)(2,1)S(1)}, bf16[128,768]{1,0:T(8,128)(2,1)S(1)}, u32[]{:S(2)}, u32[]{:S(2)}) collective-permute-start(bf16[128,768]{1,0:T(8,128)(2,1)S(1)} %get-tuple-element.349), channel_id=1, source_target_pairs={{0,8},{4,12},{8,0},{12,4},{1,9},{5,13},{9,1},{13,5},{2,10},{6,14},... | collective-permute-start | bytes 589832 | tf_op jit(solution)/shard_map/ppermute | solution.py:640
  551.6 14.5 %collective-permute-start.59 = (bf16[128,768]{1,0:T(8,128)(2,1)S(1)}, bf16[128,768]{1,0:T(8,128)(2,1)S(1)}, u32[]{:S(2)}, u32[]{:S(2)}) collective-permute-start(bf16[128,768]{1,0:T(8,128)(2,1)S(1)} %get-tuple-element.348), channel_id=1, source_target_pairs={{0,12},{4,0},{8,4},{12,8},{1,13},{5,1},{9,5},{13,9},{2,14},{6,2},{... | collective-permute-start | bytes 589832 | tf_op jit(solution)/shard_map/ppermute | solution.py:640
  566.3 21.5 %collective-permute-start.60 = (bf16[128,768]{1,0:T(8,128)(2,1)S(1)}, bf16[128,768]{1,0:T(8,128)(2,1)S(1)}, u32[]{:S(2)}, u32[]{:S(2)}) collective-permute-start(bf16[128,768]{1,0:T(8,128)(2,1)S(1)} %get-tuple-element.318), channel_id=1, source_target_pairs={{0,4},{4,8},{8,12},{12,0},{1,5},{5,9},{9,13},{13,1},{2,6},{6,10},{... | collective-permute-start | bytes 589832 | tf_op jit(solution)/shard_map/ppermute | solution.py:640
  572.2 22.3 %collective-permute-start.61 = (bf16[128,768]{1,0:T(8,128)(2,1)S(1)}, bf16[128,768]{1,0:T(8,128)(2,1)S(1)}, u32[]{:S(2)}, u32[]{:S(2)}) collective-permute-start(bf16[128,768]{1,0:T(8,128)(2,1)S(1)} %get-tuple-element.318), channel_id=1, source_target_pairs={{0,8},{4,12},{8,0},{12,4},{1,9},{5,13},{9,1},{13,5},{2,10},{6,14},... | collective-permute-start | bytes 589832 | tf_op jit(solution)/shard_map/ppermute | solution.py:640
  573.3 21.2 %collective-permute-start.62 = (bf16[128,768]{1,0:T(8,128)(2,1)S(1)}, bf16[128,768]{1,0:T(8,128)(2,1)S(1)}, u32[]{:S(2)}, u32[]{:S(2)}) collective-permute-start(bf16[128,768]{1,0:T(8,128)(2,1)S(1)} %get-tuple-element.318), channel_id=1, source_target_pairs={{0,12},{4,0},{8,4},{12,8},{1,13},{5,1},{9,5},{13,9},{2,14},{6,2},{... | collective-permute-start | bytes 589832 | tf_op jit(solution)/shard_map/ppermute | solution.py:640
  574.7 40.3 %collective-permute-start.43 = (bf16[256,1024]{1,0:T(8,128)(2,1)S(1)}, bf16[256,1024]{1,0:T(8,128)(2,1)S(1)}, u32[]{:S(2)}, u32[]{:S(2)}) collective-permute-start(bf16[256,1024]{1,0:T(8,128)(2,1)S(1)} %collective-permute-done.42), channel_id=1, source_target_pairs={{0,1},{1,0},{2,3},{3,2},{4,5},{5,4},{6,7},{7,6},{8,9},{9,8},{10,11... | collective-permute-start | bytes 1572872 | tf_op jit(solution)/shard_map/ppermute | solution.py:644
  586.8 53.5 %collective-permute-start.55 = (bf16[4,1024,256]{2,1,0:T(8,128)(2,1)}, bf16[4,1024,256]{2,1,0:T(8,128)(2,1)}, u32[]{:S(2)}, u32[]{:S(2)}) collective-permute-start(bf16[4,1024,256]{2,1,0:T(8,128)(2,1)} %get-tuple-element.184), channel_id=1, source_target_pairs={{0,2},{1,3},{2,0},{3,1},{4,6},{5,7},{6,4},{7,5},{8,10},{9,11},{10,... | collective-permute-start | bytes 6291464 | tf_op jit(solution)/shard_map/ppermute | solution.py:648
  594.6 36.9 %collective-permute-start.63 = (bf16[512,768]{1,0:T(8,128)(2,1)S(1)}, bf16[512,768]{1,0:T(8,128)(2,1)S(1)}, u32[]{:S(2)}, u32[]{:S(2)}) collective-permute-start(bf16[512,768]{1,0:T(8,128)(2,1)S(1)} %constant_dynamic-update-slice_fusion.15), channel_id=1, source_target_pairs={{0,16},{16,0},{1,17},{17,1},{2,18},{18,2},{3,19},{19,3},{4,20},{20... | collective-permute-start | bytes 2359304 | tf_op jit(solution)/shard_map/ppermute | solution.py:663
  596.2 23.0 %collective-permute-start.48 = (bf16[144,512]{1,0:T(8,128)(2,1)S(1)}, bf16[144,512]{1,0:T(8,128)(2,1)S(1)}, u32[]{:S(2)}, u32[]{:S(2)}) collective-permute-start(bf16[144,512]{1,0:T(8,128)(2,1)S(1)} %get-tuple-element.354), channel_id=1, source_target_pairs={{0,4},{4,8},{8,12},{12,0},{1,5},{5,9},{9,13},{13,1},{2,6},{6,10},{... | collective-permute-start | bytes 442376 | tf_op jit(solution)/shard_map/ppermute | solution.py:640
  627.8 12.3 %collective-permute-start.52 = (bf16[144,512]{1,0:T(8,128)(2,1)S(1)}, bf16[144,512]{1,0:T(8,128)(2,1)S(1)}, u32[]{:S(2)}, u32[]{:S(2)}) collective-permute-start(bf16[144,512]{1,0:T(8,128)(2,1)S(1)} %get-tuple-element.320), channel_id=1, source_target_pairs={{0,8},{4,12},{8,0},{12,4},{1,9},{5,13},{9,1},{13,5},{2,10},{6,14},... | collective-permute-start | bytes 442376 | tf_op jit(solution)/shard_map/ppermute | solution.py:640
  645.3 15.3 %collective-permute-start.64 = (bf16[576,512]{1,0:T(8,128)(2,1)S(1)}, bf16[576,512]{1,0:T(8,128)(2,1)}, u32[]{:S(2)}, u32[]{:S(2)}) collective-permute-start(bf16[576,512]{1,0:T(8,128)(2,1)S(1)} %constant_dynamic-update-slice_fusion.20), channel_id=1, source_target_pairs={{0,16},{16,0},{1,17},{17,1},{2,18},{18,2},{3,19},{19,3},{4,20},{20... | collective-permute-start | bytes 1769480 | tf_op jit(solution)/shard_map/ppermute | solution.py:663
  (101 other events, 922.9 us)
Sparse Core Ops, SparseCore 0:
  496.4 119.5 all-reduce.5

commit v3 on v2

--- a/solution.py
+++ b/solution.py
@@ -1111,7 +1111,7 @@
         return array[:, first : first + size].astype(f32)
 
     return (
-        everywhere(results, bf16),
+        everywhere(list(tie(q_grad, *results)), bf16),
         everywhere(target_grads, f32),
         source_grad,
         columns(last, 0, width),

time: 675 us -> 728 us (1.079)
  waiting for transfers between devices: 249 us -> 306 us
  starting transfers between devices: 114 us -> 106 us
    ppermute x1, waiting for transfers between devices: 21.3 us -> 49.1 us  [on_device(): side = lax.ppermute(side, 'blk', [(i, i - 1) for i in range(1, blocks)])]
    ppermute x15, waiting for transfers between devices: 153 us -> 173 us  [send_outer(): lax.ppermute(array, 'tensor', [(i, (i + 2 * distance) % size) for i in ra...]
    ppermute x4, waiting for transfers between devices: 9.93 us -> 19.6 us  [send_dp(): lax.ppermute(array, 'dp', [(i, (i + step) % groups) for i in range(groups)])]
    ppermute x28, starting transfers between devices: 89.2 us -> 80 us  [send_blk(): lax.ppermute(array, 'blk', [(i, (i + distance) % size) for i in range(siz...]
    unnamed x169 -> x173, local copies, waits for them, and re-layouts: 28.4 us -> 29.8 us
  transfers between devices with their start and end apart: 66 -> 66, of which waited for: 31 -> 29; matrix products, arithmetic and copies ran while one was open for 12% -> 12% of each run, Pallas kernels for 14% -> 12%
where the time goes in v3:
time: 728 us; the launch traced here: 721 us
  waiting for transfers between devices  306 us (42%)
  Pallas kernels  141 us (19%)
  starting transfers between devices  106 us (15%)
  local copies, waits for them, and re-layouts  69.3 us (10%)
  other arithmetic  53.7 us (7%)
  matrix products  28 us (4%)
  between operations  16.3 us (2%)
    ppermute x15, waiting for transfers between devices, send_outer(): lax.ppermute(array, 'tensor', [(i, (i + 2 * distance) % size) for i in ra...  173 us
    ppermute x28, starting transfers between devices, send_blk(): lax.ppermute(array, 'blk', [(i, (i + distance) % size) for i in range(siz...  80 us
    ppermute x28, waiting for transfers between devices, send_blk(): lax.ppermute(array, 'blk', [(i, (i + distance) % size) for i in range(siz...  54.3 us
    pallas_call x2, Pallas kernels, cross_call(): pl.pallas_call(functools.partial(cross_backward_kernel if backward else c...  53.7 us
    pallas_call x4, Pallas kernels, source_call(): pl.pallas_call(kernel, grid_spec=pltpu.PrefetchScalarGridSpec(num_scalar_...  51.9 us
    ppermute x1, waiting for transfers between devices, on_device(): side = lax.ppermute(side, 'blk', [(i, i - 1) for i in range(1, blocks)])  49.1 us
    unnamed x173, local copies, waits for them, and re-layouts  29.8 us
    ppermute x15, starting transfers between devices, send_outer(): lax.ppermute(array, 'tensor', [(i, (i + 2 * distance) % size) for i in ra...  22 us
  transfers between devices with their start and end apart: 66, of which 29 were waited for; matrix products, arithmetic and copies ran while one was open for 12% of the time, Pallas kernels for 12%

profile of v3, /device:TPU:0, one launch (start us, length us, event | category | flops | bytes accessed | tf_op | source)
XLA Modules:
  0.0 720.8 jit_solution(4650447106615228618)
XLA Ops:
  13.9 3.9 convolution_convert_fusion
  18.9 2.9 collective-permute-start
  24.0 16.1 %collective-permute-done = bf16[4,128,768]{2,1,0:T(8,128)(2,1)S(1)} collective-permute-done((bf16[4,128,768]{2,1,0:T(8,128)(2,1)S(1)}, bf16[4,128,768]{2,1,0:T(8,128)(2,1)S(1)}, u32[]{:S(2)}, u32[]{:S(2)}) %collective-permute-start) | collective-permute-done | bytes 786464 | tf_op jit(solution)/shard_map/ppermute | solution.py:648
  46.9 4.6 collective-permute-done.3
  51.5 10.4 %collective-permute-done.2 = bf16[1024,256]{1,0:T(8,128)(2,1)} collective-permute-done((bf16[1024,256]{1,0:T(8,128)(2,1)}, bf16[1024,256]{1,0:T(8,128)(2,1)}, u32[]{:S(2)}, u32[]{:S(2)}) %collective-permute-start.2) | collective-permute-done | bytes 524320 | tf_op jit(solution)/shard_map/ppermute | solution.py:648
  61.9 5.4 self_forward.1
  80.7 3.1 convolution_convert_fusion.2.refs_0_
  96.0 13.5 %collective-permute-done.12 = bf16[1024,512]{1,0:T(8,128)(2,1)} collective-permute-done((bf16[1024,512]{1,0:T(8,128)(2,1)}, bf16[1024,512]{1,0:T(8,128)(2,1)}, u32[]{:S(2)}, u32[]{:S(2)}) %collective-permute-start.12) | collective-permute-done | bytes 1048608 | tf_op jit(solution)/shard_map/ppermute | solution.py:648
  109.5 3.4 pad_maximum_fusion.1
  119.5 14.3 %source_project.1.refs_6_.refs_7_.refs_10_.refs_11_ = bf16[4,1024,1024]{2,1,0:T(8,128)(2,1)} custom-call(s32[1]{0:T(128)} %bitcast.19.row, bf16[8,1024,1024]{2,1,0:T(8,128)(2,1)} %tokens.3, bf16[1024,1024]{1,0:T(8,128)(2,1)} %copy-done.34), custom_call_target="tpu_custom_call" | custom-call | tf_op jit(solution)/shard_map/source_project/pallas_call | solution.py:497
  133.8 23.7 %cross_forward.1 = (bf16[4,144,512]{2,1,0:T(8,128)(2,1)}, bf16[4,144,512]{2,1,0:T(8,128)(2,1)}, bf16[4,144,512]{2,1,0:T(8,128)(2,1)}, bf16[4,144,512]{2,1,0:T(8,128)(2,1)}) custom-call(s32[4,8]{1,0:T(4,128)} %copy.231.table_ref, bf16[4,128,512]{2,1,0:T(8,128)(2,1)} %convolution_convert_fusion.2.refs_0_, bf16[4,128,512]{2,1,0:T(8,128)(2,1)} %collective-permute-done.9.refs_1_, ...), custom_call_target="tpu_custom_call" | custom-call | flops 4294967296 | bytes 8388608 | tf_op jit(solution)/shard_map/cross_forward/pallas_call | solution.py:379
  160.8 15.8 %collective-permute-start.14 = (bf16[4,144,512]{2,1,0:T(8,128)(2,1)S(1)}, bf16[4,144,512]{2,1,0:T(8,128)(2,1)S(1)}, u32[]{:S(2)}, u32[]{:S(2)}) collective-permute-start(bf16[4,144,512]{2,1,0:T(8,128)(2,1)S(1)} %copy-done.80), channel_id=1, source_target_pairs={{0,8},{4,12},{8,0},{12,4},{1,9},{5,13},{9,1},{13,5},{2,10},{6,14},... | collective-permute-start | bytes 1769480 | tf_op jit(solution)/shard_map/ppermute | solution.py:640
  181.4 46.2 %collective-permute-done.17 = bf16[1024,128]{1,0:T(8,128)(2,1)S(1)} collective-permute-done((bf16[1024,128]{1,0:T(8,128)(2,1)S(1)}, bf16[1024,128]{1,0:T(8,128)(2,1)S(1)}, u32[]{:S(2)}, u32[]{:S(2)}) %collective-permute-start.17) | collective-permute-done | bytes 262176 | tf_op jit(solution)/shard_map/ppermute | solution.py:648
  238.5 8.9 %ffn_forward.1 = (f32[512,1024]{1,0:T(8,128)S(1)}, bf16[512,2048]{1,0:T(8,128)(2,1)S(1)}, bf16[512,256]{1,0:T(8,128)(2,1)S(1)}, f32[512,256]{1,0:T(8,128)S(1)}) custom-call(bf16[512,1024]{1,0:T(8,128)(2,1)S(1)} %pad_maximum_fusion.10.tokens, bf16[1024,2048]{1,0:T(8,128)(2,1)S(1)} %constant_dynamic-update-slice_fusion.7.weight_in, ...), custom_call_target="tpu_custom_call" | custom-call | flops 4294967296 | bytes 8388608 | tf_op jit(solution)/shard_map/ffn_forward/pallas_call | solution.py:566
  259.9 8.4 %ffn_backward.1 = (f32[512,1024]{1,0:T(8,128)S(1)}, bf16[512,256]{1,0:T(8,128)(2,1)S(1)}) custom-call(bf16[512,1024]{1,0:T(8,128)(2,1)S(1)} %pad_maximum_fusion.11.grad, bf16[1024,2048]{1,0:T(8,128)(2,1)S(1)} %copy-done.12, bf16[2048,1024]{1,0:T(8,128)(2,1)} %pad_maximum_fusion.weight_out, bf16[1024,256]{1,0:T(8,128)(2,1)S(1)} %copy-done.25, ...), custom_call_target="tpu_custom_call" | custom-call | flops 4294967296 | bytes 8388608 | tf_op jit(solution)/shard_map/ffn_backward/pallas_call | solution.py:566
  280.4 3.8 collective-permute-start.25
  289.1 12.5 %collective-permute-done.28 = bf16[1024,512]{1,0:T(8,128)(2,1)S(1)} collective-permute-done((bf16[1024,512]{1,0:T(8,128)(2,1)S(1)}, bf16[1024,512]{1,0:T(8,128)(2,1)S(1)}, u32[]{:S(2)}, u32[]{:S(2)}) %collective-permute-start.28) | collective-permute-done | bytes 1048608 | tf_op jit(solution)/shard_map/ppermute | solution.py:648
  302.9 9.5 %collective-permute-done.29 = bf16[256,1024]{1,0:T(8,128)(2,1)} collective-permute-done((bf16[256,1024]{1,0:T(8,128)(2,1)}, bf16[256,1024]{1,0:T(8,128)(2,1)}, u32[]{:S(2)}, u32[]{:S(2)}) %collective-permute-start.29) | collective-permute-done | bytes 524320 | tf_op jit(solution)/shard_map/ppermute | solution.py:648
  312.5 10.6 %collective-permute-done.26.refs_6_ = bf16[4,144,512]{2,1,0:T(8,128)(2,1)S(1)} collective-permute-done((bf16[4,144,512]{2,1,0:T(8,128)(2,1)S(1)}, bf16[4,144,512]{2,1,0:T(8,128)(2,1)S(1)}, u32[]{:S(2)}, u32[]{:S(2)}) %collective-permute-start.26) | collective-permute-done | bytes 589856 | tf_op jit(solution)/shard_map/ppermute | solution.py:640
  324.7 30.0 %cross_backward.1 = (bf16[4,128,512]{2,1,0:T(8,128)(2,1)}, bf16[4,128,512]{2,1,0:T(8,128)(2,1)}, bf16[4,128,512]{2,1,0:T(8,128)(2,1)}, bf16[4,128,512]{2,1,0:T(8,128)(2,1)}, bf16[4,1024,1024]{2,1,0:T(8,128)(2,1)}) custom-call(s32[4,8]{1,0:T(4,128)} %copy.231.table_ref, bf16[4,128,512]{2,1,0:T(8,128)(2,1)} %convolution_convert_fusion.2.refs_0_, ...), custom_call_target="tpu_custom_call" | custom-call | flops 10737418240 | bytes 16777216 | tf_op jit(solution)/shard_map/cross_backward/pallas_call | solution.py:379
  355.5 12.8 %collective-permute-start.30 = (bf16[4,128,512]{2,1,0:T(8,128)(2,1)}, bf16[4,128,512]{2,1,0:T(8,128)(2,1)S(1)}, u32[]{:S(2)}, u32[]{:S(2)}) collective-permute-start(bf16[4,128,512]{2,1,0:T(8,128)(2,1)} %get-tuple-element.149), channel_id=1, source_target_pairs={{0,12},{4,0},{8,4},{12,8},{1,13},{5,1},{9,5},{13,9},{2,14},{6,2},{... | collective-permute-start | bytes 1572872 | tf_op jit(solution)/shard_map/ppermute | solution.py:640
  368.4 12.5 %collective-permute-start.31 = (bf16[4,128,512]{2,1,0:T(8,128)(2,1)}, bf16[4,128,512]{2,1,0:T(8,128)(2,1)}, u32[]{:S(2)}, u32[]{:S(2)}) collective-permute-start(bf16[4,128,512]{2,1,0:T(8,128)(2,1)} %get-tuple-element.150), channel_id=1, source_target_pairs={{0,8},{4,12},{8,0},{12,4},{1,9},{5,13},{9,1},{13,5},{2,10},{6,14},... | collective-permute-start | bytes 1572872 | tf_op jit(solution)/shard_map/ppermute | solution.py:640
  384.4 7.1 collective-permute-done.30
  391.6 15.3 %source_weight.1 = f32[1024,1024]{1,0:T(8,128)} custom-call(s32[1]{0:T(128)} %bitcast.19.row, bf16[8,1024,1024]{2,1,0:T(8,128)(2,1)} %tokens.3, bf16[4,1024,1024]{2,1,0:T(8,128)(2,1)} %get-tuple-element.176.grad), custom_call_target="tpu_custom_call" | custom-call | tf_op jit(solution)/shard_map/source_weight/pallas_call | solution.py:497
  410.2 10.7 %source_other.1 = bf16[4,1024,512]{2,1,0:T(8,128)(2,1)} custom-call(bf16[4,1024,1024]{2,1,0:T(8,128)(2,1)} %get-tuple-element.176.grad, bf16[512,1024]{1,0:T(8,128)(2,1)} %pad_maximum_fusion.14.weight), custom_call_target="tpu_custom_call" | custom-call | tf_op jit(solution)/shard_map/source_other/pallas_call | solution.py:497
  420.9 5.7 collective-permute-done.31
  440.7 2.8 convolution_convert_fusion.1.refs_8_
  443.4 16.8 %collective-permute-done.54 = bf16[1024,512]{1,0:T(8,128)(2,1)} collective-permute-done((bf16[1024,512]{1,0:T(8,128)(2,1)}, bf16[1024,512]{1,0:T(8,128)(2,1)}, u32[]{:S(2)}, u32[]{:S(2)}) %collective-permute-start.54) | collective-permute-done | bytes 1048608 | tf_op jit(solution)/shard_map/ppermute | solution.py:648
  464.5 8.1 %self_backward.1 = (bf16[4,128,512]{2,1,0:T(8,128)(2,1)S(1)}, f32[4,128,512]{2,1,0:T(8,128)S(1)}, f32[4,128,512]{2,1,0:T(8,128)S(1)}, bf16[4,80,1024]{2,1,0:T(8,128)(2,1)}) custom-call(bf16[4,128,1536]{2,1,0:T(8,128)(2,1)S(1)} %pad_maximum_fusion.5.refs_0_.refs_1_.refs_2_, bf16[4,128,1536]{2,1,0:T(8,128)(2,1)S(1)} %pad_maximum_fusion.5.refs_0_.refs_1_.refs_2_, ...), custom_call_target="tpu_custom_call" | custom-call | flops 1342177280 | bytes 3145728 | tf_op jit(solution)/shard_map/self_backward/pallas_call | solution.py:623
  484.4 49.1 %collective-permute-done.38 = bf16[4,80,1024]{2,1,0:T(8,128)(2,1)} collective-permute-done((bf16[4,80,1024]{2,1,0:T(8,128)(2,1)}, bf16[4,80,1024]{2,1,0:T(8,128)(2,1)}, u32[]{:S(2)}, u32[]{:S(2)}) %collective-permute-start.38) | collective-permute-done | bytes 655392 | tf_op jit(solution)/shard_map/ppermute | solution.py:1013
  547.7 10.6 %collective-permute-done.39 = bf16[4,128,768]{2,1,0:T(8,128)(2,1)} collective-permute-done((bf16[4,128,768]{2,1,0:T(8,128)(2,1)}, bf16[4,128,768]{2,1,0:T(8,128)(2,1)}, u32[]{:S(2)}, u32[]{:S(2)}) %collective-permute-start.39) | collective-permute-done | bytes 786464 | tf_op jit(solution)/shard_map/ppermute | solution.py:648
  558.3 3.1 convolution_bitcast_fusion
  561.5 2.7 fusion.9
  567.1 14.7 %collective-permute-done.45 = bf16[1152,512]{1,0:T(8,128)(2,1)S(1)} collective-permute-done((bf16[1152,512]{1,0:T(8,128)(2,1)}, bf16[1152,512]{1,0:T(8,128)(2,1)S(1)}, u32[]{:S(2)}, u32[]{:S(2)}) %collective-permute-start.45) | collective-permute-done | bytes 1179680 | tf_op jit(solution)/shard_map/ppermute | solution.py:648
  585.1 18.3 %collective-permute-done.46 = bf16[576,512]{1,0:T(8,128)(2,1)S(1)} collective-permute-done((bf16[576,512]{1,0:T(8,128)(2,1)S(1)}, bf16[576,512]{1,0:T(8,128)(2,1)S(1)}, u32[]{:S(2)}, u32[]{:S(2)}) %collective-permute-start.46) | collective-permute-done | bytes 589856 | tf_op jit(solution)/shard_map/ppermute | solution.py:663
  605.1 14.8 %collective-permute-done.58 = bf16[128,768]{1,0:T(8,128)(2,1)S(1)} collective-permute-done((bf16[128,768]{1,0:T(8,128)(2,1)S(1)}, bf16[128,768]{1,0:T(8,128)(2,1)S(1)}, u32[]{:S(2)}, u32[]{:S(2)}) %collective-permute-start.58) | collective-permute-done | bytes 196640 | tf_op jit(solution)/shard_map/ppermute | solution.py:640
  620.1 4.6 collective-permute-start.60
  627.2 11.7 %source_own.1 = (f32[4,1024,256]{2,1,0:T(8,128)}, bf16[4,1024,256]{2,1,0:T(8,128)(2,1)}) custom-call(bf16[4,1024,1024]{2,1,0:T(8,128)(2,1)} %get-tuple-element.176.grad, bf16[512,1024]{1,0:T(8,128)(2,1)} %pad_maximum_fusion.16.weight, bf16[4,1024,512]{2,1,0:T(8,128)(2,1)} %collective-permute-done.47.across), custom_call_target="tpu_custom_call" | custom-call | tf_op jit(solution)/shard_map/source_own/pallas_call | solution.py:497
  638.9 3.6 collective-permute-start.55
  644.0 3.3 collective-permute-start.49
  647.9 4.7 collective-permute-done.48
  652.6 5.6 collective-permute-done.49
  658.3 2.8 collective-permute-start.51
  667.0 4.5 collective-permute-done.52
  671.6 17.5 %collective-permute-done.55 = bf16[4,1024,256]{2,1,0:T(8,128)(2,1)} collective-permute-done((bf16[4,1024,256]{2,1,0:T(8,128)(2,1)}, bf16[4,1024,256]{2,1,0:T(8,128)(2,1)}, u32[]{:S(2)}, u32[]{:S(2)}) %collective-permute-start.55) | collective-permute-done | bytes 2097184 | tf_op jit(solution)/shard_map/ppermute | solution.py:648
  689.1 2.9 convert_bitcast_fusion
  697.5 4.1 broadcast_in_dim.30
  704.0 4.0 convert_dynamic-update-slice_fusion
  (443 shorter events, 183.1 us)
Async XLA Ops:
  7.2 664.3 %all-reduce.6.cloned.1.call-start = ((), (), s32[]{:S(2)}) async-start(), calls=%async_computation | async-start | bytes 4194304 | tf_op jit(solution)/shard_map/psum | solution.py:1015
  18.9 21.3 %collective-permute-start = (bf16[4,128,768]{2,1,0:T(8,128)(2,1)S(1)}, bf16[4,128,768]{2,1,0:T(8,128)(2,1)S(1)}, u32[]{:S(2)}, u32[]{:S(2)}) collective-permute-start(bf16[4,128,768]{2,1,0:T(8,128)(2,1)S(1)} %get-tuple-element.355), channel_id=1, source_target_pairs={{0,2},{1,3},{2,0},{3,1},{4,6},{5,7},{6,4},{7,5},{8,10},{9,11},{10,... | collective-permute-start | bytes 2359304 | tf_op jit(solution)/shard_map/ppermute | solution.py:648
  21.8 29.7 %collective-permute-start.3 = (bf16[256,1024]{1,0:T(8,128)(2,1)}, bf16[256,1024]{1,0:T(8,128)(2,1)}, u32[]{:S(2)}, u32[]{:S(2)}) collective-permute-start(bf16[256,1024]{1,0:T(8,128)(2,1)} %param.30), channel_id=1, source_target_pairs={{0,2},{1,3},{2,0},{3,1},{4,6},{5,7},{6,4},{7,5},{8,10},{9,11},{10,... | collective-permute-start | bytes 1572872 | tf_op jit(solution)/shard_map/ppermute | solution.py:648
  21.8 23.0 %collective-permute-start.4 = (s32[4,128]{1,0:T(4,128)S(1)}, s32[4,128]{1,0:T(4,128)S(1)}, u32[]{:S(2)}, u32[]{:S(2)}) collective-permute-start(s32[4,128]{1,0:T(4,128)S(1)} %constant_dynamic-slice_fusion.7), channel_id=1, source_target_pairs={{0,4},{4,8},{8,12},{12,0},{1,5},{5,9},{9,13},{13,1},{2,6},{6,10},{... | collective-permute-start | bytes 6152 | tf_op jit(solution)/shard_map/ppermute | solution.py:640
  41.1 20.8 %collective-permute-start.1 = (bf16[4,80,1024]{2,1,0:T(8,128)(2,1)S(1)}, bf16[4,80,1024]{2,1,0:T(8,128)(2,1)S(1)}, u32[]{:S(2)}, u32[]{:S(2)}) collective-permute-start(bf16[4,80,1024]{2,1,0:T(8,128)(2,1)S(1)} %pad_maximum_fusion.19), channel_id=1, source_target_pairs={{0,4},{4,8},{8,12},{12,0},{1,5},{5,9},{9,13},{13,1},{2,6},{6,10},{... | collective-permute-start | bytes 1966088 | tf_op jit(solution)/shard_map/ppermute | solution.py:640
  43.3 18.6 %collective-permute-start.2 = (bf16[1024,256]{1,0:T(8,128)(2,1)}, bf16[1024,256]{1,0:T(8,128)(2,1)}, u32[]{:S(2)}, u32[]{:S(2)}) collective-permute-start(bf16[1024,256]{1,0:T(8,128)(2,1)} %param.31), channel_id=1, source_target_pairs={{0,2},{1,3},{2,0},{3,1},{4,6},{5,7},{6,4},{7,5},{8,10},{9,11},{10,... | collective-permute-start | bytes 1572872 | tf_op jit(solution)/shard_map/ppermute | solution.py:648
  83.7 25.8 %collective-permute-start.12 = (bf16[1024,512]{1,0:T(8,128)(2,1)}, bf16[1024,512]{1,0:T(8,128)(2,1)}, u32[]{:S(2)}, u32[]{:S(2)}) collective-permute-start(bf16[1024,512]{1,0:T(8,128)(2,1)} %pad_maximum_fusion.9), channel_id=1, source_target_pairs={{0,2},{1,3},{2,0},{3,1},{4,6},{5,7},{6,4},{7,5},{8,10},{9,11},{10,... | collective-permute-start | bytes 3145736 | tf_op jit(solution)/shard_map/ppermute | solution.py:648
  92.1 41.6 %collective-permute-start.10 = (bf16[4,128,512]{2,1,0:T(8,128)(2,1)}, bf16[4,128,512]{2,1,0:T(8,128)(2,1)}, u32[]{:S(2)}, u32[]{:S(2)}) collective-permute-start(bf16[4,128,512]{2,1,0:T(8,128)(2,1)} %convolution_convert_fusion.2.refs_0_), channel_id=1, source_target_pairs={{0,8},{4,12},{8,0},{12,4},{1,9},{5,13},{9,1},{13,5},{2,10},{6,14},... | collective-permute-start | bytes 1572872 | tf_op jit(solution)/shard_map/ppermute | solution.py:640
  93.8 39.9 %collective-permute-start.11 = (bf16[4,128,512]{2,1,0:T(8,128)(2,1)}, bf16[4,128,512]{2,1,0:T(8,128)(2,1)}, u32[]{:S(2)}, u32[]{:S(2)}) collective-permute-start(bf16[4,128,512]{2,1,0:T(8,128)(2,1)} %convolution_convert_fusion.2.refs_0_), channel_id=1, source_target_pairs={{0,12},{4,0},{8,4},{12,8},{1,13},{5,1},{9,5},{13,9},{2,14},{6,2},{... | collective-permute-start | bytes 1572872 | tf_op jit(solution)/shard_map/ppermute | solution.py:640
  96.0 37.8 %collective-permute-start.9 = (bf16[4,128,512]{2,1,0:T(8,128)(2,1)}, bf16[4,128,512]{2,1,0:T(8,128)(2,1)}, u32[]{:S(2)}, u32[]{:S(2)}) collective-permute-start(bf16[4,128,512]{2,1,0:T(8,128)(2,1)} %convolution_convert_fusion.2.refs_0_), channel_id=1, source_target_pairs={{0,4},{4,8},{8,12},{12,0},{1,5},{5,9},{9,13},{13,1},{2,6},{6,10},{... | collective-permute-start | bytes 1572872 | tf_op jit(solution)/shard_map/ppermute | solution.py:640
  112.9 64.2 %collective-permute-start.16 = (bf16[1280,1024]{1,0:T(8,128)(2,1)}, bf16[1280,1024]{1,0:T(8,128)(2,1)}, u32[]{:S(2)}, u32[]{:S(2)}) collective-permute-start(bf16[1280,1024]{1,0:T(8,128)(2,1)} %pad_maximum_fusion.1), channel_id=1, source_target_pairs={{0,2},{1,3},{2,0},{3,1},{4,6},{5,7},{6,4},{7,5},{8,10},{9,11},{10,... | collective-permute-start | bytes 7864328 | tf_op jit(solution)/shard_map/ppermute | solution.py:648
  157.8 72.7 %collective-permute-start.20 = (bf16[1152,1024]{1,0:T(8,128)(2,1)S(1)}, bf16[1152,1024]{1,0:T(8,128)(2,1)S(1)}, u32[]{:S(2)}, u32[]{:S(2)}) collective-permute-start(bf16[1152,1024]{1,0:T(8,128)(2,1)S(1)} %pad_maximum_fusion.2), channel_id=1, source_target_pairs={{0,2},{1,3},{2,0},{3,1},{4,6},{5,7},{6,4},{7,5},{8,10},{9,11},{10,... | collective-permute-start | bytes 7077896 | tf_op jit(solution)/shard_map/ppermute | solution.py:648
  158.6 69.1 %collective-permute-start.13 = (bf16[4,144,512]{2,1,0:T(8,128)(2,1)S(1)}, bf16[4,144,512]{2,1,0:T(8,128)(2,1)S(1)}, u32[]{:S(2)}, u32[]{:S(2)}) collective-permute-start(bf16[4,144,512]{2,1,0:T(8,128)(2,1)S(1)} %copy-done.81), channel_id=1, source_target_pairs={{0,12},{4,0},{8,4},{12,8},{1,13},{5,1},{9,5},{13,9},{2,14},{6,2},{... | collective-permute-start | bytes 1769480 | tf_op jit(solution)/shard_map/ppermute | solution.py:640
  160.8 66.8 %collective-permute-start.14 = (bf16[4,144,512]{2,1,0:T(8,128)(2,1)S(1)}, bf16[4,144,512]{2,1,0:T(8,128)(2,1)S(1)}, u32[]{:S(2)}, u32[]{:S(2)}) collective-permute-start(bf16[4,144,512]{2,1,0:T(8,128)(2,1)S(1)} %copy-done.80), channel_id=1, source_target_pairs={{0,8},{4,12},{8,0},{12,4},{1,9},{5,13},{9,1},{13,5},{2,10},{6,14},... | collective-permute-start | bytes 1769480 | tf_op jit(solution)/shard_map/ppermute | solution.py:640
  176.6 51.1 %collective-permute-start.15 = (bf16[4,144,512]{2,1,0:T(8,128)(2,1)S(1)}, bf16[4,144,512]{2,1,0:T(8,128)(2,1)S(1)}, u32[]{:S(2)}, u32[]{:S(2)}) collective-permute-start(bf16[4,144,512]{2,1,0:T(8,128)(2,1)S(1)} %copy-done.79), channel_id=1, source_target_pairs={{0,4},{4,8},{8,12},{12,0},{1,5},{5,9},{9,13},{13,1},{2,6},{6,10},{... | collective-permute-start | bytes 1769480 | tf_op jit(solution)/shard_map/ppermute | solution.py:640
  177.1 50.5 %collective-permute-start.17 = (bf16[1024,128]{1,0:T(8,128)(2,1)S(1)}, bf16[1024,128]{1,0:T(8,128)(2,1)S(1)}, u32[]{:S(2)}, u32[]{:S(2)}) collective-permute-start(bf16[1024,128]{1,0:T(8,128)(2,1)S(1)} %copy-done.67), channel_id=1, source_target_pairs={{0,2},{1,3},{2,0},{3,1},{4,6},{5,7},{6,4},{7,5},{8,10},{9,11},{10,... | collective-permute-start | bytes 786440 | tf_op jit(solution)/shard_map/ppermute | solution.py:648
  275.6 26.1 %collective-permute-start.28 = (bf16[1024,512]{1,0:T(8,128)(2,1)S(1)}, bf16[1024,512]{1,0:T(8,128)(2,1)S(1)}, u32[]{:S(2)}, u32[]{:S(2)}) collective-permute-start(bf16[1024,512]{1,0:T(8,128)(2,1)S(1)} %pad_maximum_fusion.13), channel_id=1, source_target_pairs={{0,2},{1,3},{2,0},{3,1},{4,6},{5,7},{6,4},{7,5},{8,10},{9,11},{10,... | collective-permute-start | bytes 3145736 | tf_op jit(solution)/shard_map/ppermute | solution.py:648
  280.4 32.0 %collective-permute-start.25 = (bf16[4,144,512]{2,1,0:T(8,128)(2,1)S(1)}, bf16[4,144,512]{2,1,0:T(8,128)(2,1)S(1)}, u32[]{:S(2)}, u32[]{:S(2)}) collective-permute-start(bf16[4,144,512]{2,1,0:T(8,128)(2,1)S(1)} %cross_prepare.1.refs_4_), channel_id=1, source_target_pairs={{0,4},{4,8},{8,12},{12,0},{1,5},{5,9},{9,13},{13,1},{2,6},{6,10},{... | collective-permute-start | bytes 1769480 | tf_op jit(solution)/shard_map/ppermute | solution.py:640
  284.3 38.8 %collective-permute-start.26 = (bf16[4,144,512]{2,1,0:T(8,128)(2,1)S(1)}, bf16[4,144,512]{2,1,0:T(8,128)(2,1)S(1)}, u32[]{:S(2)}, u32[]{:S(2)}) collective-permute-start(bf16[4,144,512]{2,1,0:T(8,128)(2,1)S(1)} %cross_prepare.1.refs_4_), channel_id=1, source_target_pairs={{0,8},{4,12},{8,0},{12,4},{1,9},{5,13},{9,1},{13,5},{2,10},{6,14},... | collective-permute-start | bytes 1769480 | tf_op jit(solution)/shard_map/ppermute | solution.py:640
  284.7 38.4 %collective-permute-start.27 = (bf16[4,144,512]{2,1,0:T(8,128)(2,1)S(1)}, bf16[4,144,512]{2,1,0:T(8,128)(2,1)S(1)}, u32[]{:S(2)}, u32[]{:S(2)}) collective-permute-start(bf16[4,144,512]{2,1,0:T(8,128)(2,1)S(1)} %cross_prepare.1.refs_4_), channel_id=1, source_target_pairs={{0,12},{4,0},{8,4},{12,8},{1,13},{5,1},{9,5},{13,9},{2,14},{6,2},{... | collective-permute-start | bytes 1769480 | tf_op jit(solution)/shard_map/ppermute | solution.py:640
  286.7 25.7 %collective-permute-start.29 = (bf16[256,1024]{1,0:T(8,128)(2,1)}, bf16[256,1024]{1,0:T(8,128)(2,1)}, u32[]{:S(2)}, u32[]{:S(2)}) collective-permute-start(bf16[256,1024]{1,0:T(8,128)(2,1)} %get-tuple-element.162), channel_id=1, source_target_pairs={{0,2},{1,3},{2,0},{3,1},{4,6},{5,7},{6,4},{7,5},{8,10},{9,11},{10,... | collective-permute-start | bytes 1572872 | tf_op jit(solution)/shard_map/ppermute | solution.py:648
  354.7 71.9 %collective-permute-start.33 = (bf16[1024,768]{1,0:T(8,128)(2,1)}, bf16[1024,768]{1,0:T(8,128)(2,1)}, u32[]{:S(2)}, u32[]{:S(2)}) collective-permute-start(bf16[1024,768]{1,0:T(8,128)(2,1)} %constant_dynamic-update-slice_fusion), channel_id=1, source_target_pairs={{0,2},{1,3},{2,0},{3,1},{4,6},{5,7},{6,4},{7,5},{8,10},{9,11},{10,... | collective-permute-start | bytes 4718600 | tf_op jit(solution)/shard_map/ppermute | solution.py:648
  355.5 36.0 %collective-permute-start.30 = (bf16[4,128,512]{2,1,0:T(8,128)(2,1)}, bf16[4,128,512]{2,1,0:T(8,128)(2,1)S(1)}, u32[]{:S(2)}, u32[]{:S(2)}) collective-permute-start(bf16[4,128,512]{2,1,0:T(8,128)(2,1)} %get-tuple-element.149), channel_id=1, source_target_pairs={{0,12},{4,0},{8,4},{12,8},{1,13},{5,1},{9,5},{13,9},{2,14},{6,2},{... | collective-permute-start | bytes 1572872 | tf_op jit(solution)/shard_map/ppermute | solution.py:640
  368.4 58.2 %collective-permute-start.31 = (bf16[4,128,512]{2,1,0:T(8,128)(2,1)}, bf16[4,128,512]{2,1,0:T(8,128)(2,1)}, u32[]{:S(2)}, u32[]{:S(2)}) collective-permute-start(bf16[4,128,512]{2,1,0:T(8,128)(2,1)} %get-tuple-element.150), channel_id=1, source_target_pairs={{0,8},{4,12},{8,0},{12,4},{1,9},{5,13},{9,1},{13,5},{2,10},{6,14},... | collective-permute-start | bytes 1572872 | tf_op jit(solution)/shard_map/ppermute | solution.py:640
  380.9 45.7 %collective-permute-start.32 = (bf16[4,128,512]{2,1,0:T(8,128)(2,1)}, bf16[4,128,512]{2,1,0:T(8,128)(2,1)}, u32[]{:S(2)}, u32[]{:S(2)}) collective-permute-start(bf16[4,128,512]{2,1,0:T(8,128)(2,1)} %get-tuple-element.151), channel_id=1, source_target_pairs={{0,4},{4,8},{8,12},{12,0},{1,5},{5,9},{9,13},{13,1},{2,6},{6,10},{... | collective-permute-start | bytes 1572872 | tf_op jit(solution)/shard_map/ppermute | solution.py:640
  434.5 25.8 %collective-permute-start.54 = (bf16[1024,512]{1,0:T(8,128)(2,1)}, bf16[1024,512]{1,0:T(8,128)(2,1)}, u32[]{:S(2)}, u32[]{:S(2)}) collective-permute-start(bf16[1024,512]{1,0:T(8,128)(2,1)} %concatenate.153), channel_id=1, source_target_pairs={{0,2},{1,3},{2,0},{3,1},{4,6},{5,7},{6,4},{7,5},{8,10},{9,11},{10,... | collective-permute-start | bytes 3145736 | tf_op jit(solution)/shard_map/ppermute | solution.py:648
  438.3 188.9 %collective-permute-start.47 = (bf16[4,1024,512]{2,1,0:T(8,128)(2,1)}, bf16[4,1024,512]{2,1,0:T(8,128)(2,1)}, u32[]{:S(2)}, u32[]{:S(2)}) collective-permute-start(bf16[4,1024,512]{2,1,0:T(8,128)(2,1)} %source_other.1), channel_id=1, source_target_pairs={{0,1},{1,0},{2,3},{3,2},{4,5},{5,4},{6,7},{7,6},{8,9},{9,8},{10,11... | collective-permute-start | bytes 12582920 | tf_op jit(solution)/shard_map/ppermute | solution.py:644
  474.6 58.9 %collective-permute-start.38 = (bf16[4,80,1024]{2,1,0:T(8,128)(2,1)}, bf16[4,80,1024]{2,1,0:T(8,128)(2,1)}, u32[]{:S(2)}, u32[]{:S(2)}) collective-permute-start(bf16[4,80,1024]{2,1,0:T(8,128)(2,1)} %get-tuple-element.165), channel_id=1, source_target_pairs={{4,0},{8,4},{12,8},{5,1},{9,5},{13,9},{6,2},{10,6},{14,10},{7,3},{... | collective-permute-start | bytes 1966088 | tf_op jit(solution)/shard_map/ppermute | solution.py:1013
  479.2 61.6 %collective-permute-start.36 = (bf16[256,1024]{1,0:T(8,128)(2,1)}, bf16[256,1024]{1,0:T(8,128)(2,1)}, u32[]{:S(2)}, u32[]{:S(2)}) collective-permute-start(bf16[256,1024]{1,0:T(8,128)(2,1)} %get-tuple-element.162), channel_id=1, source_target_pairs={{0,1},{1,0},{2,3},{3,2},{4,5},{5,4},{6,7},{7,6},{8,9},{9,8},{10,11... | collective-permute-start | bytes 1572872 | tf_op jit(solution)/shard_map/ppermute | solution.py:644
  479.7 65.0 %collective-permute-start.37 = (bf16[256,1024]{1,0:T(8,128)(2,1)}, bf16[256,1024]{1,0:T(8,128)(2,1)}, u32[]{:S(2)}, u32[]{:S(2)}) collective-permute-start(bf16[256,1024]{1,0:T(8,128)(2,1)} %collective-permute-done.29), channel_id=1, source_target_pairs={{0,1},{1,0},{2,3},{3,2},{4,5},{5,4},{6,7},{7,6},{8,9},{9,8},{10,11... | collective-permute-start | bytes 1572872 | tf_op jit(solution)/shard_map/ppermute | solution.py:644
  537.5 20.8 %collective-permute-start.39 = (bf16[4,128,768]{2,1,0:T(8,128)(2,1)}, bf16[4,128,768]{2,1,0:T(8,128)(2,1)}, u32[]{:S(2)}, u32[]{:S(2)}) collective-permute-start(bf16[4,128,768]{2,1,0:T(8,128)(2,1)} %pad_maximum_fusion.18), channel_id=1, source_target_pairs={{0,2},{1,3},{2,0},{3,1},{4,6},{5,7},{6,4},{7,5},{8,10},{9,11},{10,... | collective-permute-start | bytes 2359304 | tf_op jit(solution)/shard_map/ppermute | solution.py:648
  540.3 41.4 %collective-permute-start.45 = (bf16[1152,512]{1,0:T(8,128)(2,1)}, bf16[1152,512]{1,0:T(8,128)(2,1)S(1)}, u32[]{:S(2)}, u32[]{:S(2)}) collective-permute-start(bf16[1152,512]{1,0:T(8,128)(2,1)} %fusion.21), channel_id=1, source_target_pairs={{0,2},{1,3},{2,0},{3,1},{4,6},{5,7},{6,4},{7,5},{8,10},{9,11},{10,... | collective-permute-start | bytes 3538952 | tf_op jit(solution)/shard_map/ppermute | solution.py:648
  561.5 22.1 %collective-permute-start.56 = (bf16[512,768]{1,0:T(8,128)(2,1)S(1)}, bf16[512,768]{1,0:T(8,128)(2,1)S(1)}, u32[]{:S(2)}, u32[]{:S(2)}) collective-permute-start(bf16[512,768]{1,0:T(8,128)(2,1)S(1)} %dynamic-slice_convert_fusion), channel_id=1, source_target_pairs={{0,16},{16,0},{1,17},{17,1},{2,18},{18,2},{3,19},{19,3},{4,20},{20... | collective-permute-start | bytes 2359304 | tf_op jit(solution)/shard_map/ppermute | solution.py:663
  567.0 15.3 %collective-permute-start.40 = (bf16[256,1024]{1,0:T(8,128)(2,1)S(1)}, bf16[256,1024]{1,0:T(8,128)(2,1)S(1)}, u32[]{:S(2)}, u32[]{:S(2)}) collective-permute-start(bf16[256,1024]{1,0:T(8,128)(2,1)S(1)} %dynamic-slice_convert_fusion.2), channel_id=1, source_target_pairs={{0,1},{1,0},{2,3},{3,2},{4,5},{5,4},{6,7},{7,6},{8,9},{9,8},{10,11... | collective-permute-start | bytes 1572872 | tf_op jit(solution)/shard_map/ppermute | solution.py:644
  582.2 21.1 %collective-permute-start.46 = (bf16[576,512]{1,0:T(8,128)(2,1)S(1)}, bf16[576,512]{1,0:T(8,128)(2,1)S(1)}, u32[]{:S(2)}, u32[]{:S(2)}) collective-permute-start(bf16[576,512]{1,0:T(8,128)(2,1)S(1)} %dynamic-slice_convert_fusion.1), channel_id=1, source_target_pairs={{0,16},{16,0},{1,17},{17,1},{2,18},{18,2},{3,19},{19,3},{4,20},{20... | collective-permute-start | bytes 1769480 | tf_op jit(solution)/shard_map/ppermute | solution.py:663
  582.6 42.9 %collective-permute-start.41 = (bf16[256,1024]{1,0:T(8,128)(2,1)S(1)}, bf16[256,1024]{1,0:T(8,128)(2,1)S(1)}, u32[]{:S(2)}, u32[]{:S(2)}) collective-permute-start(bf16[256,1024]{1,0:T(8,128)(2,1)S(1)} %add_convert_fusion.1), channel_id=1, source_target_pairs={{0,1},{1,0},{2,3},{3,2},{4,5},{5,4},{6,7},{7,6},{8,9},{9,8},{10,11... | collective-permute-start | bytes 1572872 | tf_op jit(solution)/shard_map/ppermute | solution.py:644
  582.6 44.4 %collective-permute-start.42 = (bf16[256,1024]{1,0:T(8,128)(2,1)S(1)}, bf16[256,1024]{1,0:T(8,128)(2,1)S(1)}, u32[]{:S(2)}, u32[]{:S(2)}) collective-permute-start(bf16[256,1024]{1,0:T(8,128)(2,1)S(1)} %add_convert_fusion.1), channel_id=1, source_target_pairs={{0,2},{1,3},{2,0},{3,1},{4,6},{5,7},{6,4},{7,5},{8,10},{9,11},{10,... | collective-permute-start | bytes 1572872 | tf_op jit(solution)/shard_map/ppermute | solution.py:648
  583.8 19.5 %collective-permute-start.57 = (bf16[128,768]{1,0:T(8,128)(2,1)S(1)}, bf16[128,768]{1,0:T(8,128)(2,1)S(1)}, u32[]{:S(2)}, u32[]{:S(2)}) collective-permute-start(bf16[128,768]{1,0:T(8,128)(2,1)S(1)} %get-tuple-element.351), channel_id=1, source_target_pairs={{0,4},{4,8},{8,12},{12,0},{1,5},{5,9},{9,13},{13,1},{2,6},{6,10},{... | collective-permute-start | bytes 589832 | tf_op jit(solution)/shard_map/ppermute | solution.py:640
  603.3 16.6 %collective-permute-start.58 = (bf16[128,768]{1,0:T(8,128)(2,1)S(1)}, bf16[128,768]{1,0:T(8,128)(2,1)S(1)}, u32[]{:S(2)}, u32[]{:S(2)}) collective-permute-start(bf16[128,768]{1,0:T(8,128)(2,1)S(1)} %get-tuple-element.353), channel_id=1, source_target_pairs={{0,8},{4,12},{8,0},{12,4},{1,9},{5,13},{9,1},{13,5},{2,10},{6,14},... | collective-permute-start | bytes 589832 | tf_op jit(solution)/shard_map/ppermute | solution.py:640
  603.3 16.6 %collective-permute-start.59 = (bf16[128,768]{1,0:T(8,128)(2,1)S(1)}, bf16[128,768]{1,0:T(8,128)(2,1)S(1)}, u32[]{:S(2)}, u32[]{:S(2)}) collective-permute-start(bf16[128,768]{1,0:T(8,128)(2,1)S(1)} %get-tuple-element.352), channel_id=1, source_target_pairs={{0,12},{4,0},{8,4},{12,8},{1,13},{5,1},{9,5},{13,9},{2,14},{6,2},{... | collective-permute-start | bytes 589832 | tf_op jit(solution)/shard_map/ppermute | solution.py:640
  620.1 22.4 %collective-permute-start.60 = (bf16[128,768]{1,0:T(8,128)(2,1)S(1)}, bf16[128,768]{1,0:T(8,128)(2,1)S(1)}, u32[]{:S(2)}, u32[]{:S(2)}) collective-permute-start(bf16[128,768]{1,0:T(8,128)(2,1)S(1)} %get-tuple-element.322), channel_id=1, source_target_pairs={{0,4},{4,8},{8,12},{12,0},{1,5},{5,9},{9,13},{13,1},{2,6},{6,10},{... | collective-permute-start | bytes 589832 | tf_op jit(solution)/shard_map/ppermute | solution.py:640
  624.6 17.9 %collective-permute-start.61 = (bf16[128,768]{1,0:T(8,128)(2,1)S(1)}, bf16[128,768]{1,0:T(8,128)(2,1)S(1)}, u32[]{:S(2)}, u32[]{:S(2)}) collective-permute-start(bf16[128,768]{1,0:T(8,128)(2,1)S(1)} %get-tuple-element.322), channel_id=1, source_target_pairs={{0,8},{4,12},{8,0},{12,4},{1,9},{5,13},{9,1},{13,5},{2,10},{6,14},... | collective-permute-start | bytes 589832 | tf_op jit(solution)/shard_map/ppermute | solution.py:640
  625.5 17.1 %collective-permute-start.62 = (bf16[128,768]{1,0:T(8,128)(2,1)S(1)}, bf16[128,768]{1,0:T(8,128)(2,1)S(1)}, u32[]{:S(2)}, u32[]{:S(2)}) collective-permute-start(bf16[128,768]{1,0:T(8,128)(2,1)S(1)} %get-tuple-element.322), channel_id=1, source_target_pairs={{0,12},{4,0},{8,4},{12,8},{1,13},{5,1},{9,5},{13,9},{2,14},{6,2},{... | collective-permute-start | bytes 589832 | tf_op jit(solution)/shard_map/ppermute | solution.py:640
  627.1 20.2 %collective-permute-start.43 = (bf16[256,1024]{1,0:T(8,128)(2,1)S(1)}, bf16[256,1024]{1,0:T(8,128)(2,1)S(1)}, u32[]{:S(2)}, u32[]{:S(2)}) collective-permute-start(bf16[256,1024]{1,0:T(8,128)(2,1)S(1)} %collective-permute-done.42), channel_id=1, source_target_pairs={{0,1},{1,0},{2,3},{3,2},{4,5},{5,4},{6,7},{7,6},{8,9},{9,8},{10,11... | collective-permute-start | bytes 1572872 | tf_op jit(solution)/shard_map/ppermute | solution.py:644
  638.9 50.2 %collective-permute-start.55 = (bf16[4,1024,256]{2,1,0:T(8,128)(2,1)}, bf16[4,1024,256]{2,1,0:T(8,128)(2,1)}, u32[]{:S(2)}, u32[]{:S(2)}) collective-permute-start(bf16[4,1024,256]{2,1,0:T(8,128)(2,1)} %get-tuple-element.188), channel_id=1, source_target_pairs={{0,2},{1,3},{2,0},{3,1},{4,6},{5,7},{6,4},{7,5},{8,10},{9,11},{10,... | collective-permute-start | bytes 6291464 | tf_op jit(solution)/shard_map/ppermute | solution.py:648
  642.6 21.3 %collective-permute-start.63 = (bf16[512,768]{1,0:T(8,128)(2,1)S(1)}, bf16[512,768]{1,0:T(8,128)(2,1)S(1)}, u32[]{:S(2)}, u32[]{:S(2)}) collective-permute-start(bf16[512,768]{1,0:T(8,128)(2,1)S(1)} %constant_dynamic-update-slice_fusion.15), channel_id=1, source_target_pairs={{0,16},{16,0},{1,17},{17,1},{2,18},{18,2},{3,19},{19,3},{4,20},{20... | collective-permute-start | bytes 2359304 | tf_op jit(solution)/shard_map/ppermute | solution.py:663
  644.0 14.2 %collective-permute-start.49 = (bf16[144,512]{1,0:T(8,128)(2,1)S(1)}, bf16[144,512]{1,0:T(8,128)(2,1)S(1)}, u32[]{:S(2)}, u32[]{:S(2)}) collective-permute-start(bf16[144,512]{1,0:T(8,128)(2,1)S(1)} %get-tuple-element.360), channel_id=1, source_target_pairs={{0,8},{4,12},{8,0},{12,4},{1,9},{5,13},{9,1},{13,5},{2,10},{6,14},... | collective-permute-start | bytes 442376 | tf_op jit(solution)/shard_map/ppermute | solution.py:640
  694.0 15.3 %collective-permute-start.64 = (bf16[576,512]{1,0:T(8,128)(2,1)S(1)}, bf16[576,512]{1,0:T(8,128)(2,1)}, u32[]{:S(2)}, u32[]{:S(2)}) collective-permute-start(bf16[576,512]{1,0:T(8,128)(2,1)S(1)} %constant_dynamic-update-slice_fusion.20), channel_id=1, source_target_pairs={{0,16},{16,0},{1,17},{17,1},{2,18},{18,2},{3,19},{19,3},{4,20},{20... | collective-permute-start | bytes 1769480 | tf_op jit(solution)/shard_map/ppermute | solution.py:663
  (103 other events, 1052.9 us)
Sparse Core Ops, SparseCore 0:
  474.7 144.2 all-reduce.5
